TPU v7x, 32 devices: a whole 2x2x4 slice. The times are simulated.
32 devices in a mesh: dp: 4 (over y, x), row: 2 (over core), col: 4 (over z).
Axes of the slice: x: 2, y: 2, z: 4, core: 2. Of those that a mesh axis runs over, the one named last changes fastest.
Arguments:
- block_input: bfloat16 [8192, 2048], P(('dp', 'col'), 'row'), may hold values from -6 to 6
- attn_gain: float32 [2048], P('row'), may hold values from 0.5 to 1.5
- attn_weight: bfloat16 [2048, 6144], P('row', 'col'), may hold values from -3.5 to 3.5
- out_weight: bfloat16 [2048, 2048], P('col', 'row'), may hold values from -1 to 1
- feed_gain: float32 [2048], P('row'), may hold values from 0.5 to 1.5
- gate_weight: bfloat16 [2048, 8192], P('row', 'col'), may hold values from -0.125 to 0.125
- up_weight: bfloat16 [2048, 8192], P('row', 'col'), may hold values from -0.125 to 0.125
- down_weight: bfloat16 [8192, 2048], P('col', 'row'), may hold values from -0.0625 to 0.0625
- out_cotangent: bfloat16 [8192, 2048], P(('dp', 'col'), 'row'), may hold values from -6 to 6
Outputs:
- block_output: bfloat16 [8192, 2048], P(('dp', 'col'), 'row')
- input_grad: float32 [8192, 2048], P(('dp', 'col'), 'row')
- attn_gain_grad: float32 [2048], P('row')
- attn_weight_grad: float32 [2048, 6144], P('row', 'col')
- out_weight_grad: float32 [2048, 2048], P('col', 'row')
- feed_gain_grad: float32 [2048], P('row')
- gate_weight_grad: float32 [2048, 8192], P('row', 'col')
- up_weight_grad: float32 [2048, 8192], P('row', 'col')
- down_weight_grad: float32 [8192, 2048], P('col', 'row')
All inputs are finite; a program needn't handle non-finite values.
Results may differ from a plain program's by a relative error of at most 0.014.
Values may be sent and summed in bfloat16 or wider, within the bound.
No kernel may reach another device: no remote copies, remote signals or barrier semaphores. Data moves between devices by JAX's collectives and lax.ppermute only.
A program may use at most 320 MiB of HBM per device.

v0:
```python
import jax
import jax.numpy as jnp
from jax import lax
from jax.sharding import PartitionSpec as P

HD = 64
LEN = 1024


norm_epsilon = 1e-05
rope_base = 130000.0
masked_score = -1e30


def rope_tables(positions):
    steps_half = jnp.arange(HD // 2).astype(jnp.float32)
    frequency = rope_base ** (-2.0 * steps_half / HD)
    angles = positions.astype(jnp.float32)[:, None] * frequency[None, :]
    return (jnp.cos(angles)[:, None, :], jnp.sin(angles)[:, None, :])


def rotate(tensor, cosines, sines, sign):
    half = tensor.shape[-1] // 2
    first = tensor[..., :half]
    second = tensor[..., half:]
    return jnp.concatenate(
        [first * cosines - second * (sign * sines), second * cosines + first * (sign * sines)],
        axis=-1,
    )


def transposed_left(left, right):
    return lax.dot_general(
        left, right, (((0,), (0,)), ((), ())), preferred_element_type=jnp.float32
    )


def transposed_right(left, right):
    return lax.dot_general(
        left, right, (((1,), (1,)), ((), ())), preferred_element_type=jnp.float32
    )


def by_sequence(tensor, seq_count):
    heads = tensor.shape[1]
    shaped = tensor.reshape(seq_count, LEN, heads, tensor.shape[2])
    return jnp.transpose(shaped, (0, 2, 1, 3)).reshape(seq_count * heads, LEN, tensor.shape[2])


def by_token(tensor, seq_count):
    heads = tensor.shape[0] // seq_count
    shaped = tensor.reshape(seq_count, heads, LEN, tensor.shape[2])
    return jnp.transpose(shaped, (0, 2, 1, 3)).reshape(seq_count * LEN, heads, tensor.shape[2])


def block_scores(query_block, key_mat, start, block):
    scores = transposed_right(query_block, key_mat) * HD ** (-0.5)
    allowed = (start + jnp.arange(block))[:, None] >= jnp.arange(LEN)[None, :]
    return jnp.where(allowed, scores, masked_score)


def attend(operands):
    query, key_mat, value = operands
    block = min(512, LEN)

    def one_block(index):
        start = index * block
        query_block = lax.dynamic_slice_in_dim(query, start, block, 0)
        scores = block_scores(query_block, key_mat, start, block)
        peak = jnp.max(scores, axis=1, keepdims=True)
        log_total = peak + jnp.log(jnp.sum(jnp.exp(scores - peak), axis=1, keepdims=True))
        probs = jnp.exp(scores - log_total).astype(jnp.bfloat16)
        return (
            jnp.dot(probs, value, preferred_element_type=jnp.float32).astype(jnp.bfloat16),
            log_total[:, 0],
        )

    block_out, block_totals = lax.map(one_block, jnp.arange(LEN // block))
    return (block_out.reshape(LEN, query.shape[1]), block_totals.reshape(LEN))


def attend_back(operands):
    query, key_mat, value, log_total, grad_out = operands
    block = min(512, LEN)

    def one_block(carry, index):
        key_acc, value_acc = carry
        start = index * block
        query_block = lax.dynamic_slice_in_dim(query, start, block, 0)
        grad_block = lax.dynamic_slice_in_dim(grad_out, start, block, 0)
        total_block = lax.dynamic_slice_in_dim(log_total, start, block, 0)
        scores = block_scores(query_block, key_mat, start, block)
        back_probs = jnp.exp(scores - total_block[:, None])
        value_acc = value_acc + transposed_left(back_probs.astype(jnp.bfloat16), grad_block)
        prob_grad = transposed_right(grad_block, value)
        center = jnp.sum(back_probs * prob_grad, axis=1, keepdims=True)
        score_grad = (back_probs * (prob_grad - center) * HD ** (-0.5)).astype(jnp.bfloat16)
        query_grad = jnp.dot(score_grad, key_mat, preferred_element_type=jnp.float32)
        key_acc = key_acc + transposed_left(score_grad, query_block)
        return ((key_acc, value_acc), query_grad)

    zeros_init = jnp.zeros((LEN, query.shape[1]), jnp.float32)
    (key_grad, value_grad), query_grads = lax.scan(
        one_block, (zeros_init, zeros_init), jnp.arange(LEN // block)
    )
    return (query_grads.reshape(LEN, query.shape[1]), key_grad, value_grad)


def row_total(values):
    return lax.psum(values, "row")


def gather_tokens(values):
    return lax.all_gather(values, "col", axis=0, tiled=True)


def reduce_tokens(term_fn, rows):
    return lax.psum_scatter(
        term_fn(jnp.int32(0), rows * lax.axis_size("col")), "col", scatter_dimension=0, tiled=True
    )


def reduce_heads(values):
    return lax.psum_scatter(values, "row", scatter_dimension=1, tiled=True)


def gather_heads(values):
    return lax.all_gather(values, "row", axis=1, tiled=True)


def gather_units(values):
    return lax.all_gather(values, "row", axis=0, tiled=True)


def shards(
    block_input,
    attn_gain,
    attn_weight,
    out_weight,
    feed_gain,
    gate_weight,
    up_weight,
    down_weight,
    out_cotangent,
):
    local_rows = block_input.shape[0]
    row_count = lax.axis_size("row")
    group_rows = local_rows * lax.axis_size("col")
    width = block_input.shape[1] * row_count
    units = gate_weight.shape[1]
    local_heads = attn_weight.shape[1] // (3 * HD * row_count)
    seq_count = group_rows // LEN
    inputs = block_input.astype(jnp.float32)
    first_scale = lax.rsqrt(row_total(jnp.sum(inputs * inputs, axis=1)) / width + norm_epsilon)[
        :, None
    ]
    first_normed = (inputs * first_scale * attn_gain).astype(jnp.bfloat16)
    first_gathered = gather_tokens(first_normed)
    projected = reduce_heads(
        jnp.dot(first_gathered, attn_weight, preferred_element_type=jnp.float32)
    )
    projected = projected.reshape(group_rows, local_heads, 3, HD)
    cosines, sines = rope_tables(jnp.arange(group_rows) % LEN)
    queries = rotate(projected[:, :, 0], cosines, sines, 1.0).astype(jnp.bfloat16)
    keys = rotate(projected[:, :, 1], cosines, sines, 1.0).astype(jnp.bfloat16)
    values = projected[:, :, 2].astype(jnp.bfloat16)
    query_items = by_sequence(queries, seq_count)
    key_items = by_sequence(keys, seq_count)
    value_items = by_sequence(values, seq_count)
    head_out, log_totals = lax.map(attend, (query_items, key_items, value_items))
    attended = by_token(head_out, seq_count).reshape(group_rows, local_heads * HD)
    heads_gathered = gather_heads(attended)

    def attn_term(start, count):
        return jnp.dot(heads_gathered, out_weight, preferred_element_type=jnp.float32)

    residual = inputs + reduce_tokens(attn_term, local_rows)
    second_scale = lax.rsqrt(
        row_total(jnp.sum(residual * residual, axis=1)) / width + norm_epsilon
    )[:, None]
    second_normed = (residual * second_scale * feed_gain).astype(jnp.bfloat16)
    second_gathered = gather_tokens(second_normed)
    gate_share, upper_share = (
        lax.psum_scatter(
            jnp.dot(second_gathered, gate_weight, preferred_element_type=jnp.float32),
            "row",
            scatter_dimension=0,
            tiled=True,
        ),
        lax.psum_scatter(
            jnp.dot(second_gathered, up_weight, preferred_element_type=jnp.float32),
            "row",
            scatter_dimension=0,
            tiled=True,
        ),
    )
    hidden_share = (jax.nn.silu(gate_share) * upper_share).astype(jnp.bfloat16)
    hidden_gathered = gather_units(hidden_share)

    def down_term(start, count):
        return jnp.dot(hidden_gathered, down_weight, preferred_element_type=jnp.float32)

    block_output = (residual + reduce_tokens(down_term, local_rows)).astype(jnp.bfloat16)
    cotangent_gathered = gather_tokens(out_cotangent)
    down_grad = transposed_left(hidden_gathered, cotangent_gathered)
    hidden_grad = lax.psum_scatter(
        transposed_right(cotangent_gathered, down_weight), "row", scatter_dimension=0, tiled=True
    )
    gate_sigmoid = jax.nn.sigmoid(gate_share)
    gate_grad = (
        hidden_grad * upper_share * gate_sigmoid * (1.0 + gate_share * (1.0 - gate_sigmoid))
    ).astype(jnp.bfloat16)
    upper_grad = (hidden_grad * jax.nn.silu(gate_share)).astype(jnp.bfloat16)
    unit_gathered = gather_units(jnp.concatenate([gate_grad, upper_grad], axis=1))
    both_grad = transposed_left(second_gathered, unit_gathered)
    gate_w_grad = both_grad[:, :units]
    up_w_grad = both_grad[:, units:]

    def second_term(start, count):
        return transposed_right(unit_gathered[:, :units], gate_weight) + transposed_right(
            unit_gathered[:, units:], up_weight
        )

    second_grad = reduce_tokens(second_term, local_rows)
    second_hat = residual * second_scale
    feed_part = jnp.sum(second_grad * second_hat, axis=0)
    weighted = second_grad * feed_gain
    second_mean = row_total(jnp.sum(weighted * second_hat, axis=1))[:, None] / width
    residual_grad = out_cotangent.astype(jnp.float32) + second_scale * (
        weighted - second_hat * second_mean
    )
    residual_low = residual_grad.astype(jnp.bfloat16)
    residual_gathered = gather_tokens(residual_low)
    out_w_grad = transposed_left(heads_gathered, residual_gathered)
    attended_grad = reduce_heads(transposed_right(residual_gathered, out_weight)).astype(
        jnp.bfloat16
    )
    grad_items = by_sequence(attended_grad.reshape(group_rows, local_heads, HD), seq_count)
    query_grad, key_grad, value_grad = lax.map(
        attend_back, (query_items, key_items, value_items, log_totals, grad_items)
    )
    query_pre = rotate(by_token(query_grad, seq_count), cosines, sines, -1.0)
    key_pre = rotate(by_token(key_grad, seq_count), cosines, sines, -1.0)
    projected_grad = (
        jnp.stack([query_pre, key_pre, by_token(value_grad, seq_count)], axis=2)
        .reshape(group_rows, local_heads * 3 * HD)
        .astype(jnp.bfloat16)
    )
    projected_gathered = gather_heads(projected_grad)
    attn_w_grad = transposed_left(first_gathered, projected_gathered)

    def first_term(start, count):
        return transposed_right(projected_gathered, attn_weight)

    first_grad = reduce_tokens(first_term, local_rows)
    first_hat = inputs * first_scale
    attn_part = jnp.sum(first_grad * first_hat, axis=0)
    weighted_first = first_grad * attn_gain
    first_mean = row_total(jnp.sum(weighted_first * first_hat, axis=1))[:, None] / width
    input_grad = residual_grad + first_scale * (weighted_first - first_hat * first_mean)
    attn_gain_grad, feed_gain_grad = lax.psum((attn_part, feed_part), ("dp", "col"))
    attn_summed, out_summed, gate_summed, up_summed, down_summed = lax.psum(
        (attn_w_grad, out_w_grad, gate_w_grad, up_w_grad, down_grad), "dp"
    )
    return (
        block_output,
        input_grad,
        attn_gain_grad,
        attn_summed,
        out_summed,
        feed_gain_grad,
        gate_summed,
        up_summed,
        down_summed,
    )


def solution(mesh):
    in_specs = (
        P(("dp", "col"), "row"),
        P("row"),
        P("row", "col"),
        P("col", "row"),
        P("row"),
        P("row", "col"),
        P("row", "col"),
        P("col", "row"),
        P(("dp", "col"), "row"),
    )
    out_specs = (
        P(("dp", "col"), "row"),
        P(("dp", "col"), "row"),
        P("row"),
        P("row", "col"),
        P("col", "row"),
        P("row"),
        P("row", "col"),
        P("row", "col"),
        P("col", "row"),
    )
    return jax.shard_map(shards, mesh=mesh, in_specs=in_specs, out_specs=out_specs, check_vma=False)
```

profile of v0, /device:TPU:0, one launch (start us, length us, event | category | flops | bytes accessed | tf_op | source)
XLA Modules:
  0.0 2362.3 jit_solution(1648682400817345293)
XLA Ops:
  14.6 83.5 %all-gather.9.cloned.1.call-done = bf16[2048,1024]{1,0:T(8,128)(2,1)} async-done(((bf16[512,1024]{1,0:T(8,128)(2,1)}), bf16[2048,1024]{1,0:T(8,128)(2,1)}) %all-gather.9.cloned.1.call-update) | async-done | bytes 4194320 | tf_op jit(solution)/shard_map/all_gather | solution.py:114
  98.1 11.3 fusion.42
  111.6 18.0 reduce-scatter.10.cloned.1.call-done
  174.0 110.1 %while.54 = (s32[]{:T(128)}, bf16[8,1024,64]{2,1,0:T(8,128)(2,1)}, f32[8,1024]{1,0:T(8,128)}, bf16[8,1024,64]{2,1,0:T(8,128)(2,1)}, bf16[8,1024,64]{2,1,0:T(8,12...) while((s32[]{:T(128)}, bf16[8,1024,64]{2,1,0:T(8,128)(2,1)}, ...), condition=%wide.region_8.9_spmd, body=%wide.region_3.8_spmd.sunk | while | flops 138444800 | bytes 8493492 | solution.py:170
  191.2 8.0 while.57
  204.9 8.0 while.57
  218.7 8.0 while.57
  232.4 8.0 while.57
  246.2 8.0 while.57
  260.0 8.0 while.57
  273.7 8.0 while.57
  290.9 11.6 all-gather.11.cloned.1.call-done
  310.8 145.2 %reduce-scatter.12.cloned.1.call-done = f32[512,1024]{1,0:T(8,128)} async-done(((f32[2048,1024]{1,0:T(8,128)}), f32[512,1024]{1,0:T(8,128)}) %reduce-scatter.12.cloned.1.call-update) | async-done | bytes 2097168 | tf_op jit(solution)/shard_map/reduce_scatter | solution.py:118
  464.8 74.1 %all-gather.17.cloned.1.call-done = bf16[2048,1024]{1,0:T(8,128)(2,1)} async-done(((bf16[512,1024]{1,0:T(8,128)(2,1)}), bf16[2048,1024]{1,0:T(8,128)(2,1)}) %all-gather.17.cloned.1.call-update) | async-done | bytes 4194320 | tf_op jit(solution)/shard_map/all_gather | solution.py:114
  538.9 15.3 fusion.47
  554.3 65.9 %all-gather.13.cloned.1.call-done = bf16[2048,1024]{1,0:T(8,128)(2,1)} async-done(((bf16[512,1024]{1,0:T(8,128)(2,1)}), bf16[2048,1024]{1,0:T(8,128)(2,1)}) %all-gather.13.cloned.1.call-update) | async-done | bytes 4194320 | tf_op jit(solution)/shard_map/all_gather | solution.py:114
  620.2 16.9 fusion.44
  637.7 16.7 fusion.45
  654.5 22.8 reduce-scatter.14.cloned.1.call-done
  677.3 29.8 %reduce-scatter.16.cloned.1.call-done = f32[1024,2048]{1,0:T(8,128)} async-done(((f32[2048,2048]{1,0:T(8,128)}), f32[1024,2048]{1,0:T(8,128)}) %reduce-scatter.16.cloned.1.call-update) | async-done | bytes 8388624 | tf_op jit(solution)/shard_map/reduce_scatter | solution.py:190
  707.1 14.4 multiply_convert_fusion.2
  729.7 31.3 %all-gather.19.cloned.1.call-done = bf16[2048,4096]{1,0:T(8,128)(2,1)} async-done(((bf16[1024,4096]{1,0:T(8,128)(2,1)}), bf16[2048,4096]{1,0:T(8,128)(2,1)}) %all-gather.19.cloned.1.call-update) | async-done | bytes 16777232 | tf_op jit(solution)/shard_map/all_gather | solution.py:132
  760.9 14.7 fusion.16
  775.6 14.6 fusion.21
  790.2 145.7 %reduce-scatter.22.cloned.1.call-done = f32[512,1024]{1,0:T(8,128)} async-done(((f32[2048,1024]{1,0:T(8,128)}), f32[512,1024]{1,0:T(8,128)}) %reduce-scatter.22.cloned.1.call-update) | async-done | bytes 2097168 | tf_op jit(solution)/shard_map/reduce_scatter | solution.py:118
  946.5 81.6 %all-gather.21.cloned.1.call-done = bf16[2048,1024]{1,0:T(8,128)(2,1)} async-done(((bf16[512,1024]{1,0:T(8,128)(2,1)}), bf16[2048,1024]{1,0:T(8,128)(2,1)}) %all-gather.21.cloned.1.call-update) | async-done | bytes 4194320 | tf_op jit(solution)/shard_map/all_gather | solution.py:114
  1035.3 10.4 reduce-scatter.24.cloned.1.call-done
  1057.3 313.8 %while.56 = (s32[]{:T(128)}, f32[8,1024,64]{2,1,0:T(8,128)}, f32[8,1024,64]{1,2,0:T(8,128)}, bf16[8,1024,64]{1,2,0:T(8,128)(2,1)}, bf16[8,1024,64]{2,1,0:T(8,128...) while((s32[]{:T(128)}, f32[8,1024,64]{2,1,0:T(8,128)}, ...), condition=%wide.region_24.25_spmd, body=%wide.region_20.24_spmd.sunk | while | flops 341573632 | bytes 36461196 | solution.py:239
  1064.0 26.8 %while.58 = (s32[]{:T(128)}, f32[1024,64]{0,1:T(8,128)}, f32[1024,64]{0,1:T(8,128)}, f32[2,512,64]{1,2,0:T(8,128)}, s32[2]{0:T(128)S(1)}, /*index=5*/bf16[1024,6...) while((s32[]{:T(128)}, f32[1024,64]{0,1:T(8,128)}, ...), condition=%wide.region_23.23_spmd.clone, body=%wide.region_21.22_spmd.clone.sunk | while | flops 341573632 | bytes 32782684 | solution.py:103
  1103.3 26.8 %while.58 = (s32[]{:T(128)}, f32[1024,64]{0,1:T(8,128)}, f32[1024,64]{0,1:T(8,128)}, f32[2,512,64]{1,2,0:T(8,128)}, s32[2]{0:T(128)S(1)}, /*index=5*/bf16[1024,6...) while((s32[]{:T(128)}, f32[1024,64]{0,1:T(8,128)}, ...), condition=%wide.region_23.23_spmd.clone, body=%wide.region_21.22_spmd.clone.sunk | while | flops 341573632 | bytes 32782684 | solution.py:103
  1142.5 26.8 %while.58 = (s32[]{:T(128)}, f32[1024,64]{0,1:T(8,128)}, f32[1024,64]{0,1:T(8,128)}, f32[2,512,64]{1,2,0:T(8,128)}, s32[2]{0:T(128)S(1)}, /*index=5*/bf16[1024,6...) while((s32[]{:T(128)}, f32[1024,64]{0,1:T(8,128)}, ...), condition=%wide.region_23.23_spmd.clone, body=%wide.region_21.22_spmd.clone.sunk | while | flops 341573632 | bytes 32782684 | solution.py:103
  1181.7 26.8 %while.58 = (s32[]{:T(128)}, f32[1024,64]{0,1:T(8,128)}, f32[1024,64]{0,1:T(8,128)}, f32[2,512,64]{1,2,0:T(8,128)}, s32[2]{0:T(128)S(1)}, /*index=5*/bf16[1024,6...) while((s32[]{:T(128)}, f32[1024,64]{0,1:T(8,128)}, ...), condition=%wide.region_23.23_spmd.clone, body=%wide.region_21.22_spmd.clone.sunk | while | flops 341573632 | bytes 32782684 | solution.py:103
  1220.9 26.8 %while.58 = (s32[]{:T(128)}, f32[1024,64]{0,1:T(8,128)}, f32[1024,64]{0,1:T(8,128)}, f32[2,512,64]{1,2,0:T(8,128)}, s32[2]{0:T(128)S(1)}, /*index=5*/bf16[1024,6...) while((s32[]{:T(128)}, f32[1024,64]{0,1:T(8,128)}, ...), condition=%wide.region_23.23_spmd.clone, body=%wide.region_21.22_spmd.clone.sunk | while | flops 341573632 | bytes 32782684 | solution.py:103
  1260.2 26.8 %while.58 = (s32[]{:T(128)}, f32[1024,64]{0,1:T(8,128)}, f32[1024,64]{0,1:T(8,128)}, f32[2,512,64]{1,2,0:T(8,128)}, s32[2]{0:T(128)S(1)}, /*index=5*/bf16[1024,6...) while((s32[]{:T(128)}, f32[1024,64]{0,1:T(8,128)}, ...), condition=%wide.region_23.23_spmd.clone, body=%wide.region_21.22_spmd.clone.sunk | while | flops 341573632 | bytes 32782684 | solution.py:103
  1299.4 26.8 %while.58 = (s32[]{:T(128)}, f32[1024,64]{0,1:T(8,128)}, f32[1024,64]{0,1:T(8,128)}, f32[2,512,64]{1,2,0:T(8,128)}, s32[2]{0:T(128)S(1)}, /*index=5*/bf16[1024,6...) while((s32[]{:T(128)}, f32[1024,64]{0,1:T(8,128)}, ...), condition=%wide.region_23.23_spmd.clone, body=%wide.region_21.22_spmd.clone.sunk | while | flops 341573632 | bytes 32782684 | solution.py:103
  1338.6 26.8 %while.58 = (s32[]{:T(128)}, f32[1024,64]{0,1:T(8,128)}, f32[1024,64]{0,1:T(8,128)}, f32[2,512,64]{1,2,0:T(8,128)}, s32[2]{0:T(128)S(1)}, /*index=5*/bf16[1024,6...) while((s32[]{:T(128)}, f32[1024,64]{0,1:T(8,128)}, ...), condition=%wide.region_23.23_spmd.clone, body=%wide.region_21.22_spmd.clone.sunk | while | flops 341573632 | bytes 32782684 | solution.py:103
  1401.9 17.2 all-gather.23.cloned.1.call-done
  1419.1 11.0 fusion.49
  1430.2 12.0 all-gather.15.cloned.1.call-done
  1442.1 14.5 fusion.46
  1456.9 14.8 fusion.53
  1471.7 21.4 fusion.52
  1505.7 11.0 fusion.50
  1516.7 73.9 %reduce-scatter.26.cloned.1.call-done = f32[512,1024]{1,0:T(8,128)} async-done(((f32[2048,1024]{1,0:T(8,128)}), f32[512,1024]{1,0:T(8,128)}) %reduce-scatter.26.cloned.1.call-update) | async-done | bytes 2097168 | tf_op jit(solution)/shard_map/reduce_scatter | solution.py:118
  1595.6 45.6 %all-reduce = (f32[1024]{0:T(1024)}, f32[1024]{0:T(1024)}) all-reduce(f32[1024]{0:T(1024)S(1)} %get-tuple-element.256, f32[1024]{0:T(1024)S(1)} %copy-done.19), channel_id=1, replica_groups=mesh['dp'=4,'row'=2,'col'=4] {'dp','col'}, use_global_device_ids=true, to_apply=%region_29.30 | all-reduce | flops 2048 | bytes 16384 | tf_op jit(solution)/shard_map/psum | solution.py:261
  1641.2 99.8 %reduce-scatter.18.cloned.1.call-done = f32[512,1024]{1,0:T(8,128)} async-done(((f32[2048,1024]{1,0:T(8,128)}), f32[512,1024]{1,0:T(8,128)}) %reduce-scatter.18.cloned.1.call-update) | async-done | bytes 2097168 | tf_op jit(solution)/shard_map/reduce_scatter | solution.py:118
  1746.7 583.8 %all-reduce.4.cloned.1.call-done = (f32[1024,1536]{1,0:T(8,128)}, f32[512,1024]{1,0:T(8,128)}, f32[1024,2048]{1,0:T(8,128)}, f32[1024,2048]{1,0:T(8,128)}, f32[2048,1024]{1,0:T(8,128)}) async-done(((f32[1024,1536]{1,0:T(8,128)}, f32[512,1024]{1,0:T(8,128)}, f32[1024,2048]{1,0:T(8,128)}, f32[1024,2048]{1,0:T(8,128)}, f32[2048,1024]{1,0:T(8,128)}), (f32[1024,1536]{1,0:T(8,128)}, f32[512,1024]{1,0:T(8,128)}, ...) | async-done | bytes 33554448 | tf_op jit(solution)/shard_map/psum | solution.py:262
  2338.0 8.6 copy.146
  (703 shorter events, 596.4 us)
Async XLA Ops:
  7.2 90.9 %copy-start = (bf16[1024,1536]{1,0:T(8,128)(2,1)S(1)}, bf16[1024,1536]{1,0:T(8,128)(2,1)}, u32[]{:S(2)}) copy-start(bf16[1024,1536]{1,0:T(8,128)(2,1)} %param.19) | copy-start | bytes 9437188
  7.2 90.9 %all-gather.9.cloned.1.call-start = ((), (), s32[]{:S(2)}) async-start(), calls=%async_computation.9 | async-start | bytes 5242880 | tf_op jit(solution)/shard_map/all_gather | solution.py:114
  14.6 115.0 %reduce-scatter.10.cloned.1.call-start = ((), (), s32[]{:S(2)}) async-start(), calls=%async_computation.10 | async-start | bytes 18874368 | tf_op jit(solution)/shard_map/reduce_scatter | solution.py:124
  109.4 193.1 %all-gather.11.cloned.1.call-start = ((), (), s32[]{:S(2)}) async-start(), calls=%async_computation.11 | async-start | bytes 3145728 | tf_op jit(solution)/shard_map/all_gather | solution.py:128
  111.6 29.9 %copy-start.6 = (f32[2048,32]{0,1:T(8,128)}, f32[2048,32]{0,1:T(8,128)S(1)}, u32[]{:S(2)}) copy-start(f32[2048,32]{0,1:T(8,128)S(1)} %get-tuple-element.362) | copy-start | bytes 786436
  136.2 5.3 copy-start.9
  290.6 165.4 %reduce-scatter.12.cloned.1.call-start = ((), (), s32[]{:S(2)}) async-start(), calls=%async_computation.12 | async-start | bytes 10485760 | tf_op jit(solution)/shard_map/reduce_scatter | solution.py:118
  310.2 151.7 %copy-start.10 = (f32[1024]{0:T(1024)S(1)}, f32[1024]{0:T(1024)}, u32[]{:S(2)}) copy-start(f32[1024]{0:T(1024)} %param.21) | copy-start | bytes 12292
  310.2 228.7 %all-gather.17.cloned.1.call-start = ((), (), s32[]{:S(2)}) async-start(), calls=%async_computation.18 | async-start | bytes 5242880 | tf_op jit(solution)/shard_map/all_gather | solution.py:114
  310.8 309.5 %all-gather.13.cloned.1.call-start = ((), (), s32[]{:S(2)}) async-start(), calls=%async_computation.13 | async-start | bytes 5242880 | tf_op jit(solution)/shard_map/all_gather | solution.py:114
  461.9 480.0 %copy-start.12 = (f32[512]{0:T(512)}, f32[512]{0:T(512)S(1)}, u32[]{:S(2)}) copy-start(f32[512]{0:T(512)S(1)} %add_rsqrt_fusion) | copy-start | bytes 6148
  464.7 189.8 %reduce-scatter.20.cloned.1.call-start = ((), (), s32[]{:S(2)}) async-start(), calls=%async_computation.19 | async-start | bytes 25165824 | tf_op jit(solution)/shard_map/reduce_scatter | solution.py:206
  554.2 123.0 %reduce-scatter.14.cloned.1.call-start = ((), (), s32[]{:S(2)}) async-start(), calls=%async_computation.14 | async-start | bytes 25165824 | tf_op jit(solution)/shard_map/reduce_scatter | solution.py:184
  637.1 70.0 %reduce-scatter.16.cloned.1.call-start = ((), (), s32[]{:S(2)}) async-start(), calls=%async_computation.15 | async-start | bytes 25165824 | tf_op jit(solution)/shard_map/reduce_scatter | solution.py:190
  654.4 106.5 %all-gather.19.cloned.1.call-start = ((), (), s32[]{:S(2)}) async-start(), calls=%async_computation.20 | async-start | bytes 25165824 | tf_op jit(solution)/shard_map/all_gather | solution.py:132
  729.5 206.5 %reduce-scatter.22.cloned.1.call-start = ((), (), s32[]{:S(2)}) async-start(), calls=%async_computation.21 | async-start | bytes 10485760 | tf_op jit(solution)/shard_map/reduce_scatter | solution.py:118
  760.9 14.7 copy-start.20
  790.2 237.9 %all-gather.21.cloned.1.call-start = ((), (), s32[]{:S(2)}) async-start(), calls=%async_computation.22 | async-start | bytes 5242880 | tf_op jit(solution)/shard_map/all_gather | solution.py:114
  946.5 99.3 %reduce-scatter.24.cloned.1.call-start = ((), (), s32[]{:S(2)}) async-start(), calls=%async_computation.23 | async-start | bytes 6291456 | tf_op jit(solution)/shard_map/reduce_scatter | solution.py:124
  1035.0 384.1 %all-gather.23.cloned.1.call-start = ((), (), s32[]{:S(2)}) async-start(), calls=%async_computation.24 | async-start | bytes 9437184 | tf_op jit(solution)/shard_map/all_gather | solution.py:128
  1084.6 5.1 copy-start.3
  1123.8 5.1 copy-start.2
  1123.8 5.1 copy-start.3
  1163.0 5.1 copy-start.2
  1163.0 5.1 copy-start.3
  1202.2 5.1 copy-start.3
  1241.5 5.1 copy-start.3
  1280.7 5.1 copy-start.3
  1319.9 5.1 copy-start.3
  1359.1 5.1 copy-start.3
  1400.9 41.2 %all-gather.15.cloned.1.call-start = ((), (), s32[]{:S(2)}) async-start(), calls=%async_computation.16 | async-start | bytes 12582912 | tf_op jit(solution)/shard_map/all_gather | solution.py:132
  1401.5 189.1 %reduce-scatter.26.cloned.1.call-start = ((), (), s32[]{:S(2)}) async-start(), calls=%async_computation.25 | async-start | bytes 10485760 | tf_op jit(solution)/shard_map/reduce_scatter | solution.py:118
  1430.1 310.9 %reduce-scatter.18.cloned.1.call-start = ((), (), s32[]{:S(2)}) async-start(), calls=%async_computation.17 | async-start | bytes 10485760 | tf_op jit(solution)/shard_map/reduce_scatter | solution.py:118
  1456.6 873.9 %all-reduce.4.cloned.1.call-start = ((), (), s32[]{:S(2)}) async-start(), calls=%async_computation.26 | async-start | bytes 67108864 | tf_op jit(solution)/shard_map/psum | solution.py:262
  1456.9 14.8 copy-start.22
  1493.1 6.6 copy-start.23
  1499.7 6.0 copy-start.21
  1516.6 74.0 %copy-start.14 = (f32[1024]{0:T(1024)S(1)}, f32[1024]{0:T(1024)}, u32[]{:S(2)}) copy-start(f32[1024]{0:T(1024)} %param.18) | copy-start | bytes 12292
  1516.6 74.0 %copy-start.16 = (f32[512]{0:T(512)S(1)}, f32[512]{0:T(512)}, u32[]{:S(2)}) copy-start(f32[512]{0:T(512)} %copy-done.15) | copy-start | bytes 6148
  1516.7 78.9 %copy-start.19 = (f32[1024]{0:T(1024)S(1)}, f32[1024]{0:T(1024)}, u32[]{:S(2)}) copy-start(f32[1024]{0:T(1024)} %get-tuple-element.254) | copy-start | bytes 12292
  1516.7 224.3 %copy-start.11 = (f32[1024]{0:T(1024)S(1)}, f32[1024]{0:T(1024)}, u32[]{:S(2)}) copy-start(f32[1024]{0:T(1024)} %param.21) | copy-start | bytes 12292
  1516.7 224.3 %copy-start.13 = (f32[512]{0:T(512)S(1)}, f32[512]{0:T(512)}, u32[]{:S(2)}) copy-start(f32[512]{0:T(512)} %copy-done.12) | copy-start | bytes 6148
  1516.7 224.3 %copy-start.18 = (f32[512]{0:T(512)S(1)}, f32[512]{0:T(512)}, u32[]{:S(2)}) copy-start(f32[512]{0:T(512)} %copy-done.17) | copy-start | bytes 6148
  2330.6 6.1 copy-start.8
  2336.7 9.9 slice-start.2
  2338.0 8.6 slice-start.3
  2338.0 12.9 slice-start
  2346.6 5.2 slice-start.1
  (58 other events, 150.5 us)
Sparse Core Ops, SparseCore 0:
  14.7 83.3 all-gather.8
  109.6 19.9 reduce-scatter.9
  290.7 11.7 all-gather.10
  310.3 145.6 reduce-scatter.11
  457.4 81.4 all-gather.16
  540.9 79.2 all-gather.12
  622.5 24.7 reduce-scatter.19
  649.7 27.5 reduce-scatter.13
  679.6 27.4 reduce-scatter.15
  729.6 31.3 all-gather.18
  790.3 145.6 reduce-scatter.21
  946.6 81.4 all-gather.20
  1035.1 10.5 reduce-scatter.23
  1401.0 18.0 all-gather.22
  1421.1 21.0 all-gather.14
  1444.9 145.6 reduce-scatter.25
  1593.4 147.5 reduce-scatter.17
  1745.7 584.7 all-reduce.3
where the time goes:
time: 2370 us; the launch traced here: 2360 us
  waiting for transfers between devices  1510 us (64%)
  matrix products  358 us (15%)
  local copies, waits for them, and re-layouts  307 us (13%)
  other arithmetic  93.9 us (4%)
  blocking collectives  55.5 us (2%)
    psum x1, waiting for transfers between devices, shards(): lax.psum((attn_w_grad, out_w_grad, gate_w_grad, up_w_grad, down_grad), 'dp')  584 us
    reduce_scatter x4, waiting for transfers between devices, reduce_tokens(): lax.psum_scatter(term_fn(jnp.int32(0), rows * lax.axis_size('col')), 'col...  465 us
    all_gather x4, waiting for transfers between devices, gather_tokens(): return lax.all_gather(values, 'col', axis=0, tiled=True)  305 us
    dot_general x53, matrix products, transposed_right(): lax.dot_general(left, right, (((1,), (1,)), ((), ())), preferred_element_...  141 us
    dot_general x36, matrix products, transposed_left(): lax.dot_general(left, right, (((0,), (0,)), ((), ())), preferred_element_...  134 us
    squeeze x48, local copies, waits for them, and re-layouts, shards(): lax.map(attend, (query_items, key_items, value_items))  75.3 us
  transfers between devices with their start and end apart: 18, of which 17 were waited for; matrix products, arithmetic and copies ran while one was open for 6% of the time, Pallas kernels for 0%

commit v1 on v0

v1 whole, which is shorter than its diff:
```python
import functools

import jax
import jax.numpy as jnp
from jax import lax
from jax.experimental import pallas as pl
from jax.experimental.pallas import tpu as pltpu
from jax.sharding import PartitionSpec as P

HD = 64
LEN = 1024
PAIR = 6 * HD
BLOCK = 256

norm_epsilon = 1e-05
rope_base = 130000.0
masked_score = -1e30
LOG2E = 1.4426950408889634
BF = jnp.bfloat16
F32 = jnp.float32
MIB = 1024 * 1024


def nn(left, right):
    return lax.dot_general(left, right, (((1,), (0,)), ((), ())), preferred_element_type=F32)


def nt(left, right):
    return lax.dot_general(left, right, (((1,), (1,)), ((), ())), preferred_element_type=F32)


def tn(left, right):
    return lax.dot_general(left, right, (((0,), (0,)), ((), ())), preferred_element_type=F32)


def params(mib):
    return pltpu.CompilerParams(vmem_limit_bytes=mib * MIB)


def rope_tables():
    steps_half = jnp.arange(HD // 2).astype(F32)
    frequency = rope_base ** (-2.0 * steps_half / HD)
    angles = jnp.arange(LEN).astype(F32)[:, None] * frequency[None, :]
    cos, sin = jnp.cos(angles), jnp.sin(angles)
    return (
        jnp.concatenate([cos] * 4, axis=1),
        jnp.concatenate([-sin, sin] * 2, axis=1),
    )


def project_kernel(xo, xt, go, gt, wo, wt, cos, sin, no, nt_, out):
    @pl.when(pl.program_id(0) == 0)
    def _():
        rows = 256
        for i in range(LEN // rows):
            at = slice(i * rows, (i + 1) * rows)
            a = xo[at, :].astype(F32)
            b = xt[at, :].astype(F32)
            total = jnp.sum(a * a, axis=1, keepdims=True) + jnp.sum(b * b, axis=1, keepdims=True)
            scale = lax.rsqrt(total / (a.shape[1] + b.shape[1]) + norm_epsilon)
            no[at, :] = (a * scale * go[...]).astype(BF)
            nt_[at, :] = (b * scale * gt[...]).astype(BF)

    proj = nn(no[...], wo[...]) + nn(nt_[...], wt[...])
    lane = lax.broadcasted_iota(jnp.int32, (LEN, 128), 1)
    low = (lane % HD) < HD // 2
    for piece in range(3):
        part = proj[:, piece * 128 : (piece + 1) * 128]
        swapped = jnp.where(low, pltpu.roll(part, 96, 1), pltpu.roll(part, 32, 1))
        turned = part * cos[...] + swapped * sin[...]
        if piece == 1:
            turned = jnp.where(lane < HD, part, turned)
        if piece == 2:
            turned = jnp.where(lane < HD, turned, part)
        out[:, piece * 128 : (piece + 1) * 128] = turned.astype(BF)


def project(xo, xt, go, gt, wo, wt, cos, sin):
    half, columns = wo.shape
    fixed = lambda shape: pl.BlockSpec(shape, lambda i: (0, 0))
    weight = pl.BlockSpec((half, PAIR), lambda i: (0, i))
    return pl.pallas_call(
        project_kernel,
        grid=(columns // PAIR,),
        in_specs=[fixed((LEN, half))] * 2
        + [fixed((1, half))] * 2
        + [weight] * 2
        + [fixed((LEN, 128))] * 2,
        out_specs=[fixed((LEN, half))] * 2 + [pl.BlockSpec((LEN, PAIR), lambda i: (0, i))],
        out_shape=[jax.ShapeDtypeStruct((LEN, half), BF)] * 2
        + [jax.ShapeDtypeStruct((LEN, columns), BF)],
        compiler_params=params(56),
        cost_estimate=pl.CostEstimate(
            flops=4 * LEN * half * columns, bytes_accessed=2 * LEN * half * 8, transcendentals=0
        ),
    )(xo, xt, go, gt, wo, wt, cos, sin)


def head_parts(qkv, head):
    at = head * 3 * HD
    return qkv[:, at : at + HD], qkv[:, at + HD : at + 2 * HD], qkv[:, at + 2 * HD : at + 3 * HD]


def attend_kernel(qkv, out, log_total):
    scale = HD**-0.5 * LOG2E
    row = lax.broadcasted_iota(jnp.int32, (BLOCK, BLOCK), 0)
    col = lax.broadcasted_iota(jnp.int32, (BLOCK, BLOCK), 1)
    for head in range(2):
        q, k, v = head_parts(qkv, head)
        for i in range(LEN // BLOCK):
            start, end = i * BLOCK, (i + 1) * BLOCK
            scores = nt(q[start:end], k[:end])
            last = jnp.where(row >= col, scores[:, start:], masked_score)
            scores = jnp.concatenate([scores[:, :start], last], axis=1) if i else last
            peak = jnp.max(scores, axis=1, keepdims=True)
            probs = jnp.exp2((scores - peak) * scale)
            total = jnp.sum(probs, axis=1, keepdims=True)
            mixed = nn(probs.astype(BF), v[:end]) / total
            out[start:end, head * HD : (head + 1) * HD] = mixed.astype(BF)
            log_total[start:end, head * HD : (head + 1) * HD] = jnp.broadcast_to(
                peak * scale + jnp.log2(total), (BLOCK, HD)
            )


def attend(qkv):
    pairs = qkv.shape[1] // PAIR
    narrow = pl.BlockSpec((LEN, 2 * HD), lambda i: (0, i))
    return pl.pallas_call(
        attend_kernel,
        grid=(pairs,),
        in_specs=[pl.BlockSpec((LEN, PAIR), lambda i: (0, i))],
        out_specs=[narrow, narrow],
        out_shape=[
            jax.ShapeDtypeStruct((LEN, pairs * 2 * HD), BF),
            jax.ShapeDtypeStruct((LEN, pairs * 2 * HD), F32),
        ],
        compiler_params=params(48),
        cost_estimate=pl.CostEstimate(
            flops=pairs * 8 * LEN * LEN * 256, bytes_accessed=LEN * pairs * 1500, transcendentals=0
        ),
    )(qkv)


def attend_back_kernel(qkv, grad, mixed, log_total, cos, sin, out):
    scale = HD**-0.5 * LOG2E
    row = lax.broadcasted_iota(jnp.int32, (BLOCK, BLOCK), 0)
    col = lax.broadcasted_iota(jnp.int32, (BLOCK, BLOCK), 1)
    blocks = LEN // BLOCK
    totals = jnp.transpose(log_total[...])
    product = jnp.transpose(grad[...].astype(F32) * mixed[...].astype(F32))
    cosines, sines = cos[:, :HD], sin[:, :HD]

    def unturn(part, start, end):
        swapped = jnp.concatenate([part[:, HD // 2 :], part[:, : HD // 2]], axis=1)
        return (part * cosines[start:end] - swapped * sines[start:end]).astype(BF)

    for head in range(2):
        q, k, v = head_parts(qkv, head)
        at = head * 3 * HD
        g = grad[:, head * HD : (head + 1) * HD]
        total = totals[head * HD : head * HD + 1]
        center = jnp.sum(product[head * HD : (head + 1) * HD], axis=0, keepdims=True)
        query_grad = [None] * blocks
        for j in range(blocks):
            start, end = j * BLOCK, (j + 1) * BLOCK
            scores = nt(k[start:end], q[start:])
            probs = jnp.exp2(scores * scale - total[:, start:])
            first = jnp.where(col >= row, probs[:, :BLOCK], 0.0)
            probs = jnp.concatenate([first, probs[:, BLOCK:]], axis=1) if end < LEN else first
            out[start:end, at + 2 * HD : at + 3 * HD] = nn(probs.astype(BF), g[start:]).astype(BF)
            prob_grad = nt(v[start:end], g[start:])
            score_grad = (probs * (prob_grad - center[:, start:])).astype(BF)
            key_grad = nn(score_grad, q[start:]) * (HD**-0.5)
            out[start:end, at + HD : at + 2 * HD] = unturn(key_grad, start, end)
            term = tn(k[start:end], score_grad)
            for b in range(j, blocks):
                here = term[:, (b - j) * BLOCK : (b - j + 1) * BLOCK]
                query_grad[b] = here if query_grad[b] is None else query_grad[b] + here
        for b in range(blocks):
            start, end = b * BLOCK, (b + 1) * BLOCK
            out[start:end, at : at + HD] = unturn(
                jnp.transpose(query_grad[b]) * (HD**-0.5), start, end
            )


def attend_back(qkv, grad, mixed, log_total, cos, sin):
    pairs = qkv.shape[1] // PAIR
    wide = pl.BlockSpec((LEN, PAIR), lambda i: (0, i))
    narrow = pl.BlockSpec((LEN, 2 * HD), lambda i: (0, i))
    fixed = pl.BlockSpec((LEN, 128), lambda i: (0, 0))
    return pl.pallas_call(
        attend_back_kernel,
        grid=(pairs,),
        in_specs=[wide, narrow, narrow, narrow, fixed, fixed],
        out_specs=wide,
        out_shape=jax.ShapeDtypeStruct((LEN, pairs * PAIR), BF),
        compiler_params=params(56),
        cost_estimate=pl.CostEstimate(
            flops=pairs * 12 * LEN * LEN * 256, bytes_accessed=LEN * pairs * 2500, transcendentals=0
        ),
    )(qkv, grad, mixed, log_total, cos, sin)


def residual_kernel(count, *refs):
    mixed = refs[:count]
    wo, wt, xo, xt, go, gt, ro, rt, no, nt_ = refs[count:]
    a = xo[...].astype(F32)
    b = xt[...].astype(F32)
    for step in range(count):
        left = mixed[step][...]
        a = a + nn(left, wo[step])
        b = b + nn(left, wt[step])
    total = jnp.sum(a * a, axis=1, keepdims=True) + jnp.sum(b * b, axis=1, keepdims=True)
    scale = lax.rsqrt(total / (a.shape[1] + b.shape[1]) + norm_epsilon)
    ro[...] = a
    rt[...] = b
    no[...] = (a * scale * go[...]).astype(BF)
    nt_[...] = (b * scale * gt[...]).astype(BF)


def add_residual(mixed, wo, wt, xo, xt, go, gt):
    count, depth, half = wo.shape
    rows = 256
    left = pl.BlockSpec((rows, depth), lambda i: (i, 0))
    weight = pl.BlockSpec((count, depth, half), lambda i: (0, 0, 0))
    part = pl.BlockSpec((rows, half), lambda i: (i, 0))
    gain = pl.BlockSpec((1, half), lambda i: (0, 0))
    return pl.pallas_call(
        functools.partial(residual_kernel, count),
        grid=(LEN // rows,),
        in_specs=[left] * count + [weight] * 2 + [part] * 2 + [gain] * 2,
        out_specs=[part] * 4,
        out_shape=[jax.ShapeDtypeStruct((LEN, half), F32)] * 2
        + [jax.ShapeDtypeStruct((LEN, half), BF)] * 2,
        compiler_params=params(56),
        cost_estimate=pl.CostEstimate(
            flops=4 * LEN * half * count * depth, bytes_accessed=LEN * half * 20, transcendentals=0
        ),
    )(*mixed, wo, wt, xo, xt, go, gt)


def feed_kernel(no, nt_, co, ct, gwo, gwt, uwo, uwt, dwo, dwt, hidden, gate_grad, upper_grad):
    gate = nn(no[...], gwo[...]) + nn(nt_[...], gwt[...])
    upper = nn(no[...], uwo[...]) + nn(nt_[...], uwt[...])
    sigmoid = 1.0 / (1.0 + jnp.exp(-gate))
    silu = gate * sigmoid
    hidden[...] = (silu * upper).astype(BF)
    hidden_grad = nt(co[...], dwo[...]) + nt(ct[...], dwt[...])
    gate_grad[...] = (hidden_grad * upper * sigmoid * (1.0 + gate * (1.0 - sigmoid))).astype(BF)
    upper_grad[...] = (hidden_grad * silu).astype(BF)


def feed(no, nt_, co, ct, gwo, gwt, uwo, uwt, dwo, dwt):
    half, units = gwo.shape
    tokens = pl.BlockSpec((LEN, half), lambda i: (0, 0))
    weight = pl.BlockSpec((half, BLOCK), lambda i: (0, i))
    down = pl.BlockSpec((BLOCK, half), lambda i: (i, 0))
    out = pl.BlockSpec((LEN, BLOCK), lambda i: (0, i))
    return pl.pallas_call(
        feed_kernel,
        grid=(units // BLOCK,),
        in_specs=[tokens] * 4 + [weight] * 4 + [down] * 2,
        out_specs=[out] * 3,
        out_shape=[jax.ShapeDtypeStruct((LEN, units), BF)] * 3,
        compiler_params=params(60),
        cost_estimate=pl.CostEstimate(
            flops=12 * LEN * half * units, bytes_accessed=12 * half * units, transcendentals=0
        ),
    )(no, nt_, co, ct, gwo, gwt, uwo, uwt, dwo, dwt)


def swap_row(values):
    return lax.ppermute(values, "row", [(0, 1), (1, 0)])


class Ring:
    def __init__(self):
        count = lax.axis_size("col")
        order = list(range(0, count, 2)) + list(range(count - 1 - count % 2, 0, -2))
        self.count = count
        self.order = order
        self.table = jnp.array(order, jnp.int32)
        place = [order.index(i) for i in range(count)]
        self.here = jnp.array(place, jnp.int32)[lax.axis_index("col")]
        self.core = lax.axis_index("row")

    def shift(self, values, by):
        count, order = self.count, self.order
        pairs = [(order[p], order[(p + by) % count]) for p in range(count)]
        return lax.ppermute(values, "col", pairs)

    def owner(self, back):
        return self.table[(self.here - back) % self.count]

    def split(self, owner):
        per = self.count // 2
        return owner // per, owner % per

    def gather_list(self, values):
        out = [values]
        for _ in range(self.count - 1):
            out.append(self.shift(out[-1], 1))
        return out

    def place(self, blocks, direction):
        rows, columns = blocks[0].shape
        out = jnp.zeros((self.count * rows, columns), blocks[0].dtype)
        for step, block in enumerate(blocks):
            sequence, at = self.split(self.owner(direction * step))
            slot = jnp.where(sequence == self.core, 0, self.count // 2) + at
            out = lax.dynamic_update_slice(out, block, (slot * rows, 0))
        return out

    def gather_tokens(self, values):
        both = self.place(self.gather_list(values), 1)
        half = both.shape[0] // 2
        return both[:half], swap_row(both[half:])

    def reduce_tokens(self, own, other):
        other = swap_row(other.astype(BF))
        own = own.astype(BF)
        rows = own.shape[0] * 2 // self.count

        def term(back):
            sequence, at = self.split(self.owner(back))
            take = lambda values: lax.dynamic_slice_in_dim(values, at * rows, rows, 0)
            return jnp.where(sequence == self.core, take(own), take(other))

        total = term(1)
        for step in range(1, self.count):
            total = self.shift(total.astype(BF), 1).astype(F32) + term(step + 1).astype(F32)
        return total


def reduce_weights(own, other):
    mine = own
    theirs = swap_row(other)
    rows = own.shape[0]
    index = lax.axis_index("dp")
    bit_x, bit_y = index % 2, index // 2
    hop_x = lambda v: lax.ppermute(v, "dp", [(i, i ^ 1) for i in range(4)])
    hop_y = lambda v: lax.ppermute(v, "dp", [(i, i ^ 2) for i in range(4)])

    def first(base, bit):
        at = base + bit * (rows // 4)
        take = lambda v: lax.dynamic_slice_in_dim(v, at, rows // 4, 0).astype(F32)
        return take(mine) + take(theirs)

    def part(values, bit):
        size = values.shape[0] // 2
        return lax.dynamic_slice_in_dim(values, bit * size, size, 0)

    pieces = []
    for base, bit_1, hop_1, bit_2, hop_2 in (
        (0, bit_x, hop_x, bit_y, hop_y),
        (rows // 2, bit_y, hop_y, bit_x, hop_x),
    ):
        got = hop_1(first(base, 1 - bit_1).astype(BF))
        kept = first(base, bit_1) + got.astype(F32)
        got = hop_2(part(kept, 1 - bit_2).astype(BF))
        kept = (part(kept, bit_2) + got.astype(F32)).astype(BF)
        got = hop_2(kept)
        low = jnp.where(bit_2 == 0, kept, got)
        high = jnp.where(bit_2 == 0, got, kept)
        both = jnp.concatenate([low, high], axis=0)
        got = hop_1(both)
        pieces.append(jnp.where(bit_1 == 0, both, got))
        pieces.append(jnp.where(bit_1 == 0, got, both))
    return jnp.concatenate(pieces, axis=0).astype(F32)


def gather_out_weight(ring, weight):
    rows, half = weight.shape
    size = rows // 4
    index = lax.axis_index("dp")
    quarter = lax.dynamic_slice_in_dim(weight, index * size, size, 0)
    held = jnp.stack(ring.gather_list(quarter), axis=0)
    hop_x = lambda v: lax.ppermute(v, "dp", [(i, i ^ 1) for i in range(4)])
    hop_y = lambda v: lax.ppermute(v, "dp", [(i, i ^ 2) for i in range(4)])
    beside = hop_x(held)
    even = index % 2 == 0
    pair = jnp.concatenate(
        [jnp.where(even, held, beside), jnp.where(even, beside, held)], axis=1
    )
    beside = hop_y(pair)
    low = index // 2 == 0
    own = jnp.concatenate([jnp.where(low, pair, beside), jnp.where(low, beside, pair)], axis=1)
    return own, swap_row(own)


def row_total(values):
    return values + swap_row(values)


def shards(
    block_input,
    attn_gain,
    attn_weight,
    out_weight,
    feed_gain,
    gate_weight,
    up_weight,
    down_weight,
    out_cotangent,
):
    ring = Ring()
    rows, half = block_input.shape
    width = 2 * half
    cos, sin = rope_tables()
    go1, go2 = attn_gain[None, :], feed_gain[None, :]
    gains = swap_row(jnp.concatenate([go1, go2], axis=0))
    gt1, gt2 = gains[:1], gains[1:]

    xo, xt = ring.gather_tokens(block_input)
    aw_other = swap_row(attn_weight)
    n1o, n1t, qkv = project(xo, xt, go1, gt1, attn_weight, aw_other, cos, sin)
    mixed, log_total = attend(qkv)
    ow_own, ow_other = gather_out_weight(ring, out_weight)
    co, ct = ring.gather_tokens(out_cotangent)
    mixed_all = ring.gather_list(mixed)
    res_o, res_t, n2o, n2t = add_residual(mixed_all, ow_own, ow_other, xo, xt, go2, gt2)

    gw_other, uw_other, dw_other = swap_row(gate_weight), swap_row(up_weight), swap_row(down_weight)
    hidden, gate_grad, upper_grad = feed(
        n2o, n2t, co, ct, gate_weight, gw_other, up_weight, uw_other, down_weight, dw_other
    )
    second_grad = ring.reduce_tokens(
        nt(gate_grad, gate_weight) + nt(upper_grad, up_weight),
        nt(gate_grad, gw_other) + nt(upper_grad, uw_other),
    )

    sequence, at = ring.split(lax.axis_index("col"))
    take = lambda v: lax.dynamic_slice_in_dim(v, at * rows, rows, 0)
    residual = jnp.where(sequence == ring.core, take(res_o), swap_row(take(res_t)))
    second_scale = lax.rsqrt(
        row_total(jnp.sum(residual * residual, axis=1, keepdims=True)) / width + norm_epsilon
    )
    second_hat = residual * second_scale
    feed_part = jnp.sum(second_grad * second_hat, axis=0)
    weighted = second_grad * go2
    second_mean = row_total(jnp.sum(weighted * second_hat, axis=1, keepdims=True)) / width
    residual_grad = out_cotangent.astype(F32) + second_scale * (weighted - second_hat * second_mean)
    residual_low = residual_grad.astype(BF)

    size = rows // 2
    mine = lax.dynamic_slice_in_dim(residual_low, ring.core * size, size, 0)
    theirs = swap_row(lax.dynamic_slice_in_dim(residual_low, (1 - ring.core) * size, size, 0))
    heads = mixed.shape[1]
    grads = (
        nt(mine, ow_own.reshape(-1, half)) + nt(theirs, ow_other.reshape(-1, half))
    ).astype(BF)
    arrived = [
        ring.shift(grads[:, s * heads : (s + 1) * heads], -s) if s else grads[:, :heads]
        for s in range(ring.count)
    ]
    both = ring.place(arrived, -1)
    mine, theirs = both[: LEN // 2], swap_row(both[LEN // 2 :])
    mine, theirs = (v.reshape(-1, size, heads) for v in (mine, theirs))
    first = ring.core == 0
    mixed_grad = jnp.stack(
        [jnp.where(first, mine, theirs), jnp.where(first, theirs, mine)], axis=1
    ).reshape(LEN, heads)
    projected_grad = attend_back(qkv, mixed_grad, mixed, log_total, cos, sin)
    first_grad = ring.reduce_tokens(nt(projected_grad, attn_weight), nt(projected_grad, aw_other))

    block_output = (
        residual + ring.reduce_tokens(nn(hidden, down_weight), nn(hidden, dw_other))
    ).astype(BF)

    down_summed = reduce_weights_columns(hidden, co, ct)
    gate_summed = reduce_weights(tn(n2o, gate_grad).astype(BF), tn(n2t, gate_grad).astype(BF))
    up_summed = reduce_weights(tn(n2o, upper_grad).astype(BF), tn(n2t, upper_grad).astype(BF))
    ro, rt = ring.gather_tokens(residual_low)
    out_summed = reduce_weights(tn(mixed, ro).astype(BF), tn(mixed, rt).astype(BF))
    attn_summed = reduce_weights(
        tn(n1o, projected_grad).astype(BF), tn(n1t, projected_grad).astype(BF)
    )

    inputs = block_input.astype(F32)
    first_scale = lax.rsqrt(
        row_total(jnp.sum(inputs * inputs, axis=1, keepdims=True)) / width + norm_epsilon
    )
    first_hat = inputs * first_scale
    attn_part = jnp.sum(first_grad * first_hat, axis=0)
    weighted_first = first_grad * go1
    first_mean = row_total(jnp.sum(weighted_first * first_hat, axis=1, keepdims=True)) / width
    input_grad = residual_grad + first_scale * (weighted_first - first_hat * first_mean)
    attn_gain_grad, feed_gain_grad = lax.psum((attn_part, feed_part), ("dp", "col"))
    return (
        block_output,
        input_grad,
        attn_gain_grad,
        attn_summed,
        out_summed,
        feed_gain_grad,
        gate_summed,
        up_summed,
        down_summed,
    )


def reduce_weights_columns(hidden, co, ct):
    return reduce_weights(tn(hidden, co).astype(BF), tn(hidden, ct).astype(BF))


def solution(mesh):
    in_specs = (
        P(("dp", "col"), "row"),
        P("row"),
        P("row", "col"),
        P("col", "row"),
        P("row"),
        P("row", "col"),
        P("row", "col"),
        P("col", "row"),
        P(("dp", "col"), "row"),
    )
    out_specs = (
        P(("dp", "col"), "row"),
        P(("dp", "col"), "row"),
        P("row"),
        P("row", "col"),
        P("col", "row"),
        P("row"),
        P("row", "col"),
        P("row", "col"),
        P("col", "row"),
    )
    return jax.shard_map(shards, mesh=mesh, in_specs=in_specs, out_specs=out_specs, check_vma=False)
```

time: 2370 us -> 1020 us (0.43)
  waiting for transfers between devices: 1510 us -> 490 us
  local copies, waits for them, and re-layouts: 307 us -> 27.7 us
  matrix products: 358 us -> 116 us
  starting transfers between devices: 2.63 us -> 124 us
  Pallas kernels: 0 us -> 103 us
    psum x1 -> x0, waiting for transfers between devices: 584 us -> none  [shards(): lax.psum((attn_w_grad, out_w_grad, gate_w_grad, up_w_grad, down_grad), 'dp')]
    reduce_scatter x9 -> x0, waiting for transfers between devices: 546 us -> none  [the longest x4 465 us: reduce_tokens(): lax.psum_scatter(term_fn(jnp.int32(0), rows * lax.axis_size('col')), 'col...]
    ppermute x0 -> x93, waiting for transfers between devices: none -> 490 us  [the longest x27 247 us: shift(): return lax.ppermute(values, 'col', pairs)]
    all_gather x8 -> x0, waiting for transfers between devices: 377 us -> none  [the longest x4 305 us: gather_tokens(): return lax.all_gather(values, 'col', axis=0, tiled=True)]
    dot_general x126 -> x20, matrix products: 358 us -> 116 us  [the longest x10 50.9 us: tn(): lax.dot_general(left, right, (((0,), (0,)), ((), ())), preferred_element_...]
    ppermute x0 -> x93, starting transfers between devices: none -> 124 us  [the longest x27 65.4 us: shift(): return lax.ppermute(values, 'col', pairs)]
    pallas_call x0 -> x5, Pallas kernels: none -> 103 us  [the longest x1 33.9 us: feed(): pl.pallas_call(feed_kernel, grid=(units // BLOCK,), in_specs=[tokens] * 4...]
    squeeze x49 -> x0, local copies, waits for them, and re-layouts: 77.8 us -> none  [the longest x48 75.3 us: shards(): lax.map(attend, (query_items, key_items, value_items))]
  transfers between devices with their start and end apart: 18 -> 93, of which waited for: 17 -> 40; matrix products, arithmetic and copies ran while one was open for 6% -> 18% of each run, Pallas kernels for 0% -> 7%
where the time goes in v1:
time: 1020 us; the launch traced here: 1010 us
  waiting for transfers between devices  490 us (48%)
  starting transfers between devices  124 us (12%)
  matrix products  116 us (11%)
  Pallas kernels  103 us (10%)
  other arithmetic  81.8 us (8%)
  blocking collectives  40.9 us (4%)
  between operations  30.2 us (3%)
  local copies, waits for them, and re-layouts  27.7 us (3%)
    ppermute x27, waiting for transfers between devices, shift(): return lax.ppermute(values, 'col', pairs)  247 us
    ppermute x20, waiting for transfers between devices, reduce_weights(): hop_y = lambda v: lax.ppermute(v, 'dp', [(i, i ^ 2) for i in range(4)])  136 us
    ppermute x20, waiting for transfers between devices, reduce_weights(): hop_x = lambda v: lax.ppermute(v, 'dp', [(i, i ^ 1) for i in range(4)])  106 us
    ppermute x27, starting transfers between devices, shift(): return lax.ppermute(values, 'col', pairs)  65.4 us
    dot_general x10, matrix products, tn(): lax.dot_general(left, right, (((0,), (0,)), ((), ())), preferred_element_...  50.9 us
    dot_general x8, matrix products, nt(): lax.dot_general(left, right, (((1,), (1,)), ((), ())), preferred_element_...  49.2 us
    psum x1, blocking collectives, shards(): lax.psum((attn_part, feed_part), ('dp', 'col'))  40.9 us
    pallas_call x1, Pallas kernels, feed(): pl.pallas_call(feed_kernel, grid=(units // BLOCK,), in_specs=[tokens] * 4...  33.9 us
  transfers between devices with their start and end apart: 93, of which 40 were waited for; matrix products, arithmetic and copies ran while one was open for 18% of the time, Pallas kernels for 7%

profile of v1, /device:TPU:0, one launch (start us, length us, event | category | flops | bytes accessed | tf_op | source)
XLA Modules:
  0.0 1013.6 jit_solution(5484778901561872267)
XLA Ops:
  6.4 26.6 %collective-permute-done.9 = bf16[128,1024]{1,0:T(8,128)(2,1)S(1)} collective-permute-done((bf16[128,1024]{1,0:T(8,128)(2,1)S(1)}, bf16[128,1024]{1,0:T(8,128)(2,1)S(1)}, u32[]{:S(2)}, u32[]{:S(2)}) %collective-permute-start.9) | collective-permute-done | bytes 262176 | tf_op jit(solution)/shard_map/ppermute | solution.py:290
  44.6 6.7 collective-permute-done.11
  53.4 17.3 %collective-permute-done.1 = bf16[512,1024]{1,0:T(8,128)(2,1)} collective-permute-done((bf16[512,1024]{1,0:T(8,128)(2,1)S(1)}, bf16[512,1024]{1,0:T(8,128)(2,1)}, u32[]{:S(2)}, u32[]{:S(2)}) %collective-permute-start.1) | collective-permute-done | bytes 1048608 | tf_op jit(solution)/shard_map/ppermute | solution.py:290
  107.5 9.1 collective-permute-done.16
  128.5 10.6 %collective-permute-done.17 = bf16[512,1024]{1,0:T(8,128)(2,1)} collective-permute-done((bf16[512,1024]{1,0:T(8,128)(2,1)}, bf16[512,1024]{1,0:T(8,128)(2,1)}, u32[]{:S(2)}, u32[]{:S(2)}) %collective-permute-start.17) | collective-permute-done | bytes 1048608 | tf_op jit(solution)/shard_map/ppermute | solution.py:290
  143.2 17.3 %shard_map.178 = (bf16[1024,1024]{1,0:T(8,128)(2,1)}, bf16[1024,1024]{1,0:T(8,128)(2,1)}, bf16[1024,1536]{1,0:T(8,128)(2,1)}) custom-call(bf16[1024,1024]{1,0:T(8,128)(2,1)} %get-tuple-element.58.xo.refs_6_, bf16[1024,1024]{1,0:T(8,128)(2,1)} %collective-permute-done.3.xt.refs_7_, f32[1,1024]{1,0:T(1,128)} %bitcast.78, f32[1,1024]{1,0:T(1,128)} %get-tuple-element.112.gt, ...), custom_call_target="tpu_custom_call" | custom-call | flops 6442450944 | bytes 16777216 | tf_op jit(solution)/shard_map/pallas_call | solution.py:82
  160.6 15.5 %shard_map.179 = (bf16[1024,512]{1,0:T(8,128)(2,1)S(1)}, f32[1024,512]{1,0:T(8,128)S(1)}) custom-call(bf16[1024,1536]{1,0:T(8,128)(2,1)} %get-tuple-element.21.qkv), custom_call_target="tpu_custom_call" | custom-call | flops 8589934592 | bytes 6144000 | tf_op jit(solution)/shard_map/pallas_call | solution.py:128
  176.3 24.7 %collective-permute-done.6.refs_1_ = bf16[1024,512]{1,0:T(8,128)(2,1)S(1)} collective-permute-done((bf16[1024,512]{1,0:T(8,128)(2,1)S(1)}, bf16[1024,512]{1,0:T(8,128)(2,1)S(1)}, u32[]{:S(2)}, u32[]{:S(2)}) %collective-permute-start.6) | collective-permute-done | bytes 1048608 | tf_op jit(solution)/shard_map/ppermute | solution.py:290
  208.3 16.8 %collective-permute-done.7.refs_2_ = bf16[1024,512]{1,0:T(8,128)(2,1)} collective-permute-done((bf16[1024,512]{1,0:T(8,128)(2,1)S(1)}, bf16[1024,512]{1,0:T(8,128)(2,1)}, u32[]{:S(2)}, u32[]{:S(2)}) %collective-permute-start.7) | collective-permute-done | bytes 1048608 | tf_op jit(solution)/shard_map/ppermute | solution.py:290
  239.0 12.3 %collective-permute-done.8.refs_3_ = bf16[1024,512]{1,0:T(8,128)(2,1)S(1)} collective-permute-done((bf16[1024,512]{1,0:T(8,128)(2,1)}, bf16[1024,512]{1,0:T(8,128)(2,1)S(1)}, u32[]{:S(2)}, u32[]{:S(2)}) %collective-permute-start.8) | collective-permute-done | bytes 1048608 | tf_op jit(solution)/shard_map/ppermute | solution.py:290
  252.4 16.1 %shard_map.180 = (f32[1024,1024]{1,0:T(8,128)}, f32[1024,1024]{1,0:T(8,128)}, bf16[1024,1024]{1,0:T(8,128)(2,1)}, bf16[1024,1024]{1,0:T(8,128)(2,1)}) custom-call(bf16[1024,512]{1,0:T(8,128)(2,1)} %copy-done.2, bf16[1024,512]{1,0:T(8,128)(2,1)} %copy-done.59, bf16[1024,512]{1,0:T(8,128)(2,1)} %collective-permute-done.7.refs_2_, ...), custom_call_target="tpu_custom_call" | custom-call | flops 8589934592 | bytes 20971520 | tf_op jit(solution)/shard_map/pallas_call | solution.py:228
  268.6 33.9 %shard_map.181 = (bf16[1024,2048]{1,0:T(8,128)(2,1)}, bf16[1024,2048]{1,0:T(8,128)(2,1)}, bf16[1024,2048]{1,0:T(8,128)(2,1)}) custom-call(bf16[1024,1024]{1,0:T(8,128)(2,1)} %get-tuple-element.25.no, bf16[1024,1024]{1,0:T(8,128)(2,1)} %get-tuple-element.26.nt_, bf16[1024,1024]{1,0:T(8,128)(2,1)} %get-tuple-element.54.co, ...), custom_call_target="tpu_custom_call" | custom-call | flops 25769803776 | bytes 25165824 | tf_op jit(solution)/shard_map/pallas_call | solution.py:259
  302.5 7.7 fusion.28
  310.3 6.3 convolution_convert_fusion.6
  316.6 6.3 fusion.29
  322.9 7.2 add_convert_fusion
  330.2 7.0 add_convert_fusion.1
  337.2 8.1 convolution_convert_fusion.11
  345.3 7.6 convolution_convert_fusion.10
  353.5 6.2 convolution_convert_fusion.4
  361.3 6.6 convolution_convert_fusion.7
  371.7 9.6 convolution_convert_fusion.2
  381.8 12.6 %collective-permute-done.29 = bf16[512,1024]{1,0:T(8,128)(2,1)S(1)} collective-permute-done((bf16[512,1024]{1,0:T(8,128)(2,1)S(1)}, bf16[512,1024]{1,0:T(8,128)(2,1)S(1)}, u32[]{:S(2)}, u32[]{:S(2)}) %collective-permute-start.29) | collective-permute-done | bytes 1048608 | tf_op jit(solution)/shard_map/ppermute | solution.py:290
  403.3 16.2 %collective-permute-done.24 = bf16[512,1024]{1,0:T(8,128)(2,1)S(1)} collective-permute-done((bf16[512,1024]{1,0:T(8,128)(2,1)S(1)}, bf16[512,1024]{1,0:T(8,128)(2,1)S(1)}, u32[]{:S(2)}, u32[]{:S(2)}) %collective-permute-start.24) | collective-permute-done | bytes 1048608 | tf_op jit(solution)/shard_map/ppermute | solution.py:290
  423.8 7.0 convolution_convert_fusion.3
  435.2 12.2 %collective-permute-done.30 = bf16[512,1024]{1,0:T(8,128)(2,1)} collective-permute-done((bf16[512,1024]{1,0:T(8,128)(2,1)S(1)}, bf16[512,1024]{1,0:T(8,128)(2,1)}, u32[]{:S(2)}, u32[]{:S(2)}) %collective-permute-start.30) | collective-permute-done | bytes 1048608 | tf_op jit(solution)/shard_map/ppermute | solution.py:290
  456.2 13.7 %collective-permute-done.25 = bf16[512,1024]{1,0:T(8,128)(2,1)S(1)} collective-permute-done((bf16[512,1024]{1,0:T(8,128)(2,1)S(1)}, bf16[512,1024]{1,0:T(8,128)(2,1)S(1)}, u32[]{:S(2)}, u32[]{:S(2)}) %collective-permute-start.25) | collective-permute-done | bytes 1048608 | tf_op jit(solution)/shard_map/ppermute | solution.py:290
  478.0 14.3 %collective-permute-done.31 = bf16[512,1024]{1,0:T(8,128)(2,1)S(1)} collective-permute-done((bf16[512,1024]{1,0:T(8,128)(2,1)S(1)}, bf16[512,1024]{1,0:T(8,128)(2,1)S(1)}, u32[]{:S(2)}, u32[]{:S(2)}) %collective-permute-start.31) | collective-permute-done | bytes 1048608 | tf_op jit(solution)/shard_map/ppermute | solution.py:290
  506.6 18.2 %collective-permute-done.85 = bf16[512,1024]{1,0:T(8,128)(2,1)S(1)} collective-permute-done((bf16[512,1024]{1,0:T(8,128)(2,1)S(1)}, bf16[512,1024]{1,0:T(8,128)(2,1)S(1)}, u32[]{:S(2)}, u32[]{:S(2)}) %collective-permute-start.85) | collective-permute-done | bytes 1048608 | tf_op jit(solution)/shard_map/ppermute | solution.py:341
  535.6 4.9 fusion.30
  548.7 6.9 collective-permute-done.86
  569.1 59.2 %collective-permute-done.87 = bf16[256,1024]{1,0:T(8,128)(2,1)S(1)} collective-permute-done((bf16[256,1024]{1,0:T(8,128)(2,1)S(1)}, bf16[256,1024]{1,0:T(8,128)(2,1)S(1)}, u32[]{:S(2)}, u32[]{:S(2)}) %collective-permute-start.87) | collective-permute-done | bytes 524320 | tf_op jit(solution)/shard_map/ppermute | solution.py:342
  645.1 5.6 collective-permute-done.53
  654.2 20.5 %shard_map.182 = bf16[1024,1536]{1,0:T(8,128)(2,1)} custom-call(bf16[1024,1536]{1,0:T(8,128)(2,1)} %get-tuple-element.21.qkv, bf16[1024,512]{1,0:T(8,128)(2,1)} %bitcast.69, bf16[1024,512]{1,0:T(8,128)(2,1)} %copy-done.2, f32[1024,512]{1,0:T(8,128)} %copy-done.4, f32[1024,128]{1,0:T(8,128)} %get-tuple-element.124.cos, f32[1024,128]{1,0:T(8,128)} %get-tuple-element.125.sin), custom_call_target="tpu_custom_call" | custom-call | flops 12884901888 | bytes 10240000 | tf_op jit(solution)/shard_map/pallas_call | solution.py:191
  674.7 6.4 convolution_convert_fusion.9
  685.0 6.7 convolution_convert_fusion.8
  702.9 30.1 %collective-permute-done.73 = bf16[128,2048]{1,0:T(8,128)(2,1)S(1)} collective-permute-done((bf16[128,2048]{1,0:T(8,128)(2,1)S(1)}, bf16[128,2048]{1,0:T(8,128)(2,1)S(1)}, u32[]{:S(2)}, u32[]{:S(2)}) %collective-permute-start.73) | collective-permute-done | bytes 524320 | tf_op jit(solution)/shard_map/ppermute | solution.py:341
  738.5 25.4 %collective-permute-done.82 = bf16[128,2048]{1,0:T(8,128)(2,1)S(1)} collective-permute-done((bf16[128,2048]{1,0:T(8,128)(2,1)S(1)}, bf16[128,2048]{1,0:T(8,128)(2,1)S(1)}, u32[]{:S(2)}, u32[]{:S(2)}) %collective-permute-start.82) | collective-permute-done | bytes 524320 | tf_op jit(solution)/shard_map/ppermute | solution.py:341
  765.6 7.5 collective-permute-done.91
  778.0 21.9 %collective-permute-done.74 = bf16[256,2048]{1,0:T(8,128)(2,1)S(1)} collective-permute-done((bf16[256,2048]{1,0:T(8,128)(2,1)S(1)}, bf16[256,2048]{1,0:T(8,128)(2,1)S(1)}, u32[]{:S(2)}, u32[]{:S(2)}) %collective-permute-start.74) | collective-permute-done | bytes 1048608 | tf_op jit(solution)/shard_map/ppermute | solution.py:342
  806.3 16.0 %collective-permute-done.92 = bf16[512,1024]{1,0:T(8,128)(2,1)S(1)} collective-permute-done((bf16[512,1024]{1,0:T(8,128)(2,1)S(1)}, bf16[512,1024]{1,0:T(8,128)(2,1)S(1)}, u32[]{:S(2)}, u32[]{:S(2)}) %collective-permute-start.92) | collective-permute-done | bytes 1048608 | tf_op jit(solution)/shard_map/ppermute | solution.py:342
  824.7 14.3 %collective-permute-done.83 = bf16[256,2048]{1,0:T(8,128)(2,1)S(1)} collective-permute-done((bf16[256,2048]{1,0:T(8,128)(2,1)S(1)}, bf16[256,2048]{1,0:T(8,128)(2,1)S(1)}, u32[]{:S(2)}, u32[]{:S(2)}) %collective-permute-start.83) | collective-permute-done | bytes 1048608 | tf_op jit(solution)/shard_map/ppermute | solution.py:342
  853.0 16.8 %collective-permute-done.40 = bf16[512,1024]{1,0:T(8,128)(2,1)S(1)} collective-permute-done((bf16[512,1024]{1,0:T(8,128)(2,1)S(1)}, bf16[512,1024]{1,0:T(8,128)(2,1)S(1)}, u32[]{:S(2)}, u32[]{:S(2)}) %collective-permute-start.40) | collective-permute-done | bytes 1048608 | tf_op jit(solution)/shard_map/ppermute | solution.py:290
  877.2 18.2 %collective-permute-done.41 = bf16[512,1024]{1,0:T(8,128)(2,1)S(1)} collective-permute-done((bf16[512,1024]{1,0:T(8,128)(2,1)S(1)}, bf16[512,1024]{1,0:T(8,128)(2,1)S(1)}, u32[]{:S(2)}, u32[]{:S(2)}) %collective-permute-start.41) | collective-permute-done | bytes 1048608 | tf_op jit(solution)/shard_map/ppermute | solution.py:290
  904.8 5.9 collective-permute-done.47
  923.8 14.3 %collective-permute-done.58 = bf16[128,1024]{1,0:T(8,128)(2,1)S(1)} collective-permute-done((bf16[128,1024]{1,0:T(8,128)(2,1)S(1)}, bf16[128,1024]{1,0:T(8,128)(2,1)S(1)}, u32[]{:S(2)}, u32[]{:S(2)}) %collective-permute-start.58) | collective-permute-done | bytes 262176 | tf_op jit(solution)/shard_map/ppermute | solution.py:341
  941.4 40.9 %all-reduce = (f32[1024]{0:T(1024)}, f32[1024]{0:T(1024)}) all-reduce(f32[1024]{0:T(1024)} %get-tuple-element.35, f32[1024]{0:T(1024)} %get-tuple-element.33), channel_id=1, replica_groups=mesh['dp'=4,'row'=2,'col'=4] {'dp','col'}, use_global_device_ids=true, to_apply=%region_5.6 | all-reduce | flops 2048 | bytes 16384 | tf_op jit(solution)/shard_map/psum | solution.py:488
  984.2 5.5 fusion.7
  (437 shorter events, 282.5 us)
Async XLA Ops:
  0.7 43.8 %collective-permute-start = (bf16[512,1024]{1,0:T(8,128)(2,1)}, bf16[512,1024]{1,0:T(8,128)(2,1)S(1)}, u32[]{:S(2)}, u32[]{:S(2)}) collective-permute-start(bf16[512,1024]{1,0:T(8,128)(2,1)} %param.11), channel_id=1, source_target_pairs={{0,2},{2,3},{3,1},{1,0},{4,6},{6,7},{7,5},{5,4},{8,10},{10,11},{11... | collective-permute-start | bytes 3145736 | tf_op jit(solution)/shard_map/ppermute | solution.py:290
  70.7 30.5 %collective-permute-start.2 = (bf16[512,1024]{1,0:T(8,128)(2,1)}, bf16[512,1024]{1,0:T(8,128)(2,1)}, u32[]{:S(2)}, u32[]{:S(2)}) collective-permute-start(bf16[512,1024]{1,0:T(8,128)(2,1)} %collective-permute-done.1), channel_id=1, source_target_pairs={{0,2},{2,3},{3,1},{1,0},{4,6},{6,7},{7,5},{5,4},{8,10},{10,11},{11... | collective-permute-start | bytes 3145736 | tf_op jit(solution)/shard_map/ppermute | solution.py:290
  77.1 44.7 %collective-permute-start.13 = (bf16[4,256,1024]{2,1,0:T(8,128)(2,1)}, bf16[4,256,1024]{2,1,0:T(8,128)(2,1)}, u32[]{:S(2)}, u32[]{:S(2)}) collective-permute-start(bf16[4,256,1024]{2,1,0:T(8,128)(2,1)} %pad_maximum_fusion.1), channel_id=1, source_target_pairs={{0,16},{8,24},{16,0},{24,8},{1,17},{9,25},{17,1},{25,9},{2,18},{10... | collective-permute-start | bytes 6291464 | tf_op jit(solution)/shard_map/ppermute | solution.py:379
  78.7 60.5 %collective-permute-start.5 = (bf16[1024,1536]{1,0:T(8,128)(2,1)}, bf16[1024,1536]{1,0:T(8,128)(2,1)}, u32[]{:S(2)}, u32[]{:S(2)}) collective-permute-start(bf16[1024,1536]{1,0:T(8,128)(2,1)} %wo.1), channel_id=1, source_target_pairs={{0,4},{4,0},{1,5},{5,1},{2,6},{6,2},{3,7},{7,3},{8,12},{12,8},{9,1... | collective-permute-start | bytes 9437192 | tf_op jit(solution)/shard_map/ppermute | solution.py:273
  78.7 37.9 %collective-permute-start.16 = (bf16[512,1024]{1,0:T(8,128)(2,1)S(1)}, bf16[512,1024]{1,0:T(8,128)(2,1)}, u32[]{:S(2)}, u32[]{:S(2)}) collective-permute-start(bf16[512,1024]{1,0:T(8,128)(2,1)S(1)} %copy-done.9), channel_id=1, source_target_pairs={{0,2},{2,3},{3,1},{1,0},{4,6},{6,7},{7,5},{5,4},{8,10},{10,11},{11... | collective-permute-start | bytes 3145736 | tf_op jit(solution)/shard_map/ppermute | solution.py:290
  105.0 34.7 %collective-permute-start.3 = (bf16[1024,1024]{1,0:T(8,128)(2,1)}, bf16[1024,1024]{1,0:T(8,128)(2,1)}, u32[]{:S(2)}, u32[]{:S(2)}) collective-permute-start(bf16[1024,1024]{1,0:T(8,128)(2,1)} %get-tuple-element.57), channel_id=1, source_target_pairs={{0,4},{4,0},{1,5},{5,1},{2,6},{6,2},{3,7},{7,3},{8,12},{12,8},{9,1... | collective-permute-start | bytes 6291464 | tf_op jit(solution)/shard_map/ppermute | solution.py:273
  125.2 99.9 %collective-permute-start.14 = (bf16[4,512,1024]{2,1,0:T(8,128)(2,1)S(1)}, bf16[4,512,1024]{2,1,0:T(8,128)(2,1)}, u32[]{:S(2)}, u32[]{:S(2)}) collective-permute-start(bf16[4,512,1024]{2,1,0:T(8,128)(2,1)S(1)} %pad_maximum_fusion.refs_4_), channel_id=1, source_target_pairs={{0,4},{4,0},{1,5},{5,1},{2,6},{6,2},{3,7},{7,3},{8,12},{12,8},{9,1... | collective-permute-start | bytes 12582920 | tf_op jit(solution)/shard_map/ppermute | solution.py:273
  127.6 141.0 %collective-permute-start.20 = (bf16[1024,2048]{1,0:T(8,128)(2,1)}, bf16[1024,2048]{1,0:T(8,128)(2,1)}, u32[]{:S(2)}, u32[]{:S(2)}) collective-permute-start(bf16[1024,2048]{1,0:T(8,128)(2,1)} %gwo.1), channel_id=1, source_target_pairs={{0,4},{4,0},{1,5},{5,1},{2,6},{6,2},{3,7},{7,3},{8,12},{12,8},{9,1... | collective-permute-start | bytes 12582920 | tf_op jit(solution)/shard_map/ppermute | solution.py:273
  139.1 129.4 %collective-permute-start.21 = (bf16[1024,2048]{1,0:T(8,128)(2,1)}, bf16[1024,2048]{1,0:T(8,128)(2,1)}, u32[]{:S(2)}, u32[]{:S(2)}) collective-permute-start(bf16[1024,2048]{1,0:T(8,128)(2,1)} %uwo.1), channel_id=1, source_target_pairs={{0,4},{4,0},{1,5},{5,1},{2,6},{6,2},{3,7},{7,3},{8,12},{12,8},{9,1... | collective-permute-start | bytes 12582920 | tf_op jit(solution)/shard_map/ppermute | solution.py:273
  139.2 37.0 %collective-permute-start.33 = (f32[512,1]{0,1:T(1,128)S(1)}, f32[512,1]{0,1:T(1,128)S(1)}, u32[]{:S(2)}, u32[]{:S(2)}) collective-permute-start(f32[512,1]{0,1:T(1,128)S(1)} %bitcast.89), channel_id=1, source_target_pairs={{0,4},{4,0},{1,5},{5,1},{2,6},{6,2},{3,7},{7,3},{8,12},{12,8},{9,1... | collective-permute-start | bytes 6152 | tf_op jit(solution)/shard_map/ppermute | solution.py:273
  139.7 36.5 %collective-permute-start.18 = (bf16[512,1024]{1,0:T(8,128)(2,1)}, bf16[512,1024]{1,0:T(8,128)(2,1)S(1)}, u32[]{:S(2)}, u32[]{:S(2)}) collective-permute-start(bf16[512,1024]{1,0:T(8,128)(2,1)} %collective-permute-done.17), channel_id=1, source_target_pairs={{0,2},{2,3},{3,1},{1,0},{4,6},{6,7},{7,5},{5,4},{8,10},{10,11},{11... | collective-permute-start | bytes 3145736 | tf_op jit(solution)/shard_map/ppermute | solution.py:290
  176.2 92.4 %collective-permute-start.22 = (bf16[2048,1024]{1,0:T(8,128)(2,1)}, bf16[2048,1024]{1,0:T(8,128)(2,1)}, u32[]{:S(2)}, u32[]{:S(2)}) collective-permute-start(bf16[2048,1024]{1,0:T(8,128)(2,1)} %dwo.1), channel_id=1, source_target_pairs={{0,4},{4,0},{1,5},{5,1},{2,6},{6,2},{3,7},{7,3},{8,12},{12,8},{9,1... | collective-permute-start | bytes 12582920 | tf_op jit(solution)/shard_map/ppermute | solution.py:273
  225.1 43.5 %collective-permute-start.19 = (bf16[1024,1024]{1,0:T(8,128)(2,1)S(1)}, bf16[1024,1024]{1,0:T(8,128)(2,1)}, u32[]{:S(2)}, u32[]{:S(2)}) collective-permute-start(bf16[1024,1024]{1,0:T(8,128)(2,1)S(1)} %get-tuple-element.53), channel_id=1, source_target_pairs={{0,4},{4,0},{1,5},{5,1},{2,6},{6,2},{3,7},{7,3},{8,12},{12,8},{9,1... | collective-permute-start | bytes 6291464 | tf_op jit(solution)/shard_map/ppermute | solution.py:273
  330.1 37.9 %collective-permute-start.28 = (bf16[1024,1024]{1,0:T(8,128)(2,1)S(1)}, bf16[1024,1024]{1,0:T(8,128)(2,1)S(1)}, u32[]{:S(2)}, u32[]{:S(2)}) collective-permute-start(bf16[1024,1024]{1,0:T(8,128)(2,1)S(1)} %add_convert_fusion), channel_id=1, source_target_pairs={{0,4},{4,0},{1,5},{5,1},{2,6},{6,2},{3,7},{7,3},{8,12},{12,8},{9,1... | collective-permute-start | bytes 6291464 | tf_op jit(solution)/shard_map/ppermute | solution.py:273
  359.9 73.8 %collective-permute-start.15 = (f32[512,1024]{1,0:T(8,128)S(1)}, f32[512,1024]{1,0:T(8,128)S(1)}, u32[]{:S(2)}, u32[]{:S(2)}) collective-permute-start(f32[512,1024]{1,0:T(8,128)S(1)} %constant_dynamic-slice_fusion.1), channel_id=1, source_target_pairs={{0,4},{4,0},{1,5},{5,1},{2,6},{6,2},{3,7},{7,3},{8,12},{12,8},{9,1... | collective-permute-start | bytes 6291464 | tf_op jit(solution)/shard_map/ppermute | solution.py:273
  360.0 89.5 %collective-permute-start.66 = (bf16[1024,2048]{1,0:T(8,128)(2,1)}, bf16[1024,2048]{1,0:T(8,128)(2,1)}, u32[]{:S(2)}, u32[]{:S(2)}) collective-permute-start(bf16[1024,2048]{1,0:T(8,128)(2,1)} %convolution_convert_fusion.6), channel_id=1, source_target_pairs={{0,4},{4,0},{1,5},{5,1},{2,6},{6,2},{3,7},{7,3},{8,12},{12,8},{9,1... | collective-permute-start | bytes 12582920 | tf_op jit(solution)/shard_map/ppermute | solution.py:273
  360.5 114.6 %collective-permute-start.75 = (bf16[1024,2048]{1,0:T(8,128)(2,1)}, bf16[1024,2048]{1,0:T(8,128)(2,1)S(1)}, u32[]{:S(2)}, u32[]{:S(2)}) collective-permute-start(bf16[1024,2048]{1,0:T(8,128)(2,1)} %convolution_convert_fusion.4), channel_id=1, source_target_pairs={{0,4},{4,0},{1,5},{5,1},{2,6},{6,2},{3,7},{7,3},{8,12},{12,8},{9,1... | collective-permute-start | bytes 12582920 | tf_op jit(solution)/shard_map/ppermute | solution.py:273
  381.3 95.7 %collective-permute-start.84 = (bf16[2048,1024]{1,0:T(8,128)(2,1)}, bf16[2048,1024]{1,0:T(8,128)(2,1)S(1)}, u32[]{:S(2)}, u32[]{:S(2)}) collective-permute-start(bf16[2048,1024]{1,0:T(8,128)(2,1)} %convolution_convert_fusion.2), channel_id=1, source_target_pairs={{0,4},{4,0},{1,5},{5,1},{2,6},{6,2},{3,7},{7,3},{8,12},{12,8},{9,1... | collective-permute-start | bytes 12582920 | tf_op jit(solution)/shard_map/ppermute | solution.py:273
  433.7 36.2 %collective-permute-start.25 = (bf16[512,1024]{1,0:T(8,128)(2,1)S(1)}, bf16[512,1024]{1,0:T(8,128)(2,1)S(1)}, u32[]{:S(2)}, u32[]{:S(2)}) collective-permute-start(bf16[512,1024]{1,0:T(8,128)(2,1)S(1)} %add_convert_fusion.14), channel_id=1, source_target_pairs={{0,2},{2,3},{3,1},{1,0},{4,6},{6,7},{7,5},{5,4},{8,10},{10,11},{11... | collective-permute-start | bytes 3145736 | tf_op jit(solution)/shard_map/ppermute | solution.py:290
  449.5 42.9 %collective-permute-start.31 = (bf16[512,1024]{1,0:T(8,128)(2,1)S(1)}, bf16[512,1024]{1,0:T(8,128)(2,1)S(1)}, u32[]{:S(2)}, u32[]{:S(2)}) collective-permute-start(bf16[512,1024]{1,0:T(8,128)(2,1)S(1)} %add_convert_fusion.10), channel_id=1, source_target_pairs={{0,2},{2,3},{3,1},{1,0},{4,6},{6,7},{7,5},{5,4},{8,10},{10,11},{11... | collective-permute-start | bytes 3145736 | tf_op jit(solution)/shard_map/ppermute | solution.py:290
  454.7 39.2 %collective-permute-start.67 = (bf16[256,2048]{1,0:T(8,128)(2,1)S(1)}, bf16[256,2048]{1,0:T(8,128)(2,1)S(1)}, u32[]{:S(2)}, u32[]{:S(2)}) collective-permute-start(bf16[256,2048]{1,0:T(8,128)(2,1)S(1)} %add_convert_fusion.7), channel_id=1, source_target_pairs={{0,8},{8,0},{16,24},{24,16},{1,9},{9,1},{17,25},{25,17},{2,10},{10... | collective-permute-start | bytes 3145736 | tf_op jit(solution)/shard_map/ppermute | solution.py:341
  471.5 512.7 %collective-permute-start.26 = (bf16[512,1024]{1,0:T(8,128)(2,1)}, bf16[512,1024]{1,0:T(8,128)(2,1)}, u32[]{:S(2)}, u32[]{:S(2)}) collective-permute-start(bf16[512,1024]{1,0:T(8,128)(2,1)} %add_convert_fusion.13), channel_id=1, source_target_pairs={{0,2},{2,3},{3,1},{1,0},{4,6},{6,7},{7,5},{5,4},{8,10},{10,11},{11... | collective-permute-start | bytes 3145736 | tf_op jit(solution)/shard_map/ppermute | solution.py:290
  477.4 47.4 %collective-permute-start.85 = (bf16[512,1024]{1,0:T(8,128)(2,1)S(1)}, bf16[512,1024]{1,0:T(8,128)(2,1)S(1)}, u32[]{:S(2)}, u32[]{:S(2)}) collective-permute-start(bf16[512,1024]{1,0:T(8,128)(2,1)S(1)} %add_convert_fusion.3), channel_id=1, source_target_pairs={{0,8},{8,0},{16,24},{24,16},{1,9},{9,1},{17,25},{25,17},{2,10},{10... | collective-permute-start | bytes 3145736 | tf_op jit(solution)/shard_map/ppermute | solution.py:341
  493.9 33.7 %collective-permute-start.32 = (f32[512,1]{0,1:T(1,128)S(1)}, f32[512,1]{0,1:T(1,128)S(1)}, u32[]{:S(2)}, u32[]{:S(2)}) collective-permute-start(f32[512,1]{0,1:T(1,128)S(1)} %bitcast.91), channel_id=1, source_target_pairs={{0,4},{4,0},{1,5},{5,1},{2,6},{6,2},{3,7},{7,3},{8,12},{12,8},{9,1... | collective-permute-start | bytes 6152 | tf_op jit(solution)/shard_map/ppermute | solution.py:273
  496.7 69.0 %collective-permute-start.71 = (bf16[256,2048]{1,0:T(8,128)(2,1)S(1)}, bf16[256,2048]{1,0:T(8,128)(2,1)S(1)}, u32[]{:S(2)}, u32[]{:S(2)}) collective-permute-start(bf16[256,2048]{1,0:T(8,128)(2,1)S(1)} %get-tuple-element.50), channel_id=1, source_target_pairs={{0,16},{8,24},{16,0},{24,8},{1,17},{9,25},{17,1},{25,9},{2,18},{10... | collective-permute-start | bytes 3145736 | tf_op jit(solution)/shard_map/ppermute | solution.py:342
  503.2 30.7 %collective-permute-start.68 = (bf16[128,2048]{1,0:T(8,128)(2,1)S(1)}, bf16[128,2048]{1,0:T(8,128)(2,1)S(1)}, u32[]{:S(2)}, u32[]{:S(2)}) collective-permute-start(bf16[128,2048]{1,0:T(8,128)(2,1)S(1)} %dynamic-slice_convert_fusion.5), channel_id=1, source_target_pairs={{0,16},{8,24},{16,0},{24,8},{1,17},{9,25},{17,1},{25,9},{2,18},{10... | collective-permute-start | bytes 1572872 | tf_op jit(solution)/shard_map/ppermute | solution.py:342
  559.9 71.2 %collective-permute-start.80 = (bf16[256,2048]{1,0:T(8,128)(2,1)S(1)}, bf16[256,2048]{1,0:T(8,128)(2,1)S(1)}, u32[]{:S(2)}, u32[]{:S(2)}) collective-permute-start(bf16[256,2048]{1,0:T(8,128)(2,1)S(1)} %get-tuple-element.48), channel_id=1, source_target_pairs={{0,16},{8,24},{16,0},{24,8},{1,17},{9,25},{17,1},{25,9},{2,18},{10... | collective-permute-start | bytes 3145736 | tf_op jit(solution)/shard_map/ppermute | solution.py:342
  560.8 71.0 %collective-permute-start.89 = (bf16[512,1024]{1,0:T(8,128)(2,1)S(1)}, bf16[512,1024]{1,0:T(8,128)(2,1)S(1)}, u32[]{:S(2)}, u32[]{:S(2)}) collective-permute-start(bf16[512,1024]{1,0:T(8,128)(2,1)S(1)} %get-tuple-element.46), channel_id=1, source_target_pairs={{0,16},{8,24},{16,0},{24,8},{1,17},{9,25},{17,1},{25,9},{2,18},{10... | collective-permute-start | bytes 3145736 | tf_op jit(solution)/shard_map/ppermute | solution.py:342
  564.8 64.7 %collective-permute-start.69 = (bf16[128,2048]{1,0:T(8,128)(2,1)S(1)}, bf16[128,2048]{1,0:T(8,128)(2,1)S(1)}, u32[]{:S(2)}, u32[]{:S(2)}) collective-permute-start(bf16[128,2048]{1,0:T(8,128)(2,1)S(1)} %add_convert_fusion.22), channel_id=1, source_target_pairs={{0,16},{8,24},{16,0},{24,8},{1,17},{9,25},{17,1},{25,9},{2,18},{10... | collective-permute-start | bytes 1572872 | tf_op jit(solution)/shard_map/ppermute | solution.py:342
  565.7 62.6 %collective-permute-start.87 = (bf16[256,1024]{1,0:T(8,128)(2,1)S(1)}, bf16[256,1024]{1,0:T(8,128)(2,1)S(1)}, u32[]{:S(2)}, u32[]{:S(2)}) collective-permute-start(bf16[256,1024]{1,0:T(8,128)(2,1)S(1)} %add_convert_fusion.18), channel_id=1, source_target_pairs={{0,16},{8,24},{16,0},{24,8},{1,17},{9,25},{17,1},{25,9},{2,18},{10... | collective-permute-start | bytes 1572872 | tf_op jit(solution)/shard_map/ppermute | solution.py:342
  631.7 63.8 %collective-permute-start.72 = (bf16[128,2048]{1,0:T(8,128)(2,1)}, bf16[128,2048]{1,0:T(8,128)(2,1)}, u32[]{:S(2)}, u32[]{:S(2)}) collective-permute-start(bf16[128,2048]{1,0:T(8,128)(2,1)} %dynamic-slice_convert_fusion.4), channel_id=1, source_target_pairs={{0,8},{8,0},{16,24},{24,16},{1,9},{9,1},{17,25},{25,17},{2,10},{10... | collective-permute-start | bytes 1572872 | tf_op jit(solution)/shard_map/ppermute | solution.py:341
  641.2 94.0 %collective-permute-start.70 = (bf16[256,2048]{1,0:T(8,128)(2,1)}, bf16[256,2048]{1,0:T(8,128)(2,1)}, u32[]{:S(2)}, u32[]{:S(2)}) collective-permute-start(bf16[256,2048]{1,0:T(8,128)(2,1)} %pad_maximum_fusion.4), channel_id=1, source_target_pairs={{0,8},{8,0},{16,24},{24,16},{1,9},{9,1},{17,25},{25,17},{2,10},{10... | collective-permute-start | bytes 3145736 | tf_op jit(solution)/shard_map/ppermute | solution.py:341
  650.7 49.7 %collective-permute-start.81 = (bf16[128,2048]{1,0:T(8,128)(2,1)}, bf16[128,2048]{1,0:T(8,128)(2,1)}, u32[]{:S(2)}, u32[]{:S(2)}) collective-permute-start(bf16[128,2048]{1,0:T(8,128)(2,1)} %dynamic-slice_convert_fusion.2), channel_id=1, source_target_pairs={{0,8},{8,0},{16,24},{24,16},{1,9},{9,1},{17,25},{25,17},{2,10},{10... | collective-permute-start | bytes 1572872 | tf_op jit(solution)/shard_map/ppermute | solution.py:341
  652.4 46.0 %collective-permute-start.90 = (bf16[256,1024]{1,0:T(8,128)(2,1)}, bf16[256,1024]{1,0:T(8,128)(2,1)}, u32[]{:S(2)}, u32[]{:S(2)}) collective-permute-start(bf16[256,1024]{1,0:T(8,128)(2,1)} %dynamic-slice_convert_fusion), channel_id=1, source_target_pairs={{0,8},{8,0},{16,24},{24,16},{1,9},{9,1},{17,25},{25,17},{2,10},{10... | collective-permute-start | bytes 1572872 | tf_op jit(solution)/shard_map/ppermute | solution.py:341
  695.6 81.1 %collective-permute-start.79 = (bf16[256,2048]{1,0:T(8,128)(2,1)S(1)}, bf16[256,2048]{1,0:T(8,128)(2,1)S(1)}, u32[]{:S(2)}, u32[]{:S(2)}) collective-permute-start(bf16[256,2048]{1,0:T(8,128)(2,1)S(1)} %copy-done.45), channel_id=1, source_target_pairs={{0,8},{8,0},{16,24},{24,16},{1,9},{9,1},{17,25},{25,17},{2,10},{10... | collective-permute-start | bytes 3145736 | tf_op jit(solution)/shard_map/ppermute | solution.py:341
  698.4 34.6 %collective-permute-start.73 = (bf16[128,2048]{1,0:T(8,128)(2,1)S(1)}, bf16[128,2048]{1,0:T(8,128)(2,1)S(1)}, u32[]{:S(2)}, u32[]{:S(2)}) collective-permute-start(bf16[128,2048]{1,0:T(8,128)(2,1)S(1)} %add_convert_fusion.21), channel_id=1, source_target_pairs={{0,8},{8,0},{16,24},{24,16},{1,9},{9,1},{17,25},{25,17},{2,10},{10... | collective-permute-start | bytes 1572872 | tf_op jit(solution)/shard_map/ppermute | solution.py:341
  700.5 75.6 %collective-permute-start.88 = (bf16[512,1024]{1,0:T(8,128)(2,1)S(1)}, bf16[512,1024]{1,0:T(8,128)(2,1)S(1)}, u32[]{:S(2)}, u32[]{:S(2)}) collective-permute-start(bf16[512,1024]{1,0:T(8,128)(2,1)S(1)} %copy-done.46), channel_id=1, source_target_pairs={{0,8},{8,0},{16,24},{24,16},{1,9},{9,1},{17,25},{25,17},{2,10},{10... | collective-permute-start | bytes 3145736 | tf_op jit(solution)/shard_map/ppermute | solution.py:341
  733.0 44.8 %collective-permute-start.54 = (bf16[512,1024]{1,0:T(8,128)(2,1)S(1)}, bf16[512,1024]{1,0:T(8,128)(2,1)S(1)}, u32[]{:S(2)}, u32[]{:S(2)}) collective-permute-start(bf16[512,1024]{1,0:T(8,128)(2,1)S(1)} %copy-done.42), channel_id=1, source_target_pairs={{0,2},{2,3},{3,1},{1,0},{4,6},{6,7},{7,5},{5,4},{8,10},{10,11},{11... | collective-permute-start | bytes 3145736 | tf_op jit(solution)/shard_map/ppermute | solution.py:290
  776.1 67.7 %collective-permute-start.39 = (bf16[1024,1024]{1,0:T(8,128)(2,1)}, bf16[1024,1024]{1,0:T(8,128)(2,1)S(1)}, u32[]{:S(2)}, u32[]{:S(2)}) collective-permute-start(bf16[1024,1024]{1,0:T(8,128)(2,1)} %convolution_convert_fusion.8), channel_id=1, source_target_pairs={{0,4},{4,0},{1,5},{5,1},{2,6},{6,2},{3,7},{7,3},{8,12},{12,8},{9,1... | collective-permute-start | bytes 6291464 | tf_op jit(solution)/shard_map/ppermute | solution.py:273
  776.7 69.3 %collective-permute-start.44 = (bf16[1024,1536]{1,0:T(8,128)(2,1)S(1)}, bf16[1024,1536]{1,0:T(8,128)(2,1)S(1)}, u32[]{:S(2)}, u32[]{:S(2)}) collective-permute-start(bf16[1024,1536]{1,0:T(8,128)(2,1)S(1)} %convolution_convert_fusion), channel_id=1, source_target_pairs={{0,4},{4,0},{1,5},{5,1},{2,6},{6,2},{3,7},{7,3},{8,12},{12,8},{9,1... | collective-permute-start | bytes 9437192 | tf_op jit(solution)/shard_map/ppermute | solution.py:273
  777.8 44.5 %collective-permute-start.92 = (bf16[512,1024]{1,0:T(8,128)(2,1)S(1)}, bf16[512,1024]{1,0:T(8,128)(2,1)S(1)}, u32[]{:S(2)}, u32[]{:S(2)}) collective-permute-start(bf16[512,1024]{1,0:T(8,128)(2,1)S(1)} %pad_maximum_fusion.9), channel_id=1, source_target_pairs={{0,16},{8,24},{16,0},{24,8},{1,17},{9,25},{17,1},{25,9},{2,18},{10... | collective-permute-start | bytes 3145736 | tf_op jit(solution)/shard_map/ppermute | solution.py:342
  799.9 39.1 %collective-permute-start.83 = (bf16[256,2048]{1,0:T(8,128)(2,1)S(1)}, bf16[256,2048]{1,0:T(8,128)(2,1)S(1)}, u32[]{:S(2)}, u32[]{:S(2)}) collective-permute-start(bf16[256,2048]{1,0:T(8,128)(2,1)S(1)} %pad_maximum_fusion.7), channel_id=1, source_target_pairs={{0,16},{8,24},{16,0},{24,8},{1,17},{9,25},{17,1},{25,9},{2,18},{10... | collective-permute-start | bytes 3145736 | tf_op jit(solution)/shard_map/ppermute | solution.py:342
  843.7 32.2 %collective-permute-start.56 = (bf16[1024,1024]{1,0:T(8,128)(2,1)S(1)}, bf16[1024,1024]{1,0:T(8,128)(2,1)S(1)}, u32[]{:S(2)}, u32[]{:S(2)}) collective-permute-start(bf16[1024,1024]{1,0:T(8,128)(2,1)S(1)} %slice.69), channel_id=1, source_target_pairs={{0,4},{4,0},{1,5},{5,1},{2,6},{6,2},{3,7},{7,3},{8,12},{12,8},{9,1... | collective-permute-start | bytes 6291464 | tf_op jit(solution)/shard_map/ppermute | solution.py:273
  877.2 36.1 %collective-permute-start.57 = (bf16[512,1024]{1,0:T(8,128)(2,1)S(1)}, bf16[512,1024]{1,0:T(8,128)(2,1)S(1)}, u32[]{:S(2)}, u32[]{:S(2)}) collective-permute-start(bf16[512,1024]{1,0:T(8,128)(2,1)S(1)} %convolution_convert_fusion.12), channel_id=1, source_target_pairs={{0,4},{4,0},{1,5},{5,1},{2,6},{6,2},{3,7},{7,3},{8,12},{12,8},{9,1... | collective-permute-start | bytes 3145736 | tf_op jit(solution)/shard_map/ppermute | solution.py:273
  911.8 91.5 %collective-permute-start.48 = (bf16[256,1536]{1,0:T(8,128)(2,1)}, bf16[256,1536]{1,0:T(8,128)(2,1)}, u32[]{:S(2)}, u32[]{:S(2)}) collective-permute-start(bf16[256,1536]{1,0:T(8,128)(2,1)} %pad_maximum_fusion.10), channel_id=1, source_target_pairs={{0,8},{8,0},{16,24},{24,16},{1,9},{9,1},{17,25},{25,17},{2,10},{10... | collective-permute-start | bytes 2359304 | tf_op jit(solution)/shard_map/ppermute | solution.py:341
  914.8 77.2 %collective-permute-start.51 = (bf16[128,1536]{1,0:T(8,128)(2,1)}, bf16[128,1536]{1,0:T(8,128)(2,1)}, u32[]{:S(2)}, u32[]{:S(2)}) collective-permute-start(bf16[128,1536]{1,0:T(8,128)(2,1)} %add_convert_fusion.23), channel_id=1, source_target_pairs={{0,8},{8,0},{16,24},{24,16},{1,9},{9,1},{17,25},{25,17},{2,10},{10... | collective-permute-start | bytes 1179656 | tf_op jit(solution)/shard_map/ppermute | solution.py:341
  923.8 58.6 %collective-permute-start.43 = (f32[512,1]{0,1:T(1,128)}, f32[512,1]{0,1:T(1,128)}, u32[]{:S(2)}, u32[]{:S(2)}) collective-permute-start(f32[512,1]{0,1:T(1,128)} %bitcast.26), channel_id=1, source_target_pairs={{0,4},{4,0},{1,5},{5,1},{2,6},{6,2},{3,7},{7,3},{8,12},{12,8},{9,1... | collective-permute-start | bytes 6152 | tf_op jit(solution)/shard_map/ppermute | solution.py:273
  939.0 51.7 %collective-permute-start.62 = (bf16[128,1024]{1,0:T(8,128)(2,1)}, bf16[128,1024]{1,0:T(8,128)(2,1)}, u32[]{:S(2)}, u32[]{:S(2)}) collective-permute-start(bf16[128,1024]{1,0:T(8,128)(2,1)} %get-tuple-element.72), channel_id=1, source_target_pairs={{0,16},{8,24},{16,0},{24,8},{1,17},{9,25},{17,1},{25,9},{2,18},{10... | collective-permute-start | bytes 786440 | tf_op jit(solution)/shard_map/ppermute | solution.py:342
  (116 other events, 1960.3 us)

commit v2 on v1

v2 whole, which is shorter than its diff:
```python
import functools

import jax
import jax.numpy as jnp
from jax import lax
from jax.experimental import pallas as pl
from jax.experimental.pallas import tpu as pltpu
from jax.sharding import PartitionSpec as P

HD = 64
LEN = 1024
PAIR = 6 * HD
BLOCK = 256

norm_epsilon = 1e-05
rope_base = 130000.0
masked_score = -1e30
LOG2E = 1.4426950408889634
BF = jnp.bfloat16
F32 = jnp.float32
MIB = 1024 * 1024
SCALE = 0.5 * 1.15e9


def cost(us):
    return pl.CostEstimate(flops=int(us * SCALE), bytes_accessed=1, transcendentals=0)


def nn(left, right):
    return lax.dot_general(left, right, (((1,), (0,)), ((), ())), preferred_element_type=F32)


def nt(left, right):
    return lax.dot_general(left, right, (((1,), (1,)), ((), ())), preferred_element_type=F32)


def tn(left, right):
    return lax.dot_general(left, right, (((0,), (0,)), ((), ())), preferred_element_type=F32)


def params(mib):
    return pltpu.CompilerParams(vmem_limit_bytes=mib * MIB)


def rope_tables():
    steps_half = jnp.arange(HD // 2).astype(F32)
    frequency = rope_base ** (-2.0 * steps_half / HD)
    angles = jnp.arange(LEN).astype(F32)[:, None] * frequency[None, :]
    cos, sin = jnp.cos(angles), jnp.sin(angles)
    return (
        jnp.concatenate([cos] * 4, axis=1),
        jnp.concatenate([-sin, sin] * 2, axis=1),
    )


def project_kernel(xo, xt, go, gt, wo, wt, cos, sin, no, nt_, out, scales):
    @pl.when(pl.program_id(0) == 0)
    def _():
        rows = 256
        for i in range(LEN // rows):
            at = slice(i * rows, (i + 1) * rows)
            a = xo[at, :].astype(F32)
            b = xt[at, :].astype(F32)
            total = jnp.sum(a * a, axis=1, keepdims=True) + jnp.sum(b * b, axis=1, keepdims=True)
            scale = lax.rsqrt(total / (a.shape[1] + b.shape[1]) + norm_epsilon)
            no[at, :] = (a * scale * go[...]).astype(BF)
            nt_[at, :] = (b * scale * gt[...]).astype(BF)
            scales[at, :] = jnp.broadcast_to(scale, (rows, 128))

    proj = nn(no[...], wo[...]) + nn(nt_[...], wt[...])
    lane = lax.broadcasted_iota(jnp.int32, (LEN, 128), 1)
    low = (lane % HD) < HD // 2
    for piece in range(3):
        part = proj[:, piece * 128 : (piece + 1) * 128]
        swapped = jnp.where(low, pltpu.roll(part, 96, 1), pltpu.roll(part, 32, 1))
        turned = part * cos[...] + swapped * sin[...]
        if piece == 1:
            turned = jnp.where(lane < HD, part, turned)
        if piece == 2:
            turned = jnp.where(lane < HD, turned, part)
        out[:, piece * 128 : (piece + 1) * 128] = turned.astype(BF)


def project(xo, xt, go, gt, wo, wt, cos, sin):
    half, columns = wo.shape
    fixed = lambda shape: pl.BlockSpec(shape, lambda i: (0, 0))
    weight = pl.BlockSpec((half, PAIR), lambda i: (0, i))
    return pl.pallas_call(
        project_kernel,
        grid=(columns // PAIR,),
        in_specs=[fixed((LEN, half))] * 2
        + [fixed((1, half))] * 2
        + [weight] * 2
        + [fixed((LEN, 128))] * 2,
        out_specs=[fixed((LEN, half))] * 2
        + [pl.BlockSpec((LEN, PAIR), lambda i: (0, i)), fixed((LEN, 128))],
        out_shape=[jax.ShapeDtypeStruct((LEN, half), BF)] * 2
        + [jax.ShapeDtypeStruct((LEN, columns), BF), jax.ShapeDtypeStruct((LEN, 128), F32)],
        compiler_params=params(56),
        cost_estimate=cost(17),
    )(xo, xt, go, gt, wo, wt, cos, sin)


def head_parts(qkv, head):
    at = head * 3 * HD
    return qkv[:, at : at + HD], qkv[:, at + HD : at + 2 * HD], qkv[:, at + 2 * HD : at + 3 * HD]


def attend_kernel(qkv, out, log_total):
    scale = HD**-0.5 * LOG2E
    row = lax.broadcasted_iota(jnp.int32, (BLOCK, BLOCK), 0)
    col = lax.broadcasted_iota(jnp.int32, (BLOCK, BLOCK), 1)
    for head in range(2):
        q, k, v = head_parts(qkv, head)
        for i in range(LEN // BLOCK):
            start, end = i * BLOCK, (i + 1) * BLOCK
            scores = nt(q[start:end], k[:end])
            last = jnp.where(row >= col, scores[:, start:], masked_score)
            scores = jnp.concatenate([scores[:, :start], last], axis=1) if i else last
            peak = jnp.max(scores, axis=1, keepdims=True)
            probs = jnp.exp2((scores - peak) * scale)
            total = jnp.sum(probs, axis=1, keepdims=True)
            mixed = nn(probs.astype(BF), v[:end]) / total
            out[start:end, head * HD : (head + 1) * HD] = mixed.astype(BF)
            log_total[start:end, head * HD : (head + 1) * HD] = jnp.broadcast_to(
                peak * scale + jnp.log2(total), (BLOCK, HD)
            )


def attend(qkv, group, groups):
    pairs = qkv.shape[1] // PAIR // groups
    narrow = pl.BlockSpec((LEN, 2 * HD), lambda i: (0, i))
    return pl.pallas_call(
        attend_kernel,
        grid=(pairs,),
        in_specs=[pl.BlockSpec((LEN, PAIR), lambda i: (0, group * pairs + i))],
        out_specs=[narrow, narrow],
        out_shape=[
            jax.ShapeDtypeStruct((LEN, pairs * 2 * HD), BF),
            jax.ShapeDtypeStruct((LEN, pairs * 2 * HD), F32),
        ],
        compiler_params=params(48),
        cost_estimate=cost(4 * pairs),
    )(qkv)


def attend_back_kernel(qkv, grad, mixed, log_total, cos, sin, out):
    scale = HD**-0.5 * LOG2E
    row = lax.broadcasted_iota(jnp.int32, (BLOCK, BLOCK), 0)
    col = lax.broadcasted_iota(jnp.int32, (BLOCK, BLOCK), 1)
    blocks = LEN // BLOCK
    totals = jnp.transpose(log_total[...])
    product = jnp.transpose(grad[...].astype(F32) * mixed[...].astype(F32))
    cosines, sines = cos[:, :HD], sin[:, :HD]

    def unturn(part, start, end):
        swapped = jnp.concatenate([part[:, HD // 2 :], part[:, : HD // 2]], axis=1)
        return (part * cosines[start:end] - swapped * sines[start:end]).astype(BF)

    for head in range(2):
        q, k, v = head_parts(qkv, head)
        at = head * 3 * HD
        g = grad[:, head * HD : (head + 1) * HD]
        total = totals[head * HD : head * HD + 1]
        center = jnp.sum(product[head * HD : (head + 1) * HD], axis=0, keepdims=True)
        query_grad = [None] * blocks
        for j in range(blocks):
            start, end = j * BLOCK, (j + 1) * BLOCK
            scores = nt(k[start:end], q[start:])
            probs = jnp.exp2(scores * scale - total[:, start:])
            first = jnp.where(col >= row, probs[:, :BLOCK], 0.0)
            probs = jnp.concatenate([first, probs[:, BLOCK:]], axis=1) if end < LEN else first
            out[start:end, at + 2 * HD : at + 3 * HD] = nn(probs.astype(BF), g[start:]).astype(BF)
            prob_grad = nt(v[start:end], g[start:])
            score_grad = (probs * (prob_grad - center[:, start:])).astype(BF)
            key_grad = nn(score_grad, q[start:]) * (HD**-0.5)
            out[start:end, at + HD : at + 2 * HD] = unturn(key_grad, start, end)
            term = tn(k[start:end], score_grad)
            for b in range(j, blocks):
                here = term[:, (b - j) * BLOCK : (b - j + 1) * BLOCK]
                query_grad[b] = here if query_grad[b] is None else query_grad[b] + here
        for b in range(blocks):
            start, end = b * BLOCK, (b + 1) * BLOCK
            out[start:end, at : at + HD] = unturn(
                jnp.transpose(query_grad[b]) * (HD**-0.5), start, end
            )


def attend_back(qkv, grad, mixed, log_total, cos, sin):
    pairs = qkv.shape[1] // PAIR
    wide = pl.BlockSpec((LEN, PAIR), lambda i: (0, i))
    narrow = pl.BlockSpec((LEN, 2 * HD), lambda i: (0, i))
    fixed = pl.BlockSpec((LEN, 128), lambda i: (0, 0))
    return pl.pallas_call(
        attend_back_kernel,
        grid=(pairs,),
        in_specs=[wide, narrow, narrow, narrow, fixed, fixed],
        out_specs=wide,
        out_shape=jax.ShapeDtypeStruct((LEN, pairs * PAIR), BF),
        compiler_params=params(56),
        cost_estimate=cost(5 * pairs),
    )(qkv, grad, mixed, log_total, cos, sin)


def mix_kernel(start, groups, count, last, *refs):
    mixed = refs[:count]
    wo, wt, ao, at = refs[count : count + 4]
    a = ao[...].astype(F32)
    b = at[...].astype(F32)
    for index in range(count):
        left = mixed[index][...]
        depth = left.shape[1]
        step, low = start + index // groups, index % groups * depth
        a = a + nn(left, wo[step, low : low + depth, :])
        b = b + nn(left, wt[step, low : low + depth, :])
    if not last:
        ro, rt = refs[count + 4 :]
    else:
        go, gt, ro, rt, no, nt_ = refs[count + 4 :]
        total = jnp.sum(a * a, axis=1, keepdims=True) + jnp.sum(b * b, axis=1, keepdims=True)
        scale = lax.rsqrt(total / (a.shape[1] + b.shape[1]) + norm_epsilon)
        no[...] = (a * scale * go[...]).astype(BF)
        nt_[...] = (b * scale * gt[...]).astype(BF)
    ro[...] = a
    rt[...] = b


def mix(mixed, wo, wt, ao, at, start, gains=None):
    depth, half = wo.shape[1:]
    count = len(mixed)
    groups = depth // mixed[0].shape[1]
    steps = count // groups
    rows = 256
    if start % steps == 0:
        weight = pl.BlockSpec((steps, depth, half), lambda i: (start // steps, 0, 0))
        offset = 0
    else:
        weight = pl.BlockSpec(wo.shape, lambda i: (0, 0, 0))
        offset = start
    left = pl.BlockSpec((rows, depth // groups), lambda i: (i, 0))
    part = pl.BlockSpec((rows, half), lambda i: (i, 0))
    gain = pl.BlockSpec((1, half), lambda i: (0, 0))
    last = gains is not None
    more = list(gains) if last else []
    return pl.pallas_call(
        functools.partial(mix_kernel, offset, groups, count, last),
        grid=(LEN // rows,),
        in_specs=[left] * count + [weight] * 2 + [part] * 2 + [gain] * len(more),
        out_specs=[part] * (4 if last else 2),
        out_shape=[jax.ShapeDtypeStruct((LEN, half), F32)] * 2
        + [jax.ShapeDtypeStruct((LEN, half), BF)] * (2 if last else 0),
        compiler_params=params(56),
        cost_estimate=cost(3 * count),
    )(*mixed, wo, wt, ao, at, *more)


def feed_kernel(no, nt_, back, gwo, gwt, uwo, uwt, hidden, gate_grad, upper_grad):
    gate = nn(no[...], gwo[...]) + nn(nt_[...], gwt[...])
    upper = nn(no[...], uwo[...]) + nn(nt_[...], uwt[...])
    sigmoid = 1.0 / (1.0 + jnp.exp(-gate))
    silu = gate * sigmoid
    hidden[...] = (silu * upper).astype(BF)
    hidden_grad = back[...]
    gate_grad[...] = (hidden_grad * upper * sigmoid * (1.0 + gate * (1.0 - sigmoid))).astype(BF)
    upper_grad[...] = (hidden_grad * silu).astype(BF)


def feed(no, nt_, back, gwo, gwt, uwo, uwt):
    half, units = gwo.shape
    tokens = pl.BlockSpec((LEN, half), lambda i: (0, 0))
    weight = pl.BlockSpec((half, BLOCK), lambda i: (0, i))
    out = pl.BlockSpec((LEN, BLOCK), lambda i: (0, i))
    return pl.pallas_call(
        feed_kernel,
        grid=(units // BLOCK,),
        in_specs=[tokens] * 2 + [out] + [weight] * 4,
        out_specs=[out] * 3,
        out_shape=[jax.ShapeDtypeStruct((LEN, units), BF)] * 3,
        compiler_params=params(60),
        cost_estimate=cost(26),
    )(no, nt_, back, gwo, gwt, uwo, uwt)


def product_kernel(kind, terms, more, *refs):
    lefts, rights = refs[:terms], refs[terms : 2 * terms]
    out = refs[2 * terms + more]
    if kind == "tn":
        turned = refs[2 * terms + more + 1 :]

        @pl.when(pl.program_id(0) == 0)
        def _():
            for left, kept in zip(lefts, turned):
                kept[...] = left[...].T

        lefts = turned
    dot = nt if kind == "nt" else nn
    total = refs[2 * terms][...].astype(F32) if more else None
    for left, right in zip(lefts, rights):
        term = dot(left[...], right[...])
        total = term if total is None else total + term
    out[...] = total.astype(out.dtype)


def product(kind, lefts, rights, kind_out=BF, extra=None, part=None, tile=512):
    which, parts = part or (0, 1)
    rows = lefts[0].shape[1 if kind == "tn" else 0]
    columns = rights[0].shape[0 if kind == "nt" else 1] // parts
    tile = min(tile, columns)
    first = which * (columns // tile)
    fixed = [pl.BlockSpec(v.shape, lambda i: (0, 0)) for v in lefts]
    if kind == "nt":
        moving = [pl.BlockSpec((tile, v.shape[1]), lambda i: (first + i, 0)) for v in rights]
    else:
        moving = [pl.BlockSpec((v.shape[0], tile), lambda i: (0, first + i)) for v in rights]
    out = pl.BlockSpec((rows, tile), lambda i: (0, i))
    more = [] if extra is None else [extra]
    return pl.pallas_call(
        functools.partial(product_kernel, kind, len(lefts), len(more)),
        grid=(columns // tile,),
        in_specs=fixed + moving + [out] * len(more),
        out_specs=out,
        out_shape=jax.ShapeDtypeStruct((rows, columns), kind_out),
        scratch_shapes=[pltpu.VMEM(v.shape[::-1], BF) for v in lefts] if kind == "tn" else [],
        compiler_params=params(60),
        cost_estimate=cost(1 + len(lefts) * lefts[0].size * columns / 3.4e8),
    )(*lefts, *rights, *more)


def beside_kernel(tiles, more, *refs):
    left, first, second = refs[:3]
    out, turned = refs[3 + more :]
    at = pl.program_id(0)

    @pl.when(at == 0)
    def _():
        turned[...] = left[...].T

    def store(right):
        total = nn(turned[...], right[...])
        if more:
            total = total + refs[3][...].astype(F32)
        out[...] = total.astype(out.dtype)

    @pl.when(at < tiles)
    def _():
        store(first)

    @pl.when(at >= tiles)
    def _():
        store(second)


def product_beside(left, first, second, extra=None, tile=512):
    depth, rows = left.shape
    columns = first.shape[1]
    tile = min(tile, columns)
    tiles = columns // tile
    out = pl.BlockSpec((rows, tile), lambda i: (0, i))
    more = [] if extra is None else [extra]
    return pl.pallas_call(
        functools.partial(beside_kernel, tiles, len(more)),
        grid=(2 * tiles,),
        in_specs=[
            pl.BlockSpec(left.shape, lambda i: (0, 0)),
            pl.BlockSpec((depth, tile), lambda i: (0, jnp.minimum(i, tiles - 1))),
            pl.BlockSpec((depth, tile), lambda i: (0, jnp.maximum(i - tiles, 0))),
        ]
        + [out] * len(more),
        out_specs=out,
        out_shape=jax.ShapeDtypeStruct((rows, 2 * columns), BF),
        scratch_shapes=[pltpu.VMEM((rows, depth), BF)],
        compiler_params=params(60),
        cost_estimate=cost(16),
    )(left, first, second, *more)


def swap_row(values):
    return lax.ppermute(values, "row", [(0, 1), (1, 0)])


class Ring:
    def __init__(self):
        count = lax.axis_size("col")
        self.count = count
        self.order = list(range(0, count, 2)) + list(range(count - 1, 0, -2))
        index = lax.axis_index("col")
        self.here = jnp.where(index % 2 == 0, index // 2, count - 1 - index // 2)
        self.core = lax.axis_index("row")

    def shift(self, values, by=1):
        count, order = self.count, self.order
        pairs = [(order[p], order[(p + by) % count]) for p in range(count)]
        return lax.ppermute(values, "col", pairs)

    def owner(self, back):
        count = self.count
        at = (self.here + (2 * count - back)) % count
        return jnp.where(at < count // 2, 2 * at, 2 * (count - 1 - at) + 1)

    def split(self, owner):
        per = self.count // 2
        return owner // per, owner % per

    def place(self, halves, direction):
        rows, columns = halves[0][0].shape
        whole = rows * len(halves)
        out = jnp.zeros((self.count * whole, columns), halves[0][0].dtype)
        for low, blocks in enumerate(halves):
            for step, block in enumerate(blocks):
                sequence, at = self.split(self.owner(direction * step))
                slot = jnp.where(sequence == self.core, 0, self.count // 2) + at
                out = lax.dynamic_update_slice(out, block, (slot * whole + low * rows, 0))
        return out

    def term(self, own, other, back):
        rows = own.shape[0] * 2 // self.count
        sequence, at = self.split(self.owner(back))
        take = lambda values: lax.dynamic_slice_in_dim(values, at * rows, rows, 0)
        return jnp.where(sequence == self.core, take(own), take(other))


def halve(values, bit, axis):
    size = values.shape[axis] // 2
    return lax.dynamic_slice_in_dim(values, bit * size, size, axis)


def join(values, others, bit, axis):
    first = jnp.where(bit == 0, values, others)
    second = jnp.where(bit == 0, others, values)
    return jnp.concatenate([first, second], axis=axis)


class Square:
    def __init__(self):
        index = lax.axis_index("dp")
        bits = (index % 2, index // 2)
        hops = tuple(
            lambda v, flip=flip: lax.ppermute(v, "dp", [(i, i ^ flip) for i in range(4)])
            for flip in (1, 2)
        )
        self.bits, self.hops = bits, hops
        self.index = index

    def send(self, parts, phase, axis):
        got = []
        for which, addends in enumerate(parts):
            turn = which ^ (phase - 1)
            out = sum(halve(v, 1 - self.bits[turn], axis).astype(F32) for v in addends)
            got.append(self.hops[turn](out.astype(BF)))
        return got

    def add(self, parts, got, phase, axis, kind=F32):
        kept = []
        for which, addends in enumerate(parts):
            turn = which ^ (phase - 1)
            out = sum(halve(v, self.bits[turn], axis).astype(F32) for v in addends)
            kept.append((out + got[which].astype(F32)).astype(kind))
        return kept

    def hop(self, parts, phase):
        return [self.hops[which ^ (phase - 1)](v) for which, v in enumerate(parts)]

    def join(self, parts, got, phase, axis):
        return [
            join(v, got[which], self.bits[which ^ (phase - 1)], axis)
            for which, v in enumerate(parts)
        ]


def row_total(values):
    return values + swap_row(values)


def shards(
    block_input,
    attn_gain,
    attn_weight,
    out_weight,
    feed_gain,
    gate_weight,
    up_weight,
    down_weight,
    out_cotangent,
):
    ring = Ring()
    square = Square()
    count, core = ring.count, ring.core
    rows, half = block_input.shape
    size = rows // 2
    width = 2 * half
    own_sequence, own_at = ring.split(lax.axis_index("col"))
    local = own_sequence == core

    steps = count - 1
    s = dict(
        x=block_input,
        cot=out_cotangent,
        aw=attn_weight,
        gw=gate_weight,
        uw=up_weight,
        dw=down_weight,
        gains=jnp.concatenate([attn_gain[None, :], feed_gain[None, :]], axis=0),
    )

    def tie(*held):
        kept = {name: s.pop(name) for name in held if name in s}
        fixed = lax.optimization_barrier(dict(s))
        s.clear()
        s.update(fixed)
        s.update(kept)

    def push(name):
        s[name] = s[name] + [ring.shift(s[name][-1])]

    def reduce_step(name, k):
        term = ring.term(s[name + "_own"], s[name + "_other"], k + 1)
        if k:
            term = (s[name].astype(F32) + term.astype(F32)).astype(BF)
        s[name] = ring.shift(term)

    def reduce_end(name):
        own, other = s.pop(name + "_own"), s.pop(name + "_other")
        return s.pop(name).astype(F32) + ring.term(own, other, count).astype(F32)

    quarter = out_weight.shape[0] // 4
    s["qs"] = [lax.dynamic_slice_in_dim(out_weight, square.index * quarter, quarter, 0)]
    s["xs"], s["cs"] = [s["x"]], [s["cot"]]
    for k in range(steps):
        push("xs")
        if k == 0:
            s["aw2"] = swap_row(s["aw"])
            s["gains2"] = swap_row(s["gains"])
            s["cos"], s["sin"] = rope_tables()
            inputs = s["x"].astype(F32)
            squares = jnp.sum(inputs * inputs, axis=1)
            s["first_scale"] = lax.rsqrt(row_total(squares) / width + norm_epsilon)
        if k == 1:
            s["gw2"] = swap_row(s["gw"])
        if k == 2:
            s["uw2"] = swap_row(s["uw"])
        if k >= 2 and len(s["qs"]) < count:
            push("qs")
        tie()

    push("cs")
    if len(s["qs"]) < count:
        push("qs")
    both = ring.place([s.pop("xs")], 1)
    s["xo"] = both[:LEN]
    s["xt"] = swap_row(both[LEN:])
    s["n1o"], s["n1t"], s["qkv"], s["scale1"] = project(
        s["xo"],
        s["xt"],
        s["gains"][:1],
        s["gains2"][:1],
        s["aw"],
        s["aw2"],
        s["cos"],
        s["sin"],
    )
    tie()
    for k in range(1, steps - 1):
        push("cs")
        if len(s["qs"]) < count:
            push("qs")
        if k == 1:
            mixed, s["log_total"] = attend(s["qkv"], 0, 1)
            s["mixed"] = [mixed]
        tie()

    push("mixed")
    push("cs")
    s["dw2"] = swap_row(s["dw"])
    held = jnp.stack(s.pop("qs"), axis=0)
    s["ow"] = [held[: count // 2], held[count // 2 :]]
    s["ow_got"] = square.hop(s["ow"], 1)
    tie()
    push("mixed")
    s["ow"] = square.join(s["ow"], s.pop("ow_got"), 1, 1)
    s["ow_got"] = square.hop(s["ow"], 2)
    both = ring.place([s.pop("cs")], 1)
    s["co"] = both[:LEN]
    s["ct"] = swap_row(both[LEN:])
    s["back"] = product("nt", [s["co"]], [s["dw"]], F32)
    s["back"] = product("nt", [s["ct"]], [s["dw2"]], F32, s["back"])
    tie()
    for k in range(2, steps):
        push("mixed")
        if k == 2:
            first, second = square.join(s.pop("ow"), s.pop("ow_got"), 2, 1)
            shape = second.shape
            second = second.reshape(shape[0], 2, 2, quarter, half).swapaxes(1, 2).reshape(shape)
            s["owo"] = jnp.concatenate([first, second], axis=0)
            s["owt"] = swap_row(s["owo"])
            s["ro"], s["rt"] = mix(s["mixed"][:3], s["owo"], s["owt"], s["xo"], s["xt"], 0)
        tie()

    gains, gains2 = s["gains"], s["gains2"]
    s["ro"], s["rt"], s["n2o"], s["n2t"] = mix(
        s["mixed"][3:], s["owo"], s["owt"], s["ro"], s["rt"], 3, (gains[1:], gains2[1:])
    )
    s["hidden"], s["gg"], s["ug"] = feed(
        s["n2o"], s["n2t"], s.pop("back"), s["gw"], s["gw2"], s["uw"], s["uw2"]
    )
    tie()
    s["dn_other"] = product("nn", [s["hidden"]], [s.pop("dw2")])
    tie()
    s["dn_other"] = swap_row(s["dn_other"])
    s["dn_own"] = product("nn", [s["hidden"]], [s.pop("dw")])
    tie()
    reduce_step("dn", 0)
    s["down_other"] = product("tn", [s["hidden"]], [s.pop("ct")])
    tie("dn")
    s["down_other"] = swap_row(s["down_other"])
    s["sg_other"] = product("nt", [s["gg"], s["ug"]], [s.pop("gw2"), s.pop("uw2")])
    tie()
    s["sg_other"] = swap_row(s["sg_other"])
    s["down"] = product("tn", [s.pop("hidden")], [s.pop("co")], extra=s.pop("down_other"))
    tie()
    s["down"] = lax.psum_scatter(s["down"], "dp", scatter_dimension=0, tiled=True)
    s["sg_own"] = product("nt", [s["gg"], s["ug"]], [s.pop("gw"), s.pop("uw")])
    tie("down")

    take = lambda v: lax.dynamic_slice_in_dim(v, own_at * rows, rows, 0)
    reduce_step("sg", 0)
    s["both_other"] = product_beside(s.pop("n2t"), s["gg"], s["ug"])
    s["res"] = jnp.where(local, take(s.pop("ro")), swap_row(take(s.pop("rt"))))
    tie()
    s["down"] = lax.all_gather(s["down"], "dp", axis=0, tiled=True)
    reduce_step("sg", 1)
    s["both_other"] = swap_row(s["both_other"])
    residual = s["res"]
    squares = row_total(jnp.sum(residual * residual, axis=1))
    s["second_scale"] = lax.rsqrt(squares / width + norm_epsilon)

    def tokens(which):
        part = [
            lax.dynamic_slice_in_dim(v, own_at * rows + which * size, size, 0)
            for v in s["mixed"]
        ]
        return jnp.concatenate(
            [v[:, q * quarter : (q + 1) * quarter] for q in range(4) for v in part], axis=1
        )

    s["mixed_rows"] = jnp.where(local, tokens(core), swap_row(tokens(1 - core)))
    s["mixed"] = s["mixed"][0]
    s["both"] = product_beside(s.pop("n2o"), s.pop("gg"), s.pop("ug"), s.pop("both_other"))
    tie("down")
    for k in range(2, steps):
        reduce_step("sg", k)
        if k == 2:
            s["both"] = lax.psum_scatter(s["both"], "dp", scatter_dimension=0, tiled=True)
        tie("both", "down")

    reduce_step("dn", 1)
    second_grad = reduce_end("sg")
    second_hat = s["res"] * s["second_scale"][:, None]
    s["feed_part"] = jnp.sum(second_grad * second_hat, axis=0, keepdims=True)
    weighted = second_grad * s["gains"][1:]
    second_mean = row_total(jnp.sum(weighted * second_hat, axis=1)) / width
    s["residual_grad"] = s["cot"].astype(F32) + s["second_scale"][:, None] * (
        weighted - second_hat * second_mean[:, None]
    )
    low = s["residual_grad"].astype(BF)
    s["low_own"] = lax.dynamic_slice_in_dim(low, core * size, size, 0)
    s["low_other"] = swap_row(lax.dynamic_slice_in_dim(low, (1 - core) * size, size, 0))
    heads = s["mixed"].shape[1]
    grads = product(
        "nt",
        [s["low_own"], s["low_other"]],
        [s.pop("owo").reshape(-1, half), s.pop("owt").reshape(-1, half)],
    )
    s["grads"] = [grads[:, i * heads : (i + 1) * heads] for i in range(count)]
    tie("both")

    s["grads"] = [ring.shift(v, -i) if i else v for i, v in enumerate(s["grads"])]
    other = swap_row(product("tn", [s["mixed_rows"]], [s.pop("low_other")]))
    s["out"] = product("tn", [s.pop("mixed_rows")], [s.pop("low_own")], extra=other)
    tie("both")

    for k in range(2, steps):
        reduce_step("dn", k)
        if k < steps - 1:
            tie("both", "down")
    s["out"] = lax.psum_scatter(s["out"], "dp", scatter_dimension=0, tiled=True)
    both = ring.place([s.pop("grads")], -1)
    mine, theirs = both[: LEN // 2], swap_row(both[LEN // 2 :])
    mine, theirs = (v.reshape(-1, size, heads) for v in (mine, theirs))
    grad = jnp.stack(
        [jnp.where(core == 0, mine, theirs), jnp.where(core == 0, theirs, mine)], axis=1
    ).reshape(LEN, heads)
    s["pg"] = attend_back(
        s.pop("qkv"), grad, s.pop("mixed"), s.pop("log_total"), s.pop("cos"), s.pop("sin")
    )
    tie("out")
    s["both"] = lax.all_gather(s["both"], "dp", axis=0, tiled=True)
    s["fg_local"] = product("nt", [s["pg"]], [s.pop("aw2")])
    s["attn_other"] = product("tn", [s.pop("n1t")], [s["pg"]], tile=PAIR)
    tie("both", "out")
    s["fg_other"] = swap_row(s["fg_local"])
    s["attn_other"] = swap_row(s["attn_other"])
    s["fg_own"] = product("nt", [s["pg"]], [s.pop("aw")])
    tie("both")

    def split(name):
        values = s[name]
        cut = values.shape[0] // 2
        s[name] = [[values[:cut]], [values[cut:]]]
        s[name + "_got"] = square.send(s[name], 1, 0)

    def phase(name, which):
        got = s.pop(name + "_got")
        if which == 2:
            s[name] = [[v] for v in square.add(s[name], got, 1, 0)]
            s[name + "_got"] = square.send(s[name], 2, 0)
        if which == 3:
            s[name] = square.add(s[name], got, 2, 0, BF)
            s[name + "_got"] = square.hop(s[name], 2)
        if which == 4:
            s[name] = square.join(s[name], got, 2, 0)
            s[name + "_got"] = square.hop(s[name], 1)
        if which == 5:
            halves = square.join(s[name], got, 1, 0)
            s[name] = jnp.concatenate(halves, axis=0).astype(F32)

    def out_step(k):
        term = s["out"][(k + 1) % count]
        if k:
            term = (s["out_ring"].astype(F32) + term.astype(F32)).astype(BF)
        s["out_ring"] = ring.shift(term)

    reduce_step("fg", 0)
    s["attn"] = product("tn", [s.pop("n1o")], [s.pop("pg")], extra=s.pop("attn_other"), tile=PAIR)
    scale1 = s.pop("scale1")[:, :1]
    part = lambda grad, inputs: jnp.sum(
        grad.astype(F32) * (inputs.astype(F32) * scale1), axis=0, keepdims=True
    )
    other = swap_row(part(s.pop("fg_local"), s.pop("xt")))
    s["parts"] = jnp.concatenate(
        [part(s["fg_own"], s.pop("xo")) + other, s.pop("feed_part")], axis=0
    )
    tie("both", "out")
    reduce_step("fg", 1)
    split("attn")
    s["parts"] = s["parts"] + square.hops[0](s["parts"])
    s["output"] = (s.pop("res") + reduce_end("dn")).astype(BF)
    s["down"] = s["down"].astype(F32)
    tie("both")
    s["out"] = s["out"].reshape(count, quarter, half)
    for k in range(2, steps):
        reduce_step("fg", k)
        if k == 2:
            phase("attn", 2)
            out_step(0)
            s["parts"] = s["parts"] + square.hops[1](s["parts"])
            tie("both", "fg")
            phase("attn", 3)
            out_step(1)
            parts = s.pop("parts")
            s["parts"] = sum([ring.shift(parts, i) for i in range(1, count)], parts)
        tie("both")
    phase("attn", 4)
    for k in range(2, steps):
        out_step(k)
    first_grad = reduce_end("fg")
    scale = s["first_scale"][:, None]
    first_hat = s["x"].astype(F32) * scale
    weighted = first_grad * s["gains"][:1]
    first_mean = row_total(jnp.sum(weighted * first_hat, axis=1)) / width
    s["input"] = s["residual_grad"] + scale * (weighted - first_hat * first_mean[:, None])
    tie("both")
    out = (s.pop("out_ring").astype(F32) + s["out"][0].astype(F32)).astype(BF)
    s["out"] = join(out, square.hops[0](out), square.bits[0], 0)
    tie("both")
    s["out"] = join(s["out"], square.hops[1](s["out"]), square.bits[1], 0).astype(F32)
    phase("attn", 5)
    tie()
    units = gate_weight.shape[1]
    s["gate"] = s["both"][:, :units].astype(F32)
    s["up"] = s.pop("both")[:, units:].astype(F32)
    return (
        s["output"],
        s["input"],
        s["parts"][0],
        s["attn"],
        s["out"],
        s["parts"][1],
        s["gate"],
        s["up"],
        s["down"],
    )


def solution(mesh):
    in_specs = (
        P(("dp", "col"), "row"),
        P("row"),
        P("row", "col"),
        P("col", "row"),
        P("row"),
        P("row", "col"),
        P("row", "col"),
        P("col", "row"),
        P(("dp", "col"), "row"),
    )
    out_specs = (
        P(("dp", "col"), "row"),
        P(("dp", "col"), "row"),
        P("row"),
        P("row", "col"),
        P("col", "row"),
        P("row"),
        P("row", "col"),
        P("row", "col"),
        P("col", "row"),
    )
    return jax.shard_map(shards, mesh=mesh, in_specs=in_specs, out_specs=out_specs, check_vma=False)
```

time: 1020 us -> 815 us (0.80)
  waiting for transfers between devices: 490 us -> 310 us
  Pallas kernels: 103 us -> 271 us
  matrix products: 116 us -> 0 us
  starting transfers between devices: 124 us -> 79.6 us
  blocking collectives: 40.9 us -> 0 us
  local copies, waits for them, and re-layouts: 27.7 us -> 45.9 us
  between operations: 30.2 us -> 15.1 us
    ppermute x42 -> x16, waiting for transfers between devices: 243 us -> 67.9 us  [__init__(): lax.ppermute(v, 'dp', [(i, i ^ flip) for i in range(4)])]
    pallas_call x2 -> x20, Pallas kernels: 50 us -> 218 us  [the longest x15 138 us: product(): pl.pallas_call(functools.partial(product_kernel, kind, len(lefts), len(mo...]
    dot_general x20 -> x0, matrix products: 116 us -> none  [the longest x10 50.9 us: tn(): lax.dot_general(left, right, (((0,), (0,)), ((), ())), preferred_element_...]
    psum x1 -> x0, blocking collectives: 40.9 us -> none  [shards(): lax.psum((attn_part, feed_part), ('dp', 'col'))]
    ppermute x42 -> x16, starting transfers between devices: 54.3 us -> 17.5 us  [__init__(): lax.ppermute(v, 'dp', [(i, i ^ flip) for i in range(4)])]
    ppermute x27 -> x30, waiting for transfers between devices: 247 us -> 215 us  [shift(): return lax.ppermute(values, 'col', pairs)]
    reduce_scatter x0 -> x3, waiting for transfers between devices: none -> 16 us  [the longest x1 11.3 us: shards(): s['out'] = lax.psum_scatter(s['out'], 'dp', scatter_dimension=0, tiled=True)]
    unnamed x142 -> x114, local copies, waits for them, and re-layouts: 7.76 us -> 20.3 us
  transfers between devices with their start and end apart: 93 -> 75, of which waited for: 40 -> 37; matrix products, arithmetic and copies ran while one was open for 18% -> 12% of each run, Pallas kernels for 7% -> 27%
where the time goes in v2:
time: 815 us; the launch traced here: 806 us
  waiting for transfers between devices  310 us (38%)
  Pallas kernels  271 us (33%)
  other arithmetic  84.1 us (10%)
  starting transfers between devices  79.6 us (10%)
  local copies, waits for them, and re-layouts  45.9 us (6%)
  between operations  15.1 us (2%)
    ppermute x30, waiting for transfers between devices, shift(): return lax.ppermute(values, 'col', pairs)  215 us
    pallas_call x15, Pallas kernels, product(): pl.pallas_call(functools.partial(product_kernel, kind, len(lefts), len(mo...  138 us
    ppermute x16, waiting for transfers between devices, __init__(): lax.ppermute(v, 'dp', [(i, i ^ flip) for i in range(4)])  67.9 us
    ppermute x30, starting transfers between devices, shift(): return lax.ppermute(values, 'col', pairs)  58.6 us
    pallas_call x2, Pallas kernels, product_beside(): pl.pallas_call(functools.partial(beside_kernel, tiles, len(more)), grid=(...  31.8 us
    pallas_call x1, Pallas kernels, feed(): pl.pallas_call(feed_kernel, grid=(units // BLOCK,), in_specs=[tokens] * 2...  26.2 us
    pallas_call x2, Pallas kernels, mix(): pl.pallas_call(functools.partial(mix_kernel, offset, groups, count, last)...  22 us
    unnamed x114, local copies, waits for them, and re-layouts  20.3 us
  transfers between devices with their start and end apart: 75, of which 37 were waited for; matrix products, arithmetic and copies ran while one was open for 12% of the time, Pallas kernels for 27%

profile of v2, /device:TPU:0, one launch (start us, length us, event | category | flops | bytes accessed | tf_op | source)
XLA Modules:
  0.0 806.0 jit_solution(16326777072472654884)
XLA Ops:
  18.7 16.0 %collective-permute-done.3 = bf16[512,1024]{1,0:T(8,128)(2,1)S(1)} collective-permute-done((bf16[512,1024]{1,0:T(8,128)(2,1)}, bf16[512,1024]{1,0:T(8,128)(2,1)S(1)}, u32[]{:S(2)}, u32[]{:S(2)}) %collective-permute-start.3) | collective-permute-done | bytes 1048608 | tf_op jit(solution)/shard_map/ppermute | solution.py:393
  38.1 23.0 %collective-permute-done.5 = bf16[512,1024]{1,0:T(8,128)(2,1)S(1)} collective-permute-done((bf16[512,1024]{1,0:T(8,128)(2,1)S(1)}, bf16[512,1024]{1,0:T(8,128)(2,1)S(1)}, u32[]{:S(2)}, u32[]{:S(2)}) %collective-permute-start.5) | collective-permute-done | bytes 1048608 | tf_op jit(solution)/shard_map/ppermute | solution.py:393
  66.6 27.8 %collective-permute-done.6 = bf16[128,1024]{1,0:T(8,128)(2,1)} collective-permute-done((bf16[128,1024]{1,0:T(8,128)(2,1)S(1)}, bf16[128,1024]{1,0:T(8,128)(2,1)}, u32[]{:S(2)}, u32[]{:S(2)}) %collective-permute-start.6) | collective-permute-done | bytes 262176 | tf_op jit(solution)/shard_map/ppermute | solution.py:393
  104.4 17.4 %shard_map.160 = (bf16[1024,1024]{1,0:T(8,128)(2,1)}, bf16[1024,1024]{1,0:T(8,128)(2,1)}, bf16[1024,1536]{1,0:T(8,128)(2,1)}, f32[1024,128]{1,0:T(8,128)}) custom-call(bf16[1024,1024]{1,0:T(8,128)(2,1)} %get-tuple-element.1435.xo.refs_5_, bf16[1024,1024]{1,0:T(8,128)(2,1)} %copy-done.33, f32[1,1024]{1,0:T(1,128)} %slice.184.go, f32[1,1024]{1,0:T(1,128)} %slice.185.gt, ...), custom_call_target="tpu_custom_call" | custom-call | flops 9774999552 | bytes 1 | tf_op jit(solution)/shard_map/pallas_call | solution.py:88
  121.8 8.9 %collective-permute-done.11 = bf16[128,1024]{1,0:T(8,128)(2,1)S(1)} collective-permute-done((bf16[128,1024]{1,0:T(8,128)(2,1)}, bf16[128,1024]{1,0:T(8,128)(2,1)S(1)}, u32[]{:S(2)}, u32[]{:S(2)}) %collective-permute-start.11) | collective-permute-done | bytes 262176 | tf_op jit(solution)/shard_map/ppermute | solution.py:393
  134.2 15.5 %shard_map.161 = (bf16[1024,512]{1,0:T(8,128)(2,1)S(1)}, f32[1024,512]{1,0:T(8,128)S(1)}) custom-call(bf16[1024,1536]{1,0:T(8,128)(2,1)} %get-tuple-element.1372.qkv), custom_call_target="tpu_custom_call" | custom-call | flops 9200000000 | bytes 1 | tf_op jit(solution)/shard_map/pallas_call | solution.py:133
  149.7 12.2 %collective-permute-done.13 = bf16[128,1024]{1,0:T(8,128)(2,1)S(1)} collective-permute-done((bf16[128,1024]{1,0:T(8,128)(2,1)S(1)}, bf16[128,1024]{1,0:T(8,128)(2,1)S(1)}, u32[]{:S(2)}, u32[]{:S(2)}) %collective-permute-start.13) | collective-permute-done | bytes 262176 | tf_op jit(solution)/shard_map/ppermute | solution.py:393
  169.6 10.9 %collective-permute-done.17 = bf16[2,128,1024]{2,1,0:T(8,128)(2,1)S(1)} collective-permute-done((bf16[2,128,1024]{2,1,0:T(8,128)(2,1)S(1)}, bf16[2,128,1024]{2,1,0:T(8,128)(2,1)S(1)}, u32[]{:S(2)}, u32[]{:S(2)}) %collective-permute-start.17) | collective-permute-done | bytes 524320 | tf_op jit(solution)/shard_map/ppermute | solution.py:438
  181.8 7.0 collective-permute-done.14
  188.8 22.1 %collective-permute-done.16.refs_1_ = bf16[1024,512]{1,0:T(8,128)(2,1)S(1)} collective-permute-done((bf16[1024,512]{1,0:T(8,128)(2,1)S(1)}, bf16[1024,512]{1,0:T(8,128)(2,1)S(1)}, u32[]{:S(2)}, u32[]{:S(2)}) %collective-permute-start.16) | collective-permute-done | bytes 1048608 | tf_op jit(solution)/shard_map/ppermute | solution.py:393
  222.6 9.2 %shard_map.162.refs_2_ = f32[1024,2048]{1,0:T(8,128)} custom-call(bf16[1024,1024]{1,0:T(8,128)(2,1)} %get-tuple-element.1147.refs_0_.refs_1_, bf16[2048,1024]{1,0:T(8,128)(2,1)} %refs_1_.1), custom_call_target="tpu_custom_call" | custom-call | flops 4206773760 | bytes 1 | tf_op jit(solution)/shard_map/pallas_call | solution.py:317
  231.7 11.5 %shard_map.163.back = f32[1024,2048]{1,0:T(8,128)} custom-call(bf16[1024,1024]{1,0:T(8,128)(2,1)} %collective-permute-done.19.refs_0_.refs_1_, bf16[2048,1024]{1,0:T(8,128)(2,1)} %copy-done.30, f32[1024,2048]{1,0:T(8,128)} %shard_map.162.refs_2_), custom_call_target="tpu_custom_call" | custom-call | flops 4206773760 | bytes 1 | tf_op jit(solution)/shard_map/pallas_call | solution.py:317
  249.2 6.7 collective-permute-done.24.refs_4_.refs_2_
  256.0 12.0 %shard_map.164 = (f32[1024,1024]{1,0:T(8,128)}, f32[1024,1024]{1,0:T(8,128)}) custom-call(bf16[1024,512]{1,0:T(8,128)(2,1)} %copy-done.2, bf16[1024,512]{1,0:T(8,128)(2,1)} %copy-done.44, bf16[1024,512]{1,0:T(8,128)(2,1)} %collective-permute-done.20.refs_2_, bf16[4,512,1024]{2,1,0:T(8,128)(2,1)} %copy-done.5, ...), custom_call_target="tpu_custom_call" | custom-call | flops 5175000064 | bytes 1 | tf_op jit(solution)/shard_map/pallas_call | solution.py:245
  268.0 6.7 collective-permute-done.23.refs_0_
  275.9 10.0 %shard_map.165 = (f32[1024,1024]{1,0:T(8,128)}, f32[1024,1024]{1,0:T(8,128)}, bf16[1024,1024]{1,0:T(8,128)(2,1)}, bf16[1024,1024]{1,0:T(8,128)(2,1)}) custom-call(bf16[1024,512]{1,0:T(8,128)(2,1)} %copy-done.32, bf16[4,512,1024]{2,1,0:T(8,128)(2,1)} %copy-done.5, bf16[4,512,1024]{2,1,0:T(8,128)(2,1)} %collective-permute-done.24.refs_4_.refs_2_, ...), custom_call_target="tpu_custom_call" | custom-call | flops 1724999936 | bytes 1 | tf_op jit(solution)/shard_map/pallas_call | solution.py:245
  285.9 26.2 %shard_map.166 = (bf16[1024,2048]{1,0:T(8,128)(2,1)}, bf16[1024,2048]{1,0:T(8,128)(2,1)}, bf16[1024,2048]{1,0:T(8,128)(2,1)}) custom-call(bf16[1024,1024]{1,0:T(8,128)(2,1)} %get-tuple-element.1246.no.refs_0_, bf16[1024,1024]{1,0:T(8,128)(2,1)} %get-tuple-element.1212.nt_.refs_0_, f32[1024,2048]{1,0:T(8,128)} %shard_map.163.back, bf16[1024,2048]{1,0:T(8,128)(2,1)} %refs_2_, ...), custom_call_target="tpu_custom_call" | custom-call | flops 14949999616 | bytes 1 | tf_op jit(solution)/shard_map/pallas_call | solution.py:273
  312.1 8.5 %shard_map.167 = bf16[1024,1024]{1,0:T(8,128)(2,1)} custom-call(bf16[1024,2048]{1,0:T(8,128)(2,1)} %get-tuple-element.1146.refs_0_, bf16[2048,1024]{1,0:T(8,128)(2,1)} %copy-done.30), custom_call_target="tpu_custom_call" | custom-call | flops 4206773760 | bytes 1 | tf_op jit(solution)/shard_map/pallas_call | solution.py:317
  320.6 8.5 %shard_map.168 = bf16[1024,1024]{1,0:T(8,128)(2,1)} custom-call(bf16[1024,2048]{1,0:T(8,128)(2,1)} %get-tuple-element.1146.refs_0_, bf16[2048,1024]{1,0:T(8,128)(2,1)} %refs_1_.1), custom_call_target="tpu_custom_call" | custom-call | flops 4206773760 | bytes 1 | tf_op jit(solution)/shard_map/pallas_call | solution.py:317
  329.1 10.5 %shard_map.169 = bf16[2048,1024]{1,0:T(8,128)(2,1)} custom-call(bf16[1024,2048]{1,0:T(8,128)(2,1)} %get-tuple-element.1146.refs_0_, bf16[1024,1024]{1,0:T(8,128)(2,1)} %collective-permute-done.19.refs_0_.refs_1_), custom_call_target="tpu_custom_call" | custom-call | flops 4206773760 | bytes 1 | tf_op jit(solution)/shard_map/pallas_call | solution.py:317
  344.4 14.8 %shard_map.170 = bf16[1024,1024]{1,0:T(8,128)(2,1)} custom-call(bf16[1024,2048]{1,0:T(8,128)(2,1)} %get-tuple-element.1247.refs_0_.refs_1_, bf16[1024,2048]{1,0:T(8,128)(2,1)} %get-tuple-element.1248.refs_1_.refs_2_, bf16[1024,2048]{1,0:T(8,128)(2,1)} %copy-done.47, bf16[1024,2048]{1,0:T(8,128)(2,1)} %collective-permute-done.7.uwt.refs_3_), custom_call_target="tpu_custom_call" | custom-call | flops 7838547456 | bytes 1 | tf_op jit(solution)/shard_map/pallas_call | solution.py:317
  359.1 9.4 %collective-permute-done.26 = bf16[512,1024]{1,0:T(8,128)(2,1)S(1)} collective-permute-done((bf16[512,1024]{1,0:T(8,128)(2,1)}, bf16[512,1024]{1,0:T(8,128)(2,1)S(1)}, u32[]{:S(2)}, u32[]{:S(2)}) %collective-permute-start.26) | collective-permute-done | bytes 1048608 | tf_op jit(solution)/shard_map/ppermute | solution.py:393
  368.5 10.8 %shard_map.171 = bf16[2048,1024]{1,0:T(8,128)(2,1)} custom-call(bf16[1024,2048]{1,0:T(8,128)(2,1)} %get-tuple-element.1146.refs_0_, bf16[1024,1024]{1,0:T(8,128)(2,1)} %get-tuple-element.1147.refs_0_.refs_1_, bf16[2048,1024]{1,0:T(8,128)(2,1)} %collective-permute-done.27.refs_2_), custom_call_target="tpu_custom_call" | custom-call | flops 4206773760 | bytes 1 | tf_op jit(solution)/shard_map/pallas_call | solution.py:317
  379.4 15.4 %shard_map.172 = bf16[1024,1024]{1,0:T(8,128)(2,1)} custom-call(bf16[1024,2048]{1,0:T(8,128)(2,1)} %get-tuple-element.1247.refs_0_.refs_1_, bf16[1024,2048]{1,0:T(8,128)(2,1)} %get-tuple-element.1248.refs_1_.refs_2_, bf16[1024,2048]{1,0:T(8,128)(2,1)} %refs_2_, bf16[1024,2048]{1,0:T(8,128)(2,1)} %refs_3_), custom_call_target="tpu_custom_call" | custom-call | flops 7838547456 | bytes 1 | tf_op jit(solution)/shard_map/pallas_call | solution.py:317
  402.9 15.1 %shard_map.173 = bf16[1024,4096]{1,0:T(8,128)(2,1)} custom-call(bf16[1024,1024]{1,0:T(8,128)(2,1)} %get-tuple-element.1212.nt_.refs_0_, bf16[1024,2048]{1,0:T(8,128)(2,1)} %get-tuple-element.1247.refs_0_.refs_1_, bf16[1024,2048]{1,0:T(8,128)(2,1)} %get-tuple-element.1248.refs_1_.refs_2_), custom_call_target="tpu_custom_call" | custom-call | flops 9200000000 | bytes 1 | tf_op jit(solution)/shard_map/pallas_call | solution.py:360
  420.1 6.5 collective-permute-done.30
  453.0 16.7 %shard_map.174 = bf16[1024,4096]{1,0:T(8,128)(2,1)} custom-call(bf16[1024,1024]{1,0:T(8,128)(2,1)} %get-tuple-element.1246.no.refs_0_, bf16[1024,2048]{1,0:T(8,128)(2,1)} %get-tuple-element.1247.refs_0_.refs_1_, bf16[1024,2048]{1,0:T(8,128)(2,1)} %get-tuple-element.1248.refs_1_.refs_2_, bf16[1024,4096]{1,0:T(8,128)(2,1)} %collective-permute-done.31.refs_3_), custom_call_target="tpu_custom_call" | custom-call | flops 9200000000 | bytes 1 | tf_op jit(solution)/shard_map/pallas_call | solution.py:360
  469.7 5.6 collective-permute-done.34
  481.8 22.6 %collective-permute-done.35 = bf16[512,1024]{1,0:T(8,128)(2,1)S(1)} collective-permute-done((bf16[512,1024]{1,0:T(8,128)(2,1)}, bf16[512,1024]{1,0:T(8,128)(2,1)S(1)}, u32[]{:S(2)}, u32[]{:S(2)}) %collective-permute-start.35) | collective-permute-done | bytes 1048608 | tf_op jit(solution)/shard_map/ppermute | solution.py:393
  518.6 7.0 shard_map.175
  527.7 8.1 %collective-permute-done.36 = bf16[512,1024]{1,0:T(8,128)(2,1)} collective-permute-done((bf16[512,1024]{1,0:T(8,128)(2,1)}, bf16[512,1024]{1,0:T(8,128)(2,1)}, u32[]{:S(2)}, u32[]{:S(2)}) %collective-permute-start.36) | collective-permute-done | bytes 1048608 | tf_op jit(solution)/shard_map/ppermute | solution.py:393
  547.7 5.0 shard_map.177
  552.8 5.5 collective-permute-done.40
  567.7 6.1 collective-permute-start.43
  576.0 20.1 %shard_map.178.refs_1_.refs_0_ = bf16[1024,1536]{1,0:T(8,128)(2,1)} custom-call(bf16[1024,1536]{1,0:T(8,128)(2,1)} %get-tuple-element.1372.qkv, bf16[1024,512]{1,0:T(8,128)(2,1)} %bitcast.40, bf16[1024,512]{1,0:T(8,128)(2,1)} %copy-done.2, f32[1024,512]{1,0:T(8,128)} %copy-done.4, f32[1024,128]{1,0:T(8,128)} %get-tuple-element.1379.cos, ...), custom_call_target="tpu_custom_call" | custom-call | flops 11500000256 | bytes 1 | tf_op jit(solution)/shard_map/pallas_call | solution.py:194
  597.8 8.9 %shard_map.179 = bf16[1024,1536]{1,0:T(8,128)(2,1)} custom-call(bf16[1024,1024]{1,0:T(8,128)(2,1)} %get-tuple-element.1387.refs_0_, bf16[1024,1536]{1,0:T(8,128)(2,1)} %shard_map.178.refs_1_.refs_0_), custom_call_target="tpu_custom_call" | custom-call | flops 3298830336 | bytes 1 | tf_op jit(solution)/shard_map/pallas_call | solution.py:317
  606.6 7.1 shard_map.180
  614.2 7.1 shard_map.181
  621.3 11.3 %reduce-scatter.8.cloned.1.call-done = bf16[512,1024]{1,0:T(8,128)(2,1)} async-done(((bf16[2048,1024]{1,0:T(8,128)(2,1)}), bf16[512,1024]{1,0:T(8,128)(2,1)}) %reduce-scatter.8.cloned.1.call-update) | async-done | bytes 1048592 | tf_op jit(solution)/shard_map/reduce_scatter | solution.py:685
  643.5 9.6 %shard_map.182 = bf16[1024,1536]{1,0:T(8,128)(2,1)} custom-call(bf16[1024,1024]{1,0:T(8,128)(2,1)} %get-tuple-element.1424.refs_0_, bf16[1024,1536]{1,0:T(8,128)(2,1)} %shard_map.178.refs_1_.refs_0_, bf16[1024,1536]{1,0:T(8,128)(2,1)} %collective-permute-done.45.refs_2_), custom_call_target="tpu_custom_call" | custom-call | flops 3298830336 | bytes 1 | tf_op jit(solution)/shard_map/pallas_call | solution.py:317
  653.1 8.1 collective-permute-done.47
  681.5 18.8 %collective-permute-done.52 = f32[2,1024]{1,0:T(2,128)S(1)} collective-permute-done((f32[2,1024]{1,0:T(2,128)S(1)}, f32[2,1024]{1,0:T(2,128)S(1)}, u32[]{:S(2)}, u32[]{:S(2)}) %collective-permute-start.52) | collective-permute-done | bytes 8224 | tf_op jit(solution)/shard_map/ppermute | solution.py:438
  700.2 5.0 collective-permute-done.50
  716.2 10.4 %collective-permute-done.56 = f32[2,1024]{1,0:T(2,128)S(1)} collective-permute-done((f32[2,1024]{1,0:T(2,128)S(1)}, f32[2,1024]{1,0:T(2,128)S(1)}, u32[]{:S(2)}, u32[]{:S(2)}) %collective-permute-start.56) | collective-permute-done | bytes 8224 | tf_op jit(solution)/shard_map/ppermute | solution.py:438
  735.6 7.1 collective-permute-done.63
  768.9 5.7 collective-permute-done.68
  778.6 6.7 collective-permute-done.69
  787.5 11.8 %slice_convert_fusion = (f32[1024,2048]{1,0:T(8,128)}, f32[1024,2048]{1,0:T(8,128)}) fusion(bf16[1024,4096]{1,0:T(8,128)(2,1)} %all-gather.5.cloned.1.call-done), kind=kLoop, calls=%fused_computation.1 | loop fusion | flops 4194304 | bytes 25165824 | tf_op jit(solution)/shard_map/convert_element_type | solution.py:780
  (348 shorter events, 234.1 us)
Async XLA Ops:
  7.2 424.2 %reduce-scatter.4.cloned.1.call-start = ((), (), s32[]{:S(2)}) async-start(), calls=%async_computation.3 | async-start | bytes 5242880 | tf_op jit(solution)/shard_map/reduce_scatter | solution.py:620
  7.2 27.5 %collective-permute-start = (bf16[1024,1536]{1,0:T(8,128)(2,1)}, bf16[1024,1536]{1,0:T(8,128)(2,1)}, u32[]{:S(2)}, u32[]{:S(2)}) collective-permute-start(bf16[1024,1536]{1,0:T(8,128)(2,1)} %refs_1_.2), channel_id=1, source_target_pairs={{0,4},{4,0},{1,5},{5,1},{2,6},{6,2},{3,7},{7,3},{8,12},{12,8},{9,1... | collective-permute-start | bytes 9437192 | tf_op jit(solution)/shard_map/ppermute | solution.py:378
  7.8 27.0 %collective-permute-start.3 = (bf16[512,1024]{1,0:T(8,128)(2,1)}, bf16[512,1024]{1,0:T(8,128)(2,1)S(1)}, u32[]{:S(2)}, u32[]{:S(2)}) collective-permute-start(bf16[512,1024]{1,0:T(8,128)(2,1)} %param.9), channel_id=1, source_target_pairs={{0,2},{2,3},{3,1},{1,0},{4,6},{6,7},{7,5},{5,4},{8,10},{10,11},{11... | collective-permute-start | bytes 3145736 | tf_op jit(solution)/shard_map/ppermute | solution.py:393
  34.8 26.4 %collective-permute-start.4 = (bf16[1024,2048]{1,0:T(8,128)(2,1)S(1)}, bf16[1024,2048]{1,0:T(8,128)(2,1)S(1)}, u32[]{:S(2)}, u32[]{:S(2)}) collective-permute-start(bf16[1024,2048]{1,0:T(8,128)(2,1)S(1)} %copy-done.46), channel_id=1, source_target_pairs={{0,4},{4,0},{1,5},{5,1},{2,6},{6,2},{3,7},{7,3},{8,12},{12,8},{9,1... | collective-permute-start | bytes 12582920 | tf_op jit(solution)/shard_map/ppermute | solution.py:378
  34.8 26.4 %collective-permute-start.5 = (bf16[512,1024]{1,0:T(8,128)(2,1)S(1)}, bf16[512,1024]{1,0:T(8,128)(2,1)S(1)}, u32[]{:S(2)}, u32[]{:S(2)}) collective-permute-start(bf16[512,1024]{1,0:T(8,128)(2,1)S(1)} %collective-permute-done.3), channel_id=1, source_target_pairs={{0,2},{2,3},{3,1},{1,0},{4,6},{6,7},{7,5},{5,4},{8,10},{10,11},{11... | collective-permute-start | bytes 3145736 | tf_op jit(solution)/shard_map/ppermute | solution.py:393
  61.1 33.3 %collective-permute-start.7 = (bf16[1024,2048]{1,0:T(8,128)(2,1)}, bf16[1024,2048]{1,0:T(8,128)(2,1)}, u32[]{:S(2)}, u32[]{:S(2)}) collective-permute-start(bf16[1024,2048]{1,0:T(8,128)(2,1)} %refs_3_), channel_id=1, source_target_pairs={{0,4},{4,0},{1,5},{5,1},{2,6},{6,2},{3,7},{7,3},{8,12},{12,8},{9,1... | collective-permute-start | bytes 12582920 | tf_op jit(solution)/shard_map/ppermute | solution.py:378
  63.2 31.2 %collective-permute-start.8 = (bf16[512,1024]{1,0:T(8,128)(2,1)S(1)}, bf16[512,1024]{1,0:T(8,128)(2,1)}, u32[]{:S(2)}, u32[]{:S(2)}) collective-permute-start(bf16[512,1024]{1,0:T(8,128)(2,1)S(1)} %collective-permute-done.5), channel_id=1, source_target_pairs={{0,2},{2,3},{3,1},{1,0},{4,6},{6,7},{7,5},{5,4},{8,10},{10,11},{11... | collective-permute-start | bytes 3145736 | tf_op jit(solution)/shard_map/ppermute | solution.py:393
  66.5 27.9 %collective-permute-start.6 = (bf16[128,1024]{1,0:T(8,128)(2,1)S(1)}, bf16[128,1024]{1,0:T(8,128)(2,1)}, u32[]{:S(2)}, u32[]{:S(2)}) collective-permute-start(bf16[128,1024]{1,0:T(8,128)(2,1)S(1)} %constant_dynamic-slice_fusion.5), channel_id=1, source_target_pairs={{0,2},{2,3},{3,1},{1,0},{4,6},{6,7},{7,5},{5,4},{8,10},{10,11},{11... | collective-permute-start | bytes 786440 | tf_op jit(solution)/shard_map/ppermute | solution.py:393
  98.4 32.3 %collective-permute-start.9 = (bf16[512,1024]{1,0:T(8,128)(2,1)S(1)}, bf16[512,1024]{1,0:T(8,128)(2,1)S(1)}, u32[]{:S(2)}, u32[]{:S(2)}) collective-permute-start(bf16[512,1024]{1,0:T(8,128)(2,1)S(1)} %copy-done.26), channel_id=1, source_target_pairs={{0,2},{2,3},{3,1},{1,0},{4,6},{6,7},{7,5},{5,4},{8,10},{10,11},{11... | collective-permute-start | bytes 3145736 | tf_op jit(solution)/shard_map/ppermute | solution.py:393
  103.1 27.6 %collective-permute-start.11 = (bf16[128,1024]{1,0:T(8,128)(2,1)}, bf16[128,1024]{1,0:T(8,128)(2,1)S(1)}, u32[]{:S(2)}, u32[]{:S(2)}) collective-permute-start(bf16[128,1024]{1,0:T(8,128)(2,1)} %collective-permute-done.6), channel_id=1, source_target_pairs={{0,2},{2,3},{3,1},{1,0},{4,6},{6,7},{7,5},{5,4},{8,10},{10,11},{11... | collective-permute-start | bytes 786440 | tf_op jit(solution)/shard_map/ppermute | solution.py:393
  130.7 31.2 %collective-permute-start.12 = (bf16[512,1024]{1,0:T(8,128)(2,1)S(1)}, bf16[512,1024]{1,0:T(8,128)(2,1)S(1)}, u32[]{:S(2)}, u32[]{:S(2)}) collective-permute-start(bf16[512,1024]{1,0:T(8,128)(2,1)S(1)} %collective-permute-done.9), channel_id=1, source_target_pairs={{0,2},{2,3},{3,1},{1,0},{4,6},{6,7},{7,5},{5,4},{8,10},{10,11},{11... | collective-permute-start | bytes 3145736 | tf_op jit(solution)/shard_map/ppermute | solution.py:393
  134.0 27.9 %collective-permute-start.13 = (bf16[128,1024]{1,0:T(8,128)(2,1)S(1)}, bf16[128,1024]{1,0:T(8,128)(2,1)S(1)}, u32[]{:S(2)}, u32[]{:S(2)}) collective-permute-start(bf16[128,1024]{1,0:T(8,128)(2,1)S(1)} %collective-permute-done.11), channel_id=1, source_target_pairs={{0,2},{2,3},{3,1},{1,0},{4,6},{6,7},{7,5},{5,4},{8,10},{10,11},{11... | collective-permute-start | bytes 786440 | tf_op jit(solution)/shard_map/ppermute | solution.py:393
  161.9 49.0 %collective-permute-start.15 = (bf16[2048,1024]{1,0:T(8,128)(2,1)}, bf16[2048,1024]{1,0:T(8,128)(2,1)S(1)}, u32[]{:S(2)}, u32[]{:S(2)}) collective-permute-start(bf16[2048,1024]{1,0:T(8,128)(2,1)} %refs_1_.1), channel_id=1, source_target_pairs={{0,4},{4,0},{1,5},{5,1},{2,6},{6,2},{3,7},{7,3},{8,12},{12,8},{9,1... | collective-permute-start | bytes 12582920 | tf_op jit(solution)/shard_map/ppermute | solution.py:378
  161.9 26.9 %collective-permute-start.14 = (bf16[512,1024]{1,0:T(8,128)(2,1)S(1)}, bf16[512,1024]{1,0:T(8,128)(2,1)S(1)}, u32[]{:S(2)}, u32[]{:S(2)}) collective-permute-start(bf16[512,1024]{1,0:T(8,128)(2,1)S(1)} %collective-permute-done.12), channel_id=1, source_target_pairs={{0,2},{2,3},{3,1},{1,0},{4,6},{6,7},{7,5},{5,4},{8,10},{10,11},{11... | collective-permute-start | bytes 3145736 | tf_op jit(solution)/shard_map/ppermute | solution.py:393
  165.3 45.6 %collective-permute-start.16 = (bf16[1024,512]{1,0:T(8,128)(2,1)S(1)}, bf16[1024,512]{1,0:T(8,128)(2,1)S(1)}, u32[]{:S(2)}, u32[]{:S(2)}) collective-permute-start(bf16[1024,512]{1,0:T(8,128)(2,1)S(1)} %get-tuple-element.1377.refs_0_.mixed), channel_id=1, source_target_pairs={{0,2},{2,3},{3,1},{1,0},{4,6},{6,7},{7,5},{5,4},{8,10},{10,11},{11... | collective-permute-start | bytes 3145736 | tf_op jit(solution)/shard_map/ppermute | solution.py:393
  215.7 16.0 %collective-permute-start.19 = (bf16[1024,1024]{1,0:T(8,128)(2,1)}, bf16[1024,1024]{1,0:T(8,128)(2,1)}, u32[]{:S(2)}, u32[]{:S(2)}) collective-permute-start(bf16[1024,1024]{1,0:T(8,128)(2,1)} %get-tuple-element.1541), channel_id=1, source_target_pairs={{0,4},{4,0},{1,5},{5,1},{2,6},{6,2},{3,7},{7,3},{8,12},{12,8},{9,1... | collective-permute-start | bytes 6291464 | tf_op jit(solution)/shard_map/ppermute | solution.py:378
  215.7 27.6 %collective-permute-start.20 = (bf16[1024,512]{1,0:T(8,128)(2,1)}, bf16[1024,512]{1,0:T(8,128)(2,1)}, u32[]{:S(2)}, u32[]{:S(2)}) collective-permute-start(bf16[1024,512]{1,0:T(8,128)(2,1)} %copy-done.44), channel_id=1, source_target_pairs={{0,2},{2,3},{3,1},{1,0},{4,6},{6,7},{7,5},{5,4},{8,10},{10,11},{11... | collective-permute-start | bytes 3145736 | tf_op jit(solution)/shard_map/ppermute | solution.py:393
  219.3 25.4 %collective-permute-start.21 = (bf16[2,256,1024]{2,1,0:T(8,128)(2,1)S(1)}, bf16[2,256,1024]{2,1,0:T(8,128)(2,1)S(1)}, u32[]{:S(2)}, u32[]{:S(2)}) collective-permute-start(bf16[2,256,1024]{2,1,0:T(8,128)(2,1)S(1)} %pad_maximum_fusion.2), channel_id=1, source_target_pairs={{0,16},{8,24},{16,0},{24,8},{1,17},{9,25},{17,1},{25,9},{2,18},{10... | collective-permute-start | bytes 3145736 | tf_op jit(solution)/shard_map/ppermute | solution.py:438
  221.0 25.2 %collective-permute-start.22 = (bf16[2,256,1024]{2,1,0:T(8,128)(2,1)S(1)}, bf16[2,256,1024]{2,1,0:T(8,128)(2,1)}, u32[]{:S(2)}, u32[]{:S(2)}) collective-permute-start(bf16[2,256,1024]{2,1,0:T(8,128)(2,1)S(1)} %pad_maximum_fusion.3), channel_id=1, source_target_pairs={{0,8},{8,0},{16,24},{24,16},{1,9},{9,1},{17,25},{25,17},{2,10},{10... | collective-permute-start | bytes 3145736 | tf_op jit(solution)/shard_map/ppermute | solution.py:438
  248.7 26.0 %collective-permute-start.23 = (bf16[1024,512]{1,0:T(8,128)(2,1)}, bf16[1024,512]{1,0:T(8,128)(2,1)S(1)}, u32[]{:S(2)}, u32[]{:S(2)}) collective-permute-start(bf16[1024,512]{1,0:T(8,128)(2,1)} %collective-permute-done.20.refs_2_), channel_id=1, source_target_pairs={{0,2},{2,3},{3,1},{1,0},{4,6},{6,7},{7,5},{5,4},{8,10},{10,11},{11... | collective-permute-start | bytes 3145736 | tf_op jit(solution)/shard_map/ppermute | solution.py:393
  339.6 28.9 %collective-permute-start.27 = (bf16[2048,1024]{1,0:T(8,128)(2,1)}, bf16[2048,1024]{1,0:T(8,128)(2,1)}, u32[]{:S(2)}, u32[]{:S(2)}) collective-permute-start(bf16[2048,1024]{1,0:T(8,128)(2,1)} %shard_map.169), channel_id=1, source_target_pairs={{0,4},{4,0},{1,5},{5,1},{2,6},{6,2},{3,7},{7,3},{8,12},{12,8},{9,1... | collective-permute-start | bytes 12582920 | tf_op jit(solution)/shard_map/ppermute | solution.py:378
  342.8 25.7 %collective-permute-start.26 = (bf16[512,1024]{1,0:T(8,128)(2,1)}, bf16[512,1024]{1,0:T(8,128)(2,1)S(1)}, u32[]{:S(2)}, u32[]{:S(2)}) collective-permute-start(bf16[512,1024]{1,0:T(8,128)(2,1)} %dynamic-slice_select_fusion.5), channel_id=1, source_target_pairs={{0,2},{2,3},{3,1},{1,0},{4,6},{6,7},{7,5},{5,4},{8,10},{10,11},{11... | collective-permute-start | bytes 3145736 | tf_op jit(solution)/shard_map/ppermute | solution.py:393
  379.4 148.3 %all-gather.3.cloned.1.call-start = ((), (), s32[]{:S(2)}) async-start(), calls=%async_computation.4 | async-start | bytes 5242880 | tf_op jit(solution)/shard_map/all_gather | solution.py:629
  398.0 20.1 %collective-permute-start.29 = (f32[512,1024]{1,0:T(8,128)}, f32[512,1024]{1,0:T(8,128)}, u32[]{:S(2)}, u32[]{:S(2)}) collective-permute-start(f32[512,1024]{1,0:T(8,128)} %constant_dynamic-slice_fusion.4), channel_id=1, source_target_pairs={{0,4},{4,0},{1,5},{5,1},{2,6},{6,2},{3,7},{7,3},{8,12},{12,8},{9,1... | collective-permute-start | bytes 6291464 | tf_op jit(solution)/shard_map/ppermute | solution.py:378
  400.7 25.9 %collective-permute-start.30 = (bf16[512,1024]{1,0:T(8,128)(2,1)}, bf16[512,1024]{1,0:T(8,128)(2,1)}, u32[]{:S(2)}, u32[]{:S(2)}) collective-permute-start(bf16[512,1024]{1,0:T(8,128)(2,1)} %dynamic-slice_select_fusion.4), channel_id=1, source_target_pairs={{0,2},{2,3},{3,1},{1,0},{4,6},{6,7},{7,5},{5,4},{8,10},{10,11},{11... | collective-permute-start | bytes 3145736 | tf_op jit(solution)/shard_map/ppermute | solution.py:393
  431.4 21.6 %collective-permute-start.31 = (bf16[1024,4096]{1,0:T(8,128)(2,1)}, bf16[1024,4096]{1,0:T(8,128)(2,1)}, u32[]{:S(2)}, u32[]{:S(2)}) collective-permute-start(bf16[1024,4096]{1,0:T(8,128)(2,1)} %shard_map.173), channel_id=1, source_target_pairs={{0,4},{4,0},{1,5},{5,1},{2,6},{6,2},{3,7},{7,3},{8,12},{12,8},{9,1... | collective-permute-start | bytes 25165832 | tf_op jit(solution)/shard_map/ppermute | solution.py:378
  431.4 166.4 %reduce-scatter.6.cloned.1.call-start = ((), (), s32[]{:S(2)}) async-start(), calls=%async_computation.5 | async-start | bytes 10485760 | tf_op jit(solution)/shard_map/reduce_scatter | solution.py:652
  449.4 25.8 %collective-permute-start.34 = (bf16[512,1024]{1,0:T(8,128)(2,1)}, bf16[512,1024]{1,0:T(8,128)(2,1)S(1)}, u32[]{:S(2)}, u32[]{:S(2)}) collective-permute-start(bf16[512,1024]{1,0:T(8,128)(2,1)} %add_convert_fusion.6), channel_id=1, source_target_pairs={{0,2},{2,3},{3,1},{1,0},{4,6},{6,7},{7,5},{5,4},{8,10},{10,11},{11... | collective-permute-start | bytes 3145736 | tf_op jit(solution)/shard_map/ppermute | solution.py:393
  475.3 157.3 %reduce-scatter.8.cloned.1.call-start = ((), (), s32[]{:S(2)}) async-start(), calls=%async_computation.6 | async-start | bytes 5242880 | tf_op jit(solution)/shard_map/reduce_scatter | solution.py:685
  478.5 25.9 %collective-permute-start.35 = (bf16[512,1024]{1,0:T(8,128)(2,1)}, bf16[512,1024]{1,0:T(8,128)(2,1)S(1)}, u32[]{:S(2)}, u32[]{:S(2)}) collective-permute-start(bf16[512,1024]{1,0:T(8,128)(2,1)} %add_convert_fusion.5), channel_id=1, source_target_pairs={{0,2},{2,3},{3,1},{1,0},{4,6},{6,7},{7,5},{5,4},{8,10},{10,11},{11... | collective-permute-start | bytes 3145736 | tf_op jit(solution)/shard_map/ppermute | solution.py:393
  509.8 26.0 %collective-permute-start.36 = (bf16[512,1024]{1,0:T(8,128)(2,1)}, bf16[512,1024]{1,0:T(8,128)(2,1)}, u32[]{:S(2)}, u32[]{:S(2)}) collective-permute-start(bf16[512,1024]{1,0:T(8,128)(2,1)} %add_convert_fusion.4), channel_id=1, source_target_pairs={{0,2},{2,3},{3,1},{1,0},{4,6},{6,7},{7,5},{5,4},{8,10},{10,11},{11... | collective-permute-start | bytes 3145736 | tf_op jit(solution)/shard_map/ppermute | solution.py:393
  542.8 15.4 %collective-permute-start.40 = (bf16[256,512]{1,0:T(8,128)(2,1)}, bf16[256,512]{1,0:T(8,128)(2,1)S(1)}, u32[]{:S(2)}, u32[]{:S(2)}) collective-permute-start(bf16[256,512]{1,0:T(8,128)(2,1)} %get-tuple-element.1343), channel_id=1, source_target_pairs={{0,3},{2,1},{3,0},{1,2},{4,7},{6,5},{7,4},{5,6},{8,11},{10,9},{11,... | collective-permute-start | bytes 786440 | tf_op jit(solution)/shard_map/ppermute | solution.py:393
  545.2 17.0 %collective-permute-start.41 = (bf16[256,512]{1,0:T(8,128)(2,1)S(1)}, bf16[256,512]{1,0:T(8,128)(2,1)S(1)}, u32[]{:S(2)}, u32[]{:S(2)}) collective-permute-start(bf16[256,512]{1,0:T(8,128)(2,1)S(1)} %get-tuple-element.1344), channel_id=1, source_target_pairs={{0,2},{2,3},{3,1},{1,0},{4,6},{6,7},{7,5},{5,4},{8,10},{10,11},{11... | collective-permute-start | bytes 786440 | tf_op jit(solution)/shard_map/ppermute | solution.py:393
  562.9 224.0 %all-gather.5.cloned.1.call-start = ((), (), s32[]{:S(2)}) async-start(), calls=%async_computation.7 | async-start | bytes 10485760 | tf_op jit(solution)/shard_map/all_gather | solution.py:696
  567.7 30.1 %collective-permute-start.43 = (bf16[512,1024]{1,0:T(8,128)(2,1)S(1)}, bf16[512,1024]{1,0:T(8,128)(2,1)}, u32[]{:S(2)}, u32[]{:S(2)}) collective-permute-start(bf16[512,1024]{1,0:T(8,128)(2,1)S(1)} %add_convert_fusion.3), channel_id=1, source_target_pairs={{0,2},{2,3},{3,1},{1,0},{4,6},{6,7},{7,5},{5,4},{8,10},{10,11},{11... | collective-permute-start | bytes 3145736 | tf_op jit(solution)/shard_map/ppermute | solution.py:393
  613.7 18.9 %collective-permute-start.45 = (bf16[1024,1536]{1,0:T(8,128)(2,1)}, bf16[1024,1536]{1,0:T(8,128)(2,1)}, u32[]{:S(2)}, u32[]{:S(2)}) collective-permute-start(bf16[1024,1536]{1,0:T(8,128)(2,1)} %shard_map.179), channel_id=1, source_target_pairs={{0,4},{4,0},{1,5},{5,1},{2,6},{6,2},{3,7},{7,3},{8,12},{12,8},{9,1... | collective-permute-start | bytes 9437192 | tf_op jit(solution)/shard_map/ppermute | solution.py:378
  613.7 18.9 %collective-permute-start.46 = (bf16[1024,1024]{1,0:T(8,128)(2,1)}, bf16[1024,1024]{1,0:T(8,128)(2,1)}, u32[]{:S(2)}, u32[]{:S(2)}) collective-permute-start(bf16[1024,1024]{1,0:T(8,128)(2,1)} %shard_map.180), channel_id=1, source_target_pairs={{0,4},{4,0},{1,5},{5,1},{2,6},{6,2},{3,7},{7,3},{8,12},{12,8},{9,1... | collective-permute-start | bytes 6291464 | tf_op jit(solution)/shard_map/ppermute | solution.py:378
  635.6 25.5 %collective-permute-start.47 = (bf16[512,1024]{1,0:T(8,128)(2,1)}, bf16[512,1024]{1,0:T(8,128)(2,1)S(1)}, u32[]{:S(2)}, u32[]{:S(2)}) collective-permute-start(bf16[512,1024]{1,0:T(8,128)(2,1)} %dynamic-slice_select_fusion.2), channel_id=1, source_target_pairs={{0,2},{2,3},{3,1},{1,0},{4,6},{6,7},{7,5},{5,4},{8,10},{10,11},{11... | collective-permute-start | bytes 3145736 | tf_op jit(solution)/shard_map/ppermute | solution.py:393
  664.3 40.9 %collective-permute-start.51 = (bf16[512,1024]{1,0:T(8,128)(2,1)}, bf16[512,1024]{1,0:T(8,128)(2,1)S(1)}, u32[]{:S(2)}, u32[]{:S(2)}) collective-permute-start(bf16[512,1024]{1,0:T(8,128)(2,1)} %add_convert_fusion.2), channel_id=1, source_target_pairs={{0,2},{2,3},{3,1},{1,0},{4,6},{6,7},{7,5},{5,4},{8,10},{10,11},{11... | collective-permute-start | bytes 3145736 | tf_op jit(solution)/shard_map/ppermute | solution.py:393
  668.9 31.4 %collective-permute-start.49 = (bf16[256,1536]{1,0:T(8,128)(2,1)}, bf16[256,1536]{1,0:T(8,128)(2,1)}, u32[]{:S(2)}, u32[]{:S(2)}) collective-permute-start(bf16[256,1536]{1,0:T(8,128)(2,1)} %constant_dynamic-slice_fusion.1), channel_id=1, source_target_pairs={{0,8},{8,0},{16,24},{24,16},{1,9},{9,1},{17,25},{25,17},{2,10},{10... | collective-permute-start | bytes 2359304 | tf_op jit(solution)/shard_map/ppermute | solution.py:438
  671.2 34.0 %collective-permute-start.50 = (bf16[256,1536]{1,0:T(8,128)(2,1)}, bf16[256,1536]{1,0:T(8,128)(2,1)}, u32[]{:S(2)}, u32[]{:S(2)}) collective-permute-start(bf16[256,1536]{1,0:T(8,128)(2,1)} %constant_dynamic-slice_fusion), channel_id=1, source_target_pairs={{0,16},{8,24},{16,0},{24,8},{1,17},{9,25},{17,1},{25,9},{2,18},{10... | collective-permute-start | bytes 2359304 | tf_op jit(solution)/shard_map/ppermute | solution.py:438
  671.8 28.4 %collective-permute-start.52 = (f32[2,1024]{1,0:T(2,128)S(1)}, f32[2,1024]{1,0:T(2,128)S(1)}, u32[]{:S(2)}, u32[]{:S(2)}) collective-permute-start(f32[2,1024]{1,0:T(2,128)S(1)} %pad_maximum_fusion.13), channel_id=1, source_target_pairs={{0,8},{8,0},{16,24},{24,16},{1,9},{9,1},{17,25},{25,17},{2,10},{10... | collective-permute-start | bytes 24584 | tf_op jit(solution)/shard_map/ppermute | solution.py:438
  707.5 19.1 %collective-permute-start.53 = (bf16[128,1536]{1,0:T(8,128)(2,1)}, bf16[128,1536]{1,0:T(8,128)(2,1)S(1)}, u32[]{:S(2)}, u32[]{:S(2)}) collective-permute-start(bf16[128,1536]{1,0:T(8,128)(2,1)} %dynamic-slice_convert_fusion.1), channel_id=1, source_target_pairs={{0,16},{8,24},{16,0},{24,8},{1,17},{9,25},{17,1},{25,9},{2,18},{10... | collective-permute-start | bytes 1179656 | tf_op jit(solution)/shard_map/ppermute | solution.py:438
  711.8 19.1 %collective-permute-start.54 = (bf16[128,1536]{1,0:T(8,128)(2,1)}, bf16[128,1536]{1,0:T(8,128)(2,1)}, u32[]{:S(2)}, u32[]{:S(2)}) collective-permute-start(bf16[128,1536]{1,0:T(8,128)(2,1)} %dynamic-slice_convert_fusion), channel_id=1, source_target_pairs={{0,8},{8,0},{16,24},{24,16},{1,9},{9,1},{17,25},{25,17},{2,10},{10... | collective-permute-start | bytes 1179656 | tf_op jit(solution)/shard_map/ppermute | solution.py:438
  716.1 35.7 %collective-permute-start.59 = (bf16[512,1024]{1,0:T(8,128)(2,1)S(1)}, bf16[512,1024]{1,0:T(8,128)(2,1)S(1)}, u32[]{:S(2)}, u32[]{:S(2)}) collective-permute-start(bf16[512,1024]{1,0:T(8,128)(2,1)S(1)} %add_convert_fusion), channel_id=1, source_target_pairs={{0,2},{2,3},{3,1},{1,0},{4,6},{6,7},{7,5},{5,4},{8,10},{10,11},{11... | collective-permute-start | bytes 3145736 | tf_op jit(solution)/shard_map/ppermute | solution.py:393
  731.0 20.8 %collective-permute-start.57 = (bf16[128,1536]{1,0:T(8,128)(2,1)S(1)}, bf16[128,1536]{1,0:T(8,128)(2,1)S(1)}, u32[]{:S(2)}, u32[]{:S(2)}) collective-permute-start(bf16[128,1536]{1,0:T(8,128)(2,1)S(1)} %add_convert_fusion.8), channel_id=1, source_target_pairs={{0,16},{8,24},{16,0},{24,8},{1,17},{9,25},{17,1},{25,9},{2,18},{10... | collective-permute-start | bytes 1179656 | tf_op jit(solution)/shard_map/ppermute | solution.py:438
  733.1 18.7 %collective-permute-start.58 = (bf16[128,1536]{1,0:T(8,128)(2,1)S(1)}, bf16[128,1536]{1,0:T(8,128)(2,1)S(1)}, u32[]{:S(2)}, u32[]{:S(2)}) collective-permute-start(bf16[128,1536]{1,0:T(8,128)(2,1)S(1)} %add_convert_fusion.7), channel_id=1, source_target_pairs={{0,8},{8,0},{16,24},{24,16},{1,9},{9,1},{17,25},{25,17},{2,10},{10... | collective-permute-start | bytes 1179656 | tf_op jit(solution)/shard_map/ppermute | solution.py:438
  733.5 18.3 %collective-permute-start.60 = (bf16[128,1024]{1,0:T(8,128)(2,1)S(1)}, bf16[128,1024]{1,0:T(8,128)(2,1)S(1)}, u32[]{:S(2)}, u32[]{:S(2)}) collective-permute-start(bf16[128,1024]{1,0:T(8,128)(2,1)S(1)} %fusion.3), channel_id=1, source_target_pairs={{0,2},{2,3},{3,1},{1,0},{4,6},{6,7},{7,5},{5,4},{8,10},{10,11},{11... | collective-permute-start | bytes 786440 | tf_op jit(solution)/shard_map/ppermute | solution.py:393
  (75 other events, 723.5 us)
Sparse Core Ops, SparseCore 0:
  379.5 51.8 reduce-scatter.3
  433.4 52.6 all-gather.2
  490.0 86.4 reduce-scatter.5
  579.9 52.6 reduce-scatter.7
  634.4 118.2 all-gather.4

commit v3 on v2

--- a/solution.py
+++ b/solution.py
@@ -700,7 +700,7 @@
     s["fg_other"] = swap_row(s["fg_local"])
     s["attn_other"] = swap_row(s["attn_other"])
     s["fg_own"] = product("nt", [s["pg"]], [s.pop("aw")])
-    tie("both")
+    tie("both", "out")
 
     def split(name):
         values = s[name]
@@ -739,7 +739,7 @@
     s["parts"] = jnp.concatenate(
         [part(s["fg_own"], s.pop("xo")) + other, s.pop("feed_part")], axis=0
     )
-    tie("both", "out")
+    tie("both")
     reduce_step("fg", 1)
     split("attn")
     s["parts"] = s["parts"] + square.hops[0](s["parts"])
@@ -771,10 +771,9 @@
     tie("both")
     out = (s.pop("out_ring").astype(F32) + s["out"][0].astype(F32)).astype(BF)
     s["out"] = join(out, square.hops[0](out), square.bits[0], 0)
-    tie("both")
+    tie()
     s["out"] = join(s["out"], square.hops[1](s["out"]), square.bits[1], 0).astype(F32)
     phase("attn", 5)
-    tie()
     units = gate_weight.shape[1]
     s["gate"] = s["both"][:, :units].astype(F32)
     s["up"] = s.pop("both")[:, units:].astype(F32)

time: 815 us -> 807 us (level)
  waiting for transfers between devices: 310 us -> 292 us
  starting transfers between devices: 79.6 us -> 89 us
    ppermute x16, waiting for transfers between devices: 67.9 us -> 55.7 us  [__init__(): lax.ppermute(v, 'dp', [(i, i ^ flip) for i in range(4)])]
    reduce_scatter x1, waiting for transfers between devices: 11.3 us -> 0.02 us  [shards(): s['out'] = lax.psum_scatter(s['out'], 'dp', scatter_dimension=0, tiled=True)]
    unnamed x114 -> x130, local copies, waits for them, and re-layouts: 20.3 us -> 21.6 us
  transfers between devices with their start and end apart: 75 -> 75, of which waited for: 37 -> 37; matrix products, arithmetic and copies ran while one was open for 12% -> 14% of each run, Pallas kernels for 27% -> 27%
where the time goes in v3:
time: 807 us; the launch traced here: 798 us
  waiting for transfers between devices  292 us (36%)
  Pallas kernels  271 us (34%)
  starting transfers between devices  89 us (11%)
  other arithmetic  83.1 us (10%)
  local copies, waits for them, and re-layouts  47.2 us (6%)
  between operations  15.1 us (2%)
    ppermute x30, waiting for transfers between devices, shift(): return lax.ppermute(values, 'col', pairs)  219 us
    pallas_call x15, Pallas kernels, product(): pl.pallas_call(functools.partial(product_kernel, kind, len(lefts), len(mo...  138 us
    ppermute x30, starting transfers between devices, shift(): return lax.ppermute(values, 'col', pairs)  65.2 us
    ppermute x16, waiting for transfers between devices, __init__(): lax.ppermute(v, 'dp', [(i, i ^ flip) for i in range(4)])  55.7 us
    pallas_call x2, Pallas kernels, product_beside(): pl.pallas_call(functools.partial(beside_kernel, tiles, len(more)), grid=(...  31.8 us
    pallas_call x1, Pallas kernels, feed(): pl.pallas_call(feed_kernel, grid=(units // BLOCK,), in_specs=[tokens] * 2...  26.2 us
    pallas_call x2, Pallas kernels, mix(): pl.pallas_call(functools.partial(mix_kernel, offset, groups, count, last)...  22 us
    unnamed x130, local copies, waits for them, and re-layouts  21.6 us
  transfers between devices with their start and end apart: 75, of which 37 were waited for; matrix products, arithmetic and copies ran while one was open for 14% of the time, Pallas kernels for 27%

profile of v3, /device:TPU:0, one launch (start us, length us, event | category | flops | bytes accessed | tf_op | source)
XLA Modules:
  0.0 797.7 jit_solution(9482090583888400021)
XLA Ops:
  18.7 16.0 %collective-permute-done.3 = bf16[512,1024]{1,0:T(8,128)(2,1)S(1)} collective-permute-done((bf16[512,1024]{1,0:T(8,128)(2,1)}, bf16[512,1024]{1,0:T(8,128)(2,1)S(1)}, u32[]{:S(2)}, u32[]{:S(2)}) %collective-permute-start.3) | collective-permute-done | bytes 1048608 | tf_op jit(solution)/shard_map/ppermute | solution.py:393
  38.1 23.0 %collective-permute-done.5 = bf16[512,1024]{1,0:T(8,128)(2,1)S(1)} collective-permute-done((bf16[512,1024]{1,0:T(8,128)(2,1)S(1)}, bf16[512,1024]{1,0:T(8,128)(2,1)S(1)}, u32[]{:S(2)}, u32[]{:S(2)}) %collective-permute-start.5) | collective-permute-done | bytes 1048608 | tf_op jit(solution)/shard_map/ppermute | solution.py:393
  66.6 27.8 %collective-permute-done.6 = bf16[128,1024]{1,0:T(8,128)(2,1)} collective-permute-done((bf16[128,1024]{1,0:T(8,128)(2,1)S(1)}, bf16[128,1024]{1,0:T(8,128)(2,1)}, u32[]{:S(2)}, u32[]{:S(2)}) %collective-permute-start.6) | collective-permute-done | bytes 262176 | tf_op jit(solution)/shard_map/ppermute | solution.py:393
  104.5 17.4 %shard_map.160 = (bf16[1024,1024]{1,0:T(8,128)(2,1)}, bf16[1024,1024]{1,0:T(8,128)(2,1)}, bf16[1024,1536]{1,0:T(8,128)(2,1)}, f32[1024,128]{1,0:T(8,128)}) custom-call(bf16[1024,1024]{1,0:T(8,128)(2,1)} %get-tuple-element.1427.xo.refs_5_, bf16[1024,1024]{1,0:T(8,128)(2,1)} %copy-done.37, f32[1,1024]{1,0:T(1,128)} %slice.184.go, f32[1,1024]{1,0:T(1,128)} %slice.185.gt, ...), custom_call_target="tpu_custom_call" | custom-call | flops 9774999552 | bytes 1 | tf_op jit(solution)/shard_map/pallas_call | solution.py:88
  121.8 8.9 %collective-permute-done.11 = bf16[128,1024]{1,0:T(8,128)(2,1)S(1)} collective-permute-done((bf16[128,1024]{1,0:T(8,128)(2,1)}, bf16[128,1024]{1,0:T(8,128)(2,1)S(1)}, u32[]{:S(2)}, u32[]{:S(2)}) %collective-permute-start.11) | collective-permute-done | bytes 262176 | tf_op jit(solution)/shard_map/ppermute | solution.py:393
  134.2 15.5 %shard_map.161 = (bf16[1024,512]{1,0:T(8,128)(2,1)S(1)}, f32[1024,512]{1,0:T(8,128)S(1)}) custom-call(bf16[1024,1536]{1,0:T(8,128)(2,1)} %get-tuple-element.1364.qkv), custom_call_target="tpu_custom_call" | custom-call | flops 9200000000 | bytes 1 | tf_op jit(solution)/shard_map/pallas_call | solution.py:133
  149.7 12.2 %collective-permute-done.13 = bf16[128,1024]{1,0:T(8,128)(2,1)S(1)} collective-permute-done((bf16[128,1024]{1,0:T(8,128)(2,1)S(1)}, bf16[128,1024]{1,0:T(8,128)(2,1)S(1)}, u32[]{:S(2)}, u32[]{:S(2)}) %collective-permute-start.13) | collective-permute-done | bytes 262176 | tf_op jit(solution)/shard_map/ppermute | solution.py:393
  169.6 10.9 %collective-permute-done.17 = bf16[2,128,1024]{2,1,0:T(8,128)(2,1)S(1)} collective-permute-done((bf16[2,128,1024]{2,1,0:T(8,128)(2,1)S(1)}, bf16[2,128,1024]{2,1,0:T(8,128)(2,1)S(1)}, u32[]{:S(2)}, u32[]{:S(2)}) %collective-permute-start.17) | collective-permute-done | bytes 524320 | tf_op jit(solution)/shard_map/ppermute | solution.py:438
  181.8 7.0 collective-permute-done.14
  188.8 22.1 %collective-permute-done.16.refs_1_ = bf16[1024,512]{1,0:T(8,128)(2,1)S(1)} collective-permute-done((bf16[1024,512]{1,0:T(8,128)(2,1)S(1)}, bf16[1024,512]{1,0:T(8,128)(2,1)S(1)}, u32[]{:S(2)}, u32[]{:S(2)}) %collective-permute-start.16) | collective-permute-done | bytes 1048608 | tf_op jit(solution)/shard_map/ppermute | solution.py:393
  222.6 9.2 %shard_map.162.refs_2_ = f32[1024,2048]{1,0:T(8,128)} custom-call(bf16[1024,1024]{1,0:T(8,128)(2,1)} %get-tuple-element.1140.refs_0_.refs_1_, bf16[2048,1024]{1,0:T(8,128)(2,1)} %refs_1_.1), custom_call_target="tpu_custom_call" | custom-call | flops 4206773760 | bytes 1 | tf_op jit(solution)/shard_map/pallas_call | solution.py:317
  231.8 11.5 %shard_map.163.back = f32[1024,2048]{1,0:T(8,128)} custom-call(bf16[1024,1024]{1,0:T(8,128)(2,1)} %collective-permute-done.19.refs_0_.refs_1_, bf16[2048,1024]{1,0:T(8,128)(2,1)} %copy-done.30, f32[1024,2048]{1,0:T(8,128)} %shard_map.162.refs_2_), custom_call_target="tpu_custom_call" | custom-call | flops 4206773760 | bytes 1 | tf_op jit(solution)/shard_map/pallas_call | solution.py:317
  249.3 6.7 collective-permute-done.24.refs_4_.refs_2_
  256.0 12.0 %shard_map.164 = (f32[1024,1024]{1,0:T(8,128)}, f32[1024,1024]{1,0:T(8,128)}) custom-call(bf16[1024,512]{1,0:T(8,128)(2,1)} %copy-done.2, bf16[1024,512]{1,0:T(8,128)(2,1)} %copy-done.52, bf16[1024,512]{1,0:T(8,128)(2,1)} %collective-permute-done.20.refs_2_, bf16[4,512,1024]{2,1,0:T(8,128)(2,1)} %copy-done.5, ...), custom_call_target="tpu_custom_call" | custom-call | flops 5175000064 | bytes 1 | tf_op jit(solution)/shard_map/pallas_call | solution.py:245
  268.0 6.7 collective-permute-done.23.refs_0_
  275.9 10.0 %shard_map.165 = (f32[1024,1024]{1,0:T(8,128)}, f32[1024,1024]{1,0:T(8,128)}, bf16[1024,1024]{1,0:T(8,128)(2,1)}, bf16[1024,1024]{1,0:T(8,128)(2,1)}) custom-call(bf16[1024,512]{1,0:T(8,128)(2,1)} %copy-done.36, bf16[4,512,1024]{2,1,0:T(8,128)(2,1)} %copy-done.5, bf16[4,512,1024]{2,1,0:T(8,128)(2,1)} %collective-permute-done.24.refs_4_.refs_2_, ...), custom_call_target="tpu_custom_call" | custom-call | flops 1724999936 | bytes 1 | tf_op jit(solution)/shard_map/pallas_call | solution.py:245
  285.9 26.2 %shard_map.166 = (bf16[1024,2048]{1,0:T(8,128)(2,1)}, bf16[1024,2048]{1,0:T(8,128)(2,1)}, bf16[1024,2048]{1,0:T(8,128)(2,1)}) custom-call(bf16[1024,1024]{1,0:T(8,128)(2,1)} %get-tuple-element.1238.no.refs_0_, bf16[1024,1024]{1,0:T(8,128)(2,1)} %get-tuple-element.1205.nt_.refs_0_, f32[1024,2048]{1,0:T(8,128)} %shard_map.163.back, bf16[1024,2048]{1,0:T(8,128)(2,1)} %refs_2_, ...), custom_call_target="tpu_custom_call" | custom-call | flops 14949999616 | bytes 1 | tf_op jit(solution)/shard_map/pallas_call | solution.py:273
  312.1 8.5 %shard_map.167 = bf16[1024,1024]{1,0:T(8,128)(2,1)} custom-call(bf16[1024,2048]{1,0:T(8,128)(2,1)} %get-tuple-element.1139.refs_0_, bf16[2048,1024]{1,0:T(8,128)(2,1)} %copy-done.30), custom_call_target="tpu_custom_call" | custom-call | flops 4206773760 | bytes 1 | tf_op jit(solution)/shard_map/pallas_call | solution.py:317
  320.6 8.6 %shard_map.168 = bf16[1024,1024]{1,0:T(8,128)(2,1)} custom-call(bf16[1024,2048]{1,0:T(8,128)(2,1)} %get-tuple-element.1139.refs_0_, bf16[2048,1024]{1,0:T(8,128)(2,1)} %refs_1_.1), custom_call_target="tpu_custom_call" | custom-call | flops 4206773760 | bytes 1 | tf_op jit(solution)/shard_map/pallas_call | solution.py:317
  329.2 10.5 %shard_map.169 = bf16[2048,1024]{1,0:T(8,128)(2,1)} custom-call(bf16[1024,2048]{1,0:T(8,128)(2,1)} %get-tuple-element.1139.refs_0_, bf16[1024,1024]{1,0:T(8,128)(2,1)} %collective-permute-done.19.refs_0_.refs_1_), custom_call_target="tpu_custom_call" | custom-call | flops 4206773760 | bytes 1 | tf_op jit(solution)/shard_map/pallas_call | solution.py:317
  344.4 14.7 %shard_map.170 = bf16[1024,1024]{1,0:T(8,128)(2,1)} custom-call(bf16[1024,2048]{1,0:T(8,128)(2,1)} %get-tuple-element.1239.refs_0_.refs_1_, bf16[1024,2048]{1,0:T(8,128)(2,1)} %get-tuple-element.1240.refs_1_.refs_2_, bf16[1024,2048]{1,0:T(8,128)(2,1)} %copy-done.55, bf16[1024,2048]{1,0:T(8,128)(2,1)} %collective-permute-done.7.uwt.refs_3_), custom_call_target="tpu_custom_call" | custom-call | flops 7838547456 | bytes 1 | tf_op jit(solution)/shard_map/pallas_call | solution.py:317
  359.1 9.4 %collective-permute-done.26 = bf16[512,1024]{1,0:T(8,128)(2,1)S(1)} collective-permute-done((bf16[512,1024]{1,0:T(8,128)(2,1)}, bf16[512,1024]{1,0:T(8,128)(2,1)S(1)}, u32[]{:S(2)}, u32[]{:S(2)}) %collective-permute-start.26) | collective-permute-done | bytes 1048608 | tf_op jit(solution)/shard_map/ppermute | solution.py:393
  368.5 10.8 %shard_map.171 = bf16[2048,1024]{1,0:T(8,128)(2,1)} custom-call(bf16[1024,2048]{1,0:T(8,128)(2,1)} %get-tuple-element.1139.refs_0_, bf16[1024,1024]{1,0:T(8,128)(2,1)} %get-tuple-element.1140.refs_0_.refs_1_, bf16[2048,1024]{1,0:T(8,128)(2,1)} %collective-permute-done.27.refs_2_), custom_call_target="tpu_custom_call" | custom-call | flops 4206773760 | bytes 1 | tf_op jit(solution)/shard_map/pallas_call | solution.py:317
  379.4 15.4 %shard_map.172 = bf16[1024,1024]{1,0:T(8,128)(2,1)} custom-call(bf16[1024,2048]{1,0:T(8,128)(2,1)} %get-tuple-element.1239.refs_0_.refs_1_, bf16[1024,2048]{1,0:T(8,128)(2,1)} %get-tuple-element.1240.refs_1_.refs_2_, bf16[1024,2048]{1,0:T(8,128)(2,1)} %refs_2_, bf16[1024,2048]{1,0:T(8,128)(2,1)} %refs_3_), custom_call_target="tpu_custom_call" | custom-call | flops 7838547456 | bytes 1 | tf_op jit(solution)/shard_map/pallas_call | solution.py:317
  403.0 15.1 %shard_map.173 = bf16[1024,4096]{1,0:T(8,128)(2,1)} custom-call(bf16[1024,1024]{1,0:T(8,128)(2,1)} %get-tuple-element.1205.nt_.refs_0_, bf16[1024,2048]{1,0:T(8,128)(2,1)} %get-tuple-element.1239.refs_0_.refs_1_, bf16[1024,2048]{1,0:T(8,128)(2,1)} %get-tuple-element.1240.refs_1_.refs_2_), custom_call_target="tpu_custom_call" | custom-call | flops 9200000000 | bytes 1 | tf_op jit(solution)/shard_map/pallas_call | solution.py:360
  420.2 6.5 collective-permute-done.30
  426.7 4.7 reduce-scatter.4.cloned.1.call-done
  453.0 16.7 %shard_map.174 = bf16[1024,4096]{1,0:T(8,128)(2,1)} custom-call(bf16[1024,1024]{1,0:T(8,128)(2,1)} %get-tuple-element.1238.no.refs_0_, bf16[1024,2048]{1,0:T(8,128)(2,1)} %get-tuple-element.1239.refs_0_.refs_1_, bf16[1024,2048]{1,0:T(8,128)(2,1)} %get-tuple-element.1240.refs_1_.refs_2_, bf16[1024,4096]{1,0:T(8,128)(2,1)} %collective-permute-done.31.refs_3_), custom_call_target="tpu_custom_call" | custom-call | flops 9200000000 | bytes 1 | tf_op jit(solution)/shard_map/pallas_call | solution.py:360
  469.7 5.6 collective-permute-done.34
  481.8 22.6 %collective-permute-done.35 = bf16[512,1024]{1,0:T(8,128)(2,1)S(1)} collective-permute-done((bf16[512,1024]{1,0:T(8,128)(2,1)}, bf16[512,1024]{1,0:T(8,128)(2,1)S(1)}, u32[]{:S(2)}, u32[]{:S(2)}) %collective-permute-start.35) | collective-permute-done | bytes 1048608 | tf_op jit(solution)/shard_map/ppermute | solution.py:393
  518.6 7.0 shard_map.175
  527.7 8.1 %collective-permute-done.36 = bf16[512,1024]{1,0:T(8,128)(2,1)} collective-permute-done((bf16[512,1024]{1,0:T(8,128)(2,1)}, bf16[512,1024]{1,0:T(8,128)(2,1)}, u32[]{:S(2)}, u32[]{:S(2)}) %collective-permute-start.36) | collective-permute-done | bytes 1048608 | tf_op jit(solution)/shard_map/ppermute | solution.py:393
  535.8 4.4 shard_map.176
  547.7 5.0 shard_map.177
  552.8 5.5 collective-permute-done.40
  567.7 6.1 collective-permute-start.43
  576.0 20.1 %shard_map.178.refs_1_.refs_0_ = bf16[1024,1536]{1,0:T(8,128)(2,1)} custom-call(bf16[1024,1536]{1,0:T(8,128)(2,1)} %get-tuple-element.1364.qkv, bf16[1024,512]{1,0:T(8,128)(2,1)} %bitcast.40, bf16[1024,512]{1,0:T(8,128)(2,1)} %copy-done.2, f32[1024,512]{1,0:T(8,128)} %copy-done.4, f32[1024,128]{1,0:T(8,128)} %get-tuple-element.1371.cos, ...), custom_call_target="tpu_custom_call" | custom-call | flops 11500000256 | bytes 1 | tf_op jit(solution)/shard_map/pallas_call | solution.py:194
  597.8 8.9 %shard_map.179 = bf16[1024,1536]{1,0:T(8,128)(2,1)} custom-call(bf16[1024,1024]{1,0:T(8,128)(2,1)} %get-tuple-element.1379.refs_0_, bf16[1024,1536]{1,0:T(8,128)(2,1)} %shard_map.178.refs_1_.refs_0_), custom_call_target="tpu_custom_call" | custom-call | flops 3298830336 | bytes 1 | tf_op jit(solution)/shard_map/pallas_call | solution.py:317
  606.6 7.1 shard_map.180
  614.3 7.1 shard_map.181
  633.3 9.2 %shard_map.182 = bf16[1024,1536]{1,0:T(8,128)(2,1)} custom-call(bf16[1024,1024]{1,0:T(8,128)(2,1)} %get-tuple-element.1415.refs_0_, bf16[1024,1536]{1,0:T(8,128)(2,1)} %shard_map.178.refs_1_.refs_0_, bf16[1024,1536]{1,0:T(8,128)(2,1)} %collective-permute-done.45.refs_2_), custom_call_target="tpu_custom_call" | custom-call | flops 3298830336 | bytes 1 | tf_op jit(solution)/shard_map/pallas_call | solution.py:317
  642.6 9.4 %collective-permute-done.47 = bf16[512,1024]{1,0:T(8,128)(2,1)S(1)} collective-permute-done((bf16[512,1024]{1,0:T(8,128)(2,1)}, bf16[512,1024]{1,0:T(8,128)(2,1)S(1)}, u32[]{:S(2)}, u32[]{:S(2)}) %collective-permute-start.47) | collective-permute-done | bytes 1048608 | tf_op jit(solution)/shard_map/ppermute | solution.py:393
  671.7 15.3 %collective-permute-done.52 = f32[2,1024]{1,0:T(2,128)S(1)} collective-permute-done((f32[2,1024]{1,0:T(2,128)S(1)}, f32[2,1024]{1,0:T(2,128)S(1)}, u32[]{:S(2)}, u32[]{:S(2)}) %collective-permute-start.52) | collective-permute-done | bytes 8224 | tf_op jit(solution)/shard_map/ppermute | solution.py:438
  703.9 6.2 collective-permute-done.56
  720.5 12.4 %collective-permute-done.63 = f32[2,1024]{1,0:T(2,128)S(1)} collective-permute-done((f32[2,1024]{1,0:T(2,128)S(1)}, f32[2,1024]{1,0:T(2,128)S(1)}, u32[]{:S(2)}, u32[]{:S(2)}) %collective-permute-start.63) | collective-permute-done | bytes 8224 | tf_op jit(solution)/shard_map/ppermute | solution.py:393
  755.3 9.0 %collective-permute-done.64 = bf16[256,1536]{1,0:T(8,128)(2,1)S(1)} collective-permute-done((bf16[256,1536]{1,0:T(8,128)(2,1)S(1)}, bf16[256,1536]{1,0:T(8,128)(2,1)S(1)}, u32[]{:S(2)}, u32[]{:S(2)}) %collective-permute-start.64) | collective-permute-done | bytes 786464 | tf_op jit(solution)/shard_map/ppermute | solution.py:438
  766.4 4.9 collective-permute-done.68
  772.5 11.8 %slice_convert_fusion = (f32[1024,2048]{1,0:T(8,128)}, f32[1024,2048]{1,0:T(8,128)}) fusion(bf16[1024,4096]{1,0:T(8,128)(2,1)} %all-gather.5.cloned.1.call-done), kind=kLoop, calls=%fused_computation.1 | loop fusion | flops 4194304 | bytes 25165824 | tf_op jit(solution)/shard_map/convert_element_type | solution.py:779
  (364 shorter events, 232.7 us)
Async XLA Ops:
  7.2 424.2 %reduce-scatter.4.cloned.1.call-start = ((), (), s32[]{:S(2)}) async-start(), calls=%async_computation.3 | async-start | bytes 5242880 | tf_op jit(solution)/shard_map/reduce_scatter | solution.py:620
  7.2 27.5 %collective-permute-start = (bf16[1024,1536]{1,0:T(8,128)(2,1)}, bf16[1024,1536]{1,0:T(8,128)(2,1)}, u32[]{:S(2)}, u32[]{:S(2)}) collective-permute-start(bf16[1024,1536]{1,0:T(8,128)(2,1)} %refs_1_.2), channel_id=1, source_target_pairs={{0,4},{4,0},{1,5},{5,1},{2,6},{6,2},{3,7},{7,3},{8,12},{12,8},{9,1... | collective-permute-start | bytes 9437192 | tf_op jit(solution)/shard_map/ppermute | solution.py:378
  7.8 27.0 %collective-permute-start.3 = (bf16[512,1024]{1,0:T(8,128)(2,1)}, bf16[512,1024]{1,0:T(8,128)(2,1)S(1)}, u32[]{:S(2)}, u32[]{:S(2)}) collective-permute-start(bf16[512,1024]{1,0:T(8,128)(2,1)} %param.9), channel_id=1, source_target_pairs={{0,2},{2,3},{3,1},{1,0},{4,6},{6,7},{7,5},{5,4},{8,10},{10,11},{11... | collective-permute-start | bytes 3145736 | tf_op jit(solution)/shard_map/ppermute | solution.py:393
  34.8 26.4 %collective-permute-start.4 = (bf16[1024,2048]{1,0:T(8,128)(2,1)S(1)}, bf16[1024,2048]{1,0:T(8,128)(2,1)S(1)}, u32[]{:S(2)}, u32[]{:S(2)}) collective-permute-start(bf16[1024,2048]{1,0:T(8,128)(2,1)S(1)} %copy-done.54), channel_id=1, source_target_pairs={{0,4},{4,0},{1,5},{5,1},{2,6},{6,2},{3,7},{7,3},{8,12},{12,8},{9,1... | collective-permute-start | bytes 12582920 | tf_op jit(solution)/shard_map/ppermute | solution.py:378
  34.8 26.4 %collective-permute-start.5 = (bf16[512,1024]{1,0:T(8,128)(2,1)S(1)}, bf16[512,1024]{1,0:T(8,128)(2,1)S(1)}, u32[]{:S(2)}, u32[]{:S(2)}) collective-permute-start(bf16[512,1024]{1,0:T(8,128)(2,1)S(1)} %collective-permute-done.3), channel_id=1, source_target_pairs={{0,2},{2,3},{3,1},{1,0},{4,6},{6,7},{7,5},{5,4},{8,10},{10,11},{11... | collective-permute-start | bytes 3145736 | tf_op jit(solution)/shard_map/ppermute | solution.py:393
  61.1 33.3 %collective-permute-start.7 = (bf16[1024,2048]{1,0:T(8,128)(2,1)}, bf16[1024,2048]{1,0:T(8,128)(2,1)}, u32[]{:S(2)}, u32[]{:S(2)}) collective-permute-start(bf16[1024,2048]{1,0:T(8,128)(2,1)} %refs_3_), channel_id=1, source_target_pairs={{0,4},{4,0},{1,5},{5,1},{2,6},{6,2},{3,7},{7,3},{8,12},{12,8},{9,1... | collective-permute-start | bytes 12582920 | tf_op jit(solution)/shard_map/ppermute | solution.py:378
  63.2 31.2 %collective-permute-start.8 = (bf16[512,1024]{1,0:T(8,128)(2,1)S(1)}, bf16[512,1024]{1,0:T(8,128)(2,1)}, u32[]{:S(2)}, u32[]{:S(2)}) collective-permute-start(bf16[512,1024]{1,0:T(8,128)(2,1)S(1)} %collective-permute-done.5), channel_id=1, source_target_pairs={{0,2},{2,3},{3,1},{1,0},{4,6},{6,7},{7,5},{5,4},{8,10},{10,11},{11... | collective-permute-start | bytes 3145736 | tf_op jit(solution)/shard_map/ppermute | solution.py:393
  66.6 27.9 %collective-permute-start.6 = (bf16[128,1024]{1,0:T(8,128)(2,1)S(1)}, bf16[128,1024]{1,0:T(8,128)(2,1)}, u32[]{:S(2)}, u32[]{:S(2)}) collective-permute-start(bf16[128,1024]{1,0:T(8,128)(2,1)S(1)} %constant_dynamic-slice_fusion.5), channel_id=1, source_target_pairs={{0,2},{2,3},{3,1},{1,0},{4,6},{6,7},{7,5},{5,4},{8,10},{10,11},{11... | collective-permute-start | bytes 786440 | tf_op jit(solution)/shard_map/ppermute | solution.py:393
  98.4 32.3 %collective-permute-start.9 = (bf16[512,1024]{1,0:T(8,128)(2,1)S(1)}, bf16[512,1024]{1,0:T(8,128)(2,1)S(1)}, u32[]{:S(2)}, u32[]{:S(2)}) collective-permute-start(bf16[512,1024]{1,0:T(8,128)(2,1)S(1)} %copy-done.26), channel_id=1, source_target_pairs={{0,2},{2,3},{3,1},{1,0},{4,6},{6,7},{7,5},{5,4},{8,10},{10,11},{11... | collective-permute-start | bytes 3145736 | tf_op jit(solution)/shard_map/ppermute | solution.py:393
  103.1 27.6 %collective-permute-start.11 = (bf16[128,1024]{1,0:T(8,128)(2,1)}, bf16[128,1024]{1,0:T(8,128)(2,1)S(1)}, u32[]{:S(2)}, u32[]{:S(2)}) collective-permute-start(bf16[128,1024]{1,0:T(8,128)(2,1)} %collective-permute-done.6), channel_id=1, source_target_pairs={{0,2},{2,3},{3,1},{1,0},{4,6},{6,7},{7,5},{5,4},{8,10},{10,11},{11... | collective-permute-start | bytes 786440 | tf_op jit(solution)/shard_map/ppermute | solution.py:393
  130.7 31.2 %collective-permute-start.12 = (bf16[512,1024]{1,0:T(8,128)(2,1)S(1)}, bf16[512,1024]{1,0:T(8,128)(2,1)S(1)}, u32[]{:S(2)}, u32[]{:S(2)}) collective-permute-start(bf16[512,1024]{1,0:T(8,128)(2,1)S(1)} %collective-permute-done.9), channel_id=1, source_target_pairs={{0,2},{2,3},{3,1},{1,0},{4,6},{6,7},{7,5},{5,4},{8,10},{10,11},{11... | collective-permute-start | bytes 3145736 | tf_op jit(solution)/shard_map/ppermute | solution.py:393
  134.0 27.9 %collective-permute-start.13 = (bf16[128,1024]{1,0:T(8,128)(2,1)S(1)}, bf16[128,1024]{1,0:T(8,128)(2,1)S(1)}, u32[]{:S(2)}, u32[]{:S(2)}) collective-permute-start(bf16[128,1024]{1,0:T(8,128)(2,1)S(1)} %collective-permute-done.11), channel_id=1, source_target_pairs={{0,2},{2,3},{3,1},{1,0},{4,6},{6,7},{7,5},{5,4},{8,10},{10,11},{11... | collective-permute-start | bytes 786440 | tf_op jit(solution)/shard_map/ppermute | solution.py:393
  162.0 49.0 %collective-permute-start.15 = (bf16[2048,1024]{1,0:T(8,128)(2,1)}, bf16[2048,1024]{1,0:T(8,128)(2,1)S(1)}, u32[]{:S(2)}, u32[]{:S(2)}) collective-permute-start(bf16[2048,1024]{1,0:T(8,128)(2,1)} %refs_1_.1), channel_id=1, source_target_pairs={{0,4},{4,0},{1,5},{5,1},{2,6},{6,2},{3,7},{7,3},{8,12},{12,8},{9,1... | collective-permute-start | bytes 12582920 | tf_op jit(solution)/shard_map/ppermute | solution.py:378
  162.0 26.9 %collective-permute-start.14 = (bf16[512,1024]{1,0:T(8,128)(2,1)S(1)}, bf16[512,1024]{1,0:T(8,128)(2,1)S(1)}, u32[]{:S(2)}, u32[]{:S(2)}) collective-permute-start(bf16[512,1024]{1,0:T(8,128)(2,1)S(1)} %collective-permute-done.12), channel_id=1, source_target_pairs={{0,2},{2,3},{3,1},{1,0},{4,6},{6,7},{7,5},{5,4},{8,10},{10,11},{11... | collective-permute-start | bytes 3145736 | tf_op jit(solution)/shard_map/ppermute | solution.py:393
  165.3 45.6 %collective-permute-start.16 = (bf16[1024,512]{1,0:T(8,128)(2,1)S(1)}, bf16[1024,512]{1,0:T(8,128)(2,1)S(1)}, u32[]{:S(2)}, u32[]{:S(2)}) collective-permute-start(bf16[1024,512]{1,0:T(8,128)(2,1)S(1)} %get-tuple-element.1369.refs_0_.mixed), channel_id=1, source_target_pairs={{0,2},{2,3},{3,1},{1,0},{4,6},{6,7},{7,5},{5,4},{8,10},{10,11},{11... | collective-permute-start | bytes 3145736 | tf_op jit(solution)/shard_map/ppermute | solution.py:393
  215.8 16.0 %collective-permute-start.19 = (bf16[1024,1024]{1,0:T(8,128)(2,1)}, bf16[1024,1024]{1,0:T(8,128)(2,1)}, u32[]{:S(2)}, u32[]{:S(2)}) collective-permute-start(bf16[1024,1024]{1,0:T(8,128)(2,1)} %get-tuple-element.1527), channel_id=1, source_target_pairs={{0,4},{4,0},{1,5},{5,1},{2,6},{6,2},{3,7},{7,3},{8,12},{12,8},{9,1... | collective-permute-start | bytes 6291464 | tf_op jit(solution)/shard_map/ppermute | solution.py:378
  215.8 27.6 %collective-permute-start.20 = (bf16[1024,512]{1,0:T(8,128)(2,1)}, bf16[1024,512]{1,0:T(8,128)(2,1)}, u32[]{:S(2)}, u32[]{:S(2)}) collective-permute-start(bf16[1024,512]{1,0:T(8,128)(2,1)} %copy-done.52), channel_id=1, source_target_pairs={{0,2},{2,3},{3,1},{1,0},{4,6},{6,7},{7,5},{5,4},{8,10},{10,11},{11... | collective-permute-start | bytes 3145736 | tf_op jit(solution)/shard_map/ppermute | solution.py:393
  219.3 25.4 %collective-permute-start.21 = (bf16[2,256,1024]{2,1,0:T(8,128)(2,1)S(1)}, bf16[2,256,1024]{2,1,0:T(8,128)(2,1)S(1)}, u32[]{:S(2)}, u32[]{:S(2)}) collective-permute-start(bf16[2,256,1024]{2,1,0:T(8,128)(2,1)S(1)} %pad_maximum_fusion.2), channel_id=1, source_target_pairs={{0,16},{8,24},{16,0},{24,8},{1,17},{9,25},{17,1},{25,9},{2,18},{10... | collective-permute-start | bytes 3145736 | tf_op jit(solution)/shard_map/ppermute | solution.py:438
  221.1 25.2 %collective-permute-start.22 = (bf16[2,256,1024]{2,1,0:T(8,128)(2,1)S(1)}, bf16[2,256,1024]{2,1,0:T(8,128)(2,1)}, u32[]{:S(2)}, u32[]{:S(2)}) collective-permute-start(bf16[2,256,1024]{2,1,0:T(8,128)(2,1)S(1)} %pad_maximum_fusion.3), channel_id=1, source_target_pairs={{0,8},{8,0},{16,24},{24,16},{1,9},{9,1},{17,25},{25,17},{2,10},{10... | collective-permute-start | bytes 3145736 | tf_op jit(solution)/shard_map/ppermute | solution.py:438
  248.7 26.0 %collective-permute-start.23 = (bf16[1024,512]{1,0:T(8,128)(2,1)}, bf16[1024,512]{1,0:T(8,128)(2,1)S(1)}, u32[]{:S(2)}, u32[]{:S(2)}) collective-permute-start(bf16[1024,512]{1,0:T(8,128)(2,1)} %collective-permute-done.20.refs_2_), channel_id=1, source_target_pairs={{0,2},{2,3},{3,1},{1,0},{4,6},{6,7},{7,5},{5,4},{8,10},{10,11},{11... | collective-permute-start | bytes 3145736 | tf_op jit(solution)/shard_map/ppermute | solution.py:393
  339.7 28.8 %collective-permute-start.27 = (bf16[2048,1024]{1,0:T(8,128)(2,1)}, bf16[2048,1024]{1,0:T(8,128)(2,1)}, u32[]{:S(2)}, u32[]{:S(2)}) collective-permute-start(bf16[2048,1024]{1,0:T(8,128)(2,1)} %shard_map.169), channel_id=1, source_target_pairs={{0,4},{4,0},{1,5},{5,1},{2,6},{6,2},{3,7},{7,3},{8,12},{12,8},{9,1... | collective-permute-start | bytes 12582920 | tf_op jit(solution)/shard_map/ppermute | solution.py:378
  342.8 25.7 %collective-permute-start.26 = (bf16[512,1024]{1,0:T(8,128)(2,1)}, bf16[512,1024]{1,0:T(8,128)(2,1)S(1)}, u32[]{:S(2)}, u32[]{:S(2)}) collective-permute-start(bf16[512,1024]{1,0:T(8,128)(2,1)} %dynamic-slice_select_fusion.5), channel_id=1, source_target_pairs={{0,2},{2,3},{3,1},{1,0},{4,6},{6,7},{7,5},{5,4},{8,10},{10,11},{11... | collective-permute-start | bytes 3145736 | tf_op jit(solution)/shard_map/ppermute | solution.py:393
  379.4 148.3 %all-gather.3.cloned.1.call-start = ((), (), s32[]{:S(2)}) async-start(), calls=%async_computation.4 | async-start | bytes 5242880 | tf_op jit(solution)/shard_map/all_gather | solution.py:629
  398.0 20.1 %collective-permute-start.29 = (f32[512,1024]{1,0:T(8,128)}, f32[512,1024]{1,0:T(8,128)}, u32[]{:S(2)}, u32[]{:S(2)}) collective-permute-start(f32[512,1024]{1,0:T(8,128)} %constant_dynamic-slice_fusion.4), channel_id=1, source_target_pairs={{0,4},{4,0},{1,5},{5,1},{2,6},{6,2},{3,7},{7,3},{8,12},{12,8},{9,1... | collective-permute-start | bytes 6291464 | tf_op jit(solution)/shard_map/ppermute | solution.py:378
  400.8 25.9 %collective-permute-start.30 = (bf16[512,1024]{1,0:T(8,128)(2,1)}, bf16[512,1024]{1,0:T(8,128)(2,1)}, u32[]{:S(2)}, u32[]{:S(2)}) collective-permute-start(bf16[512,1024]{1,0:T(8,128)(2,1)} %dynamic-slice_select_fusion.4), channel_id=1, source_target_pairs={{0,2},{2,3},{3,1},{1,0},{4,6},{6,7},{7,5},{5,4},{8,10},{10,11},{11... | collective-permute-start | bytes 3145736 | tf_op jit(solution)/shard_map/ppermute | solution.py:393
  431.4 21.6 %collective-permute-start.31 = (bf16[1024,4096]{1,0:T(8,128)(2,1)}, bf16[1024,4096]{1,0:T(8,128)(2,1)}, u32[]{:S(2)}, u32[]{:S(2)}) collective-permute-start(bf16[1024,4096]{1,0:T(8,128)(2,1)} %shard_map.173), channel_id=1, source_target_pairs={{0,4},{4,0},{1,5},{5,1},{2,6},{6,2},{3,7},{7,3},{8,12},{12,8},{9,1... | collective-permute-start | bytes 25165832 | tf_op jit(solution)/shard_map/ppermute | solution.py:378
  431.4 166.4 %reduce-scatter.6.cloned.1.call-start = ((), (), s32[]{:S(2)}) async-start(), calls=%async_computation.5 | async-start | bytes 10485760 | tf_op jit(solution)/shard_map/reduce_scatter | solution.py:652
  449.5 25.8 %collective-permute-start.34 = (bf16[512,1024]{1,0:T(8,128)(2,1)}, bf16[512,1024]{1,0:T(8,128)(2,1)S(1)}, u32[]{:S(2)}, u32[]{:S(2)}) collective-permute-start(bf16[512,1024]{1,0:T(8,128)(2,1)} %add_convert_fusion.6), channel_id=1, source_target_pairs={{0,2},{2,3},{3,1},{1,0},{4,6},{6,7},{7,5},{5,4},{8,10},{10,11},{11... | collective-permute-start | bytes 3145736 | tf_op jit(solution)/shard_map/ppermute | solution.py:393
  475.3 167.3 %reduce-scatter.8.cloned.1.call-start = ((), (), s32[]{:S(2)}) async-start(), calls=%async_computation.6 | async-start | bytes 5242880 | tf_op jit(solution)/shard_map/reduce_scatter | solution.py:685
  478.5 25.9 %collective-permute-start.35 = (bf16[512,1024]{1,0:T(8,128)(2,1)}, bf16[512,1024]{1,0:T(8,128)(2,1)S(1)}, u32[]{:S(2)}, u32[]{:S(2)}) collective-permute-start(bf16[512,1024]{1,0:T(8,128)(2,1)} %add_convert_fusion.5), channel_id=1, source_target_pairs={{0,2},{2,3},{3,1},{1,0},{4,6},{6,7},{7,5},{5,4},{8,10},{10,11},{11... | collective-permute-start | bytes 3145736 | tf_op jit(solution)/shard_map/ppermute | solution.py:393
  509.8 26.0 %collective-permute-start.36 = (bf16[512,1024]{1,0:T(8,128)(2,1)}, bf16[512,1024]{1,0:T(8,128)(2,1)}, u32[]{:S(2)}, u32[]{:S(2)}) collective-permute-start(bf16[512,1024]{1,0:T(8,128)(2,1)} %add_convert_fusion.4), channel_id=1, source_target_pairs={{0,2},{2,3},{3,1},{1,0},{4,6},{6,7},{7,5},{5,4},{8,10},{10,11},{11... | collective-permute-start | bytes 3145736 | tf_op jit(solution)/shard_map/ppermute | solution.py:393
  545.2 17.0 %collective-permute-start.41 = (bf16[256,512]{1,0:T(8,128)(2,1)S(1)}, bf16[256,512]{1,0:T(8,128)(2,1)S(1)}, u32[]{:S(2)}, u32[]{:S(2)}) collective-permute-start(bf16[256,512]{1,0:T(8,128)(2,1)S(1)} %get-tuple-element.1336), channel_id=1, source_target_pairs={{0,2},{2,3},{3,1},{1,0},{4,6},{6,7},{7,5},{5,4},{8,10},{10,11},{11... | collective-permute-start | bytes 786440 | tf_op jit(solution)/shard_map/ppermute | solution.py:393
  562.9 208.6 %all-gather.5.cloned.1.call-start = ((), (), s32[]{:S(2)}) async-start(), calls=%async_computation.7 | async-start | bytes 10485760 | tf_op jit(solution)/shard_map/all_gather | solution.py:696
  567.7 30.1 %collective-permute-start.43 = (bf16[512,1024]{1,0:T(8,128)(2,1)S(1)}, bf16[512,1024]{1,0:T(8,128)(2,1)}, u32[]{:S(2)}, u32[]{:S(2)}) collective-permute-start(bf16[512,1024]{1,0:T(8,128)(2,1)S(1)} %add_convert_fusion.3), channel_id=1, source_target_pairs={{0,2},{2,3},{3,1},{1,0},{4,6},{6,7},{7,5},{5,4},{8,10},{10,11},{11... | collective-permute-start | bytes 3145736 | tf_op jit(solution)/shard_map/ppermute | solution.py:393
  625.6 26.4 %collective-permute-start.47 = (bf16[512,1024]{1,0:T(8,128)(2,1)}, bf16[512,1024]{1,0:T(8,128)(2,1)S(1)}, u32[]{:S(2)}, u32[]{:S(2)}) collective-permute-start(bf16[512,1024]{1,0:T(8,128)(2,1)} %dynamic-slice_select_fusion.2), channel_id=1, source_target_pairs={{0,2},{2,3},{3,1},{1,0},{4,6},{6,7},{7,5},{5,4},{8,10},{10,11},{11... | collective-permute-start | bytes 3145736 | tf_op jit(solution)/shard_map/ppermute | solution.py:393
  655.2 32.8 %collective-permute-start.51 = (bf16[512,1024]{1,0:T(8,128)(2,1)}, bf16[512,1024]{1,0:T(8,128)(2,1)S(1)}, u32[]{:S(2)}, u32[]{:S(2)}) collective-permute-start(bf16[512,1024]{1,0:T(8,128)(2,1)} %add_convert_fusion.2), channel_id=1, source_target_pairs={{0,2},{2,3},{3,1},{1,0},{4,6},{6,7},{7,5},{5,4},{8,10},{10,11},{11... | collective-permute-start | bytes 3145736 | tf_op jit(solution)/shard_map/ppermute | solution.py:393
  659.4 27.7 %collective-permute-start.49 = (bf16[256,1536]{1,0:T(8,128)(2,1)}, bf16[256,1536]{1,0:T(8,128)(2,1)}, u32[]{:S(2)}, u32[]{:S(2)}) collective-permute-start(bf16[256,1536]{1,0:T(8,128)(2,1)} %constant_dynamic-slice_fusion.1), channel_id=1, source_target_pairs={{0,8},{8,0},{16,24},{24,16},{1,9},{9,1},{17,25},{25,17},{2,10},{10... | collective-permute-start | bytes 2359304 | tf_op jit(solution)/shard_map/ppermute | solution.py:438
  661.7 26.2 %collective-permute-start.50 = (bf16[256,1536]{1,0:T(8,128)(2,1)}, bf16[256,1536]{1,0:T(8,128)(2,1)}, u32[]{:S(2)}, u32[]{:S(2)}) collective-permute-start(bf16[256,1536]{1,0:T(8,128)(2,1)} %constant_dynamic-slice_fusion), channel_id=1, source_target_pairs={{0,16},{8,24},{16,0},{24,8},{1,17},{9,25},{17,1},{25,9},{2,18},{10... | collective-permute-start | bytes 2359304 | tf_op jit(solution)/shard_map/ppermute | solution.py:438
  662.3 24.7 %collective-permute-start.52 = (f32[2,1024]{1,0:T(2,128)S(1)}, f32[2,1024]{1,0:T(2,128)S(1)}, u32[]{:S(2)}, u32[]{:S(2)}) collective-permute-start(f32[2,1024]{1,0:T(2,128)S(1)} %pad_maximum_fusion.13), channel_id=1, source_target_pairs={{0,8},{8,0},{16,24},{24,16},{1,9},{9,1},{17,25},{25,17},{2,10},{10... | collective-permute-start | bytes 24584 | tf_op jit(solution)/shard_map/ppermute | solution.py:438
  690.2 20.0 %collective-permute-start.53 = (bf16[128,1536]{1,0:T(8,128)(2,1)}, bf16[128,1536]{1,0:T(8,128)(2,1)S(1)}, u32[]{:S(2)}, u32[]{:S(2)}) collective-permute-start(bf16[128,1536]{1,0:T(8,128)(2,1)} %dynamic-slice_convert_fusion.1), channel_id=1, source_target_pairs={{0,16},{8,24},{16,0},{24,8},{1,17},{9,25},{17,1},{25,9},{2,18},{10... | collective-permute-start | bytes 1179656 | tf_op jit(solution)/shard_map/ppermute | solution.py:438
  694.2 19.7 %collective-permute-start.54 = (bf16[128,1536]{1,0:T(8,128)(2,1)}, bf16[128,1536]{1,0:T(8,128)(2,1)}, u32[]{:S(2)}, u32[]{:S(2)}) collective-permute-start(bf16[128,1536]{1,0:T(8,128)(2,1)} %dynamic-slice_convert_fusion), channel_id=1, source_target_pairs={{0,8},{8,0},{16,24},{24,16},{1,9},{9,1},{17,25},{25,17},{2,10},{10... | collective-permute-start | bytes 1179656 | tf_op jit(solution)/shard_map/ppermute | solution.py:438
  702.3 39.8 %collective-permute-start.59 = (bf16[512,1024]{1,0:T(8,128)(2,1)S(1)}, bf16[512,1024]{1,0:T(8,128)(2,1)S(1)}, u32[]{:S(2)}, u32[]{:S(2)}) collective-permute-start(bf16[512,1024]{1,0:T(8,128)(2,1)S(1)} %add_convert_fusion), channel_id=1, source_target_pairs={{0,2},{2,3},{3,1},{1,0},{4,6},{6,7},{7,5},{5,4},{8,10},{10,11},{11... | collective-permute-start | bytes 3145736 | tf_op jit(solution)/shard_map/ppermute | solution.py:393
  714.0 28.0 %collective-permute-start.57 = (bf16[128,1536]{1,0:T(8,128)(2,1)S(1)}, bf16[128,1536]{1,0:T(8,128)(2,1)S(1)}, u32[]{:S(2)}, u32[]{:S(2)}) collective-permute-start(bf16[128,1536]{1,0:T(8,128)(2,1)S(1)} %add_convert_fusion.8), channel_id=1, source_target_pairs={{0,16},{8,24},{16,0},{24,8},{1,17},{9,25},{17,1},{25,9},{2,18},{10... | collective-permute-start | bytes 1179656 | tf_op jit(solution)/shard_map/ppermute | solution.py:438
  716.4 25.6 %collective-permute-start.58 = (bf16[128,1536]{1,0:T(8,128)(2,1)S(1)}, bf16[128,1536]{1,0:T(8,128)(2,1)S(1)}, u32[]{:S(2)}, u32[]{:S(2)}) collective-permute-start(bf16[128,1536]{1,0:T(8,128)(2,1)S(1)} %add_convert_fusion.7), channel_id=1, source_target_pairs={{0,8},{8,0},{16,24},{24,16},{1,9},{9,1},{17,25},{25,17},{2,10},{10... | collective-permute-start | bytes 1179656 | tf_op jit(solution)/shard_map/ppermute | solution.py:438
  718.0 24.0 %collective-permute-start.60 = (bf16[128,1024]{1,0:T(8,128)(2,1)S(1)}, bf16[128,1024]{1,0:T(8,128)(2,1)S(1)}, u32[]{:S(2)}, u32[]{:S(2)}) collective-permute-start(bf16[128,1024]{1,0:T(8,128)(2,1)S(1)} %fusion.3), channel_id=1, source_target_pairs={{0,2},{2,3},{3,1},{1,0},{4,6},{6,7},{7,5},{5,4},{8,10},{10,11},{11... | collective-permute-start | bytes 786440 | tf_op jit(solution)/shard_map/ppermute | solution.py:393
  742.2 22.1 %collective-permute-start.64 = (bf16[256,1536]{1,0:T(8,128)(2,1)S(1)}, bf16[256,1536]{1,0:T(8,128)(2,1)S(1)}, u32[]{:S(2)}, u32[]{:S(2)}) collective-permute-start(bf16[256,1536]{1,0:T(8,128)(2,1)S(1)} %pad_maximum_fusion.5), channel_id=1, source_target_pairs={{0,8},{8,0},{16,24},{24,16},{1,9},{9,1},{17,25},{25,17},{2,10},{10... | collective-permute-start | bytes 2359304 | tf_op jit(solution)/shard_map/ppermute | solution.py:438
  743.0 21.9 %collective-permute-start.65 = (bf16[256,1536]{1,0:T(8,128)(2,1)S(1)}, bf16[256,1536]{1,0:T(8,128)(2,1)S(1)}, u32[]{:S(2)}, u32[]{:S(2)}) collective-permute-start(bf16[256,1536]{1,0:T(8,128)(2,1)S(1)} %pad_maximum_fusion.6), channel_id=1, source_target_pairs={{0,16},{8,24},{16,0},{24,8},{1,17},{9,25},{17,1},{25,9},{2,18},{10... | collective-permute-start | bytes 2359304 | tf_op jit(solution)/shard_map/ppermute | solution.py:438
  771.5 17.8 %collective-permute-start.69 = (bf16[256,1024]{1,0:T(8,128)(2,1)S(1)}, bf16[256,1024]{1,0:T(8,128)(2,1)S(1)}, u32[]{:S(2)}, u32[]{:S(2)}) collective-permute-start(bf16[256,1024]{1,0:T(8,128)(2,1)S(1)} %pad_maximum_fusion.11), channel_id=1, source_target_pairs={{0,16},{8,24},{16,0},{24,8},{1,17},{9,25},{17,1},{25,9},{2,18},{10... | collective-permute-start | bytes 1572872 | tf_op jit(solution)/shard_map/ppermute | solution.py:438
  (83 other events, 748.1 us)
Sparse Core Ops, SparseCore 0:
  379.5 51.8 reduce-scatter.3
  433.4 52.6 all-gather.2
  490.0 86.4 reduce-scatter.5
  579.9 52.6 reduce-scatter.7
  634.5 119.8 all-gather.4
